TPU v7x, 32 devices: a whole 2x2x4 slice. The times are simulated.
32 devices in a mesh: scen: 2 (over x), grid: 16 (over z, y, core).
Axes of the slice: x: 2, y: 2, z: 4, core: 2. Of those that a mesh axis runs over, the one named last changes fastest.
Arguments:
- value_next: float32 [256, 64, 1024], P('grid', 'scen'), may hold values from -8 to 8
- scenario_ids: int32 [2], P('scen'), may hold values from 0 to 11
- inflow_table: int32 [12, 3], replicated, may hold values from 0 to 8, as said below
- release_shifts: int32 [16, 3], replicated, may hold values from 0 to 8, as said below
- price: float32 [3], replicated, may hold values from 0.5 to 4
Outputs:
- value_now: float32 [256, 64, 1024], P('grid', 'scen')
Inputs may be any that keep to these rules, and one draw needn't show every extreme that they name: `inflow_table`: inflows lie in 0 to 8; each draw holds a 0 and an 8. `release_shifts`: releases lie in 0 to 8; one decision releases 8 from every reservoir and one releases nothing.
All inputs are finite; a program needn't handle non-finite values.
Results may differ from a plain program's by a relative error of at most 0.0003.
Values sent between devices are 32-bit elements; how exact they have to be, the bound alone decides.
No kernel may reach another device: no remote copies, remote signals or barrier semaphores. Data moves between devices by JAX's collectives and lax.ppermute only.
A program may use at most 128 MiB of HBM per device.

v0:
```python
import jax
import jax.numpy as jnp
from jax import lax
from jax.sharding import PartitionSpec as P

H = 8
RELEASES = 16


softness = 0.5


def with_halo(cells, sides, width):
    for axis, dim in sides:
        count = lax.axis_size(axis)
        ends = count - 1
        head = lax.slice_in_dim(cells, 0, width, axis=dim)
        tail = lax.slice_in_dim(cells, cells.shape[dim] - width, cells.shape[dim], axis=dim)
        cells = jnp.concatenate(
            [
                lax.ppermute(tail, axis, [(i, (i + 1) % count) for i in range(ends)]),
                cells,
                lax.ppermute(head, axis, [((i + 1) % count, i) for i in range(ends)]),
            ],
            axis=dim,
        )
    return cells


def on_device(value_next, scenario_ids, inflow_table, release_shifts, price):
    row_count = value_next.shape[0]
    share_depth = value_next.shape[1]
    width_count = value_next.shape[2]
    grid_count = lax.axis_size("grid")
    scen_count = lax.axis_size("scen")
    total_rows = row_count * grid_count
    total_depth = share_depth * scen_count
    row_start = lax.axis_index("grid") * row_count
    spread = lax.all_gather(value_next, "scen", axis=1, tiled=True)
    depth_start = jnp.zeros((), jnp.int32)
    spread = with_halo(spread, (("grid", 0),), H)
    global_row = row_start - H + jnp.arange(row_count + 2 * H, dtype=jnp.int32)
    local_row = jnp.clip(global_row, 0, total_rows - 1) - (row_start - H)
    global_depth = depth_start - 2 * H + jnp.arange(total_depth + 4 * H, dtype=jnp.int32)
    local_depth = jnp.clip(global_depth, 0, total_depth - 1)
    windowed = jnp.take(jnp.take(spread, local_row, axis=0), local_depth, axis=1)
    wide_pad = 2 * H
    extended = jnp.pad(windowed, ((0, 0), (0, 0), (wide_pad, wide_pad)), mode="edge")
    height_first = (
        (row_start + jnp.arange(row_count, dtype=jnp.int32) + 1).astype(jnp.float32)
        / float(total_rows)
    ).reshape(row_count, 1, 1)
    height_third = (
        (jnp.arange(total_depth, dtype=jnp.int32) + 1).astype(jnp.float32) / float(total_depth)
    ).reshape(1, total_depth, 1)
    height_second = (
        (jnp.arange(width_count) + 1).astype(jnp.float32) / float(width_count)
    ).reshape(1, 1, width_count)
    one_hot = (
        scenario_ids[:, None] == jnp.arange(inflow_table.shape[0], dtype=jnp.int32)[None, :]
    ).astype(jnp.int32)
    inflows = jnp.sum(one_hot[:, :, None] * inflow_table[None, :, :], axis=1)

    def add_release(release_index, running):
        release = release_shifts[release_index]
        amount = release.astype(jnp.float32)
        benefit = (
            price[0] * amount[0] * height_first
            + price[1] * amount[1] * height_second
            + price[2] * amount[2] * height_third
        ) / float(H)

        def one_scenario(inflow):
            first_index = H + inflow[0] - release[0]
            third_index = wide_pad + inflow[2] + release[1] - release[2]
            second_index = wide_pad + inflow[1] + release[0] - release[1]
            return lax.dynamic_slice(
                extended,
                (first_index, third_index, second_index),
                (row_count, total_depth, width_count),
            )

        landed = jax.vmap(one_scenario)(inflows)
        return running + jnp.exp(-(landed - benefit[None]) / softness)

    start_sums = jnp.zeros((inflows.shape[0], row_count, total_depth, width_count), jnp.float32)
    running = lax.fori_loop(0, RELEASES, add_release, start_sums)
    partial_total = jnp.sum(-softness * jnp.log(running), axis=0)
    scenario_count = float(scenario_ids.shape[0] * scen_count)
    owned = lax.psum_scatter(partial_total, "scen", scatter_dimension=1, tiled=True)
    average = owned / scenario_count
    cells = float(total_rows * total_depth * width_count)
    level_sum = lax.psum(jnp.sum(average), ("scen", "grid"))
    return average - level_sum / cells


def solution(mesh):
    placed = (P("grid", "scen", None), P("scen"), P(), P(), P())
    return jax.shard_map(
        on_device, mesh=mesh, in_specs=placed, out_specs=P("grid", "scen", None), check_vma=False
    )
```

profile of v0, /device:TPU:0, one launch (start us, length us, event | category | flops | bytes accessed | tf_op | source)
XLA Modules:
  0.0 687.7 jit_solution(7164838236921421066)
XLA Ops:
  7.3 61.1 %all-gather.2.cloned.1.call-done = f32[16,64,1024]{2,1,0:T(8,128)} async-done(((f32[16,32,1024]{2,1,0:T(8,128)}), f32[16,64,1024]{2,1,0:T(8,128)}) %all-gather.2.cloned.1.call-update) | async-done | bytes 4194320 | tf_op jit(solution)/shard_map/all_gather | solution.py:39
  68.4 4.0 fusion.18
  72.4 3.0 collective-permute-start
  81.6 6.0 pad_maximum_fusion
  87.5 7.7 %gather_fusion = f32[32,64,1024]{2,1,0:T(8,128)} fusion(f32[32,64,1024]{2,1,0:T(8,128)} %pad_maximum_fusion, s32[1024]{0:T(1024)S(1)} %pad_clamp_fusion.1), kind=kCustom, calls=%fused_computation | custom fusion | bytes 16777344 | tf_op jit(solution)/shard_map/jit(_take)/gather | solution.py:46
  95.2 4.5 broadcast_select_fusion
  99.7 8.1 %copy.11 = f32[32,64,1024]{2,0,1:T(8,128)} copy(f32[32,64,1024]{2,1,0:T(8,128)S(1)} %broadcast_select_fusion) | data formatting | bytes 16777216 | tf_op jit(solution)/shard_map/jit(_take)/select_n | solution.py:46
  107.8 12.1 %gather_fusion.1 = f32[96,32,1024]{2,1,0:T(8,128)} fusion(f32[32,64,1024]{2,0,1:T(8,128)} %copy.11, s32[1024]{0:T(1024)S(1)} %pad_clamp_fusion), kind=kCustom, calls=%fused_computation.1 | custom fusion | bytes 25166208 | tf_op jit(solution)/shard_map/jit(_take)/gather | solution.py:46
  119.9 12.2 %select_bitcast_fusion = f32[32,96,1024]{2,0,1:T(8,128)} fusion(f32[96,32,1024]{2,1,0:T(8,128)} %gather_fusion.1, pred[96]{0:T(512)(128)(4,1)S(1)} %compare_and_fusion.1), kind=kLoop, calls=%fused_computation.16 | loop fusion | flops 3145728 | bytes 25165920 | tf_op jit(solution)/shard_map/jit(_take)/select_n | solution.py:46
  136.8 17.0 %concatenate.17 = f32[32,96,1056]{2,0,1:T(8,128)} concatenate(f32[32,96,16]{2,0,1:T(8,128)S(1)} %reshape.236, f32[32,96,1024]{2,0,1:T(8,128)} %select_bitcast_fusion, f32[32,96,16]{2,0,1:T(8,128)S(1)} %reshape.237), dimensions={2} | concatenate | bytes 25952256 | tf_op jit(solution)/shard_map/jit(_pad)/concatenate | solution.py:48
  153.9 380.8 %while.17 = (s32[]{:T(128)}, f32[1,16,64,1024]{3,2,1,0:T(8,128)}, s32[16,3]{0,1:T(4,128)S(1)}, s32[1]{0:T(128)}, s32[1]{0:T(128)}, /*index=5*/s32[1]{0:T(128)}, ...) while((s32[]{:T(128)}, f32[1,16,64,1024]{3,2,1,0:T(8,128)}, ...), condition=%wide.region_2.3_spmd.clone, body=%wide.region_1.2_spmd.clone.sunk | while | flops 7359770 | bytes 21111964 | solution.py:87
  157.7 6.1 dynamic-slice.5
  169.0 7.5 %fusion.29 = f32[1,16,64,1024]{3,2,1,0:T(8,128)} fusion(f32[16,64,1024]{2,0,1:T(8,128)} %dynamic-slice.5, f32[1,16,64,1024]{3,2,1,0:T(8,128)} %get-tuple-element.426, f32[64]{0:T(128)S(1)} %multiply_bitcast_fusion.5, f32[16,1024]{1,0:T(8,128)S(1)} %broadcast_add_fusion.2, pred[]{:T(512)S(6)} %compare.4), kind=kLoop, calls=%fused_computation.10.clone.1 | loop fusion | flops 7340032 | bytes 12648705 | tf_op jit(solution)/shard_map/while/body/eval_jaxpr/add | solution.py:84
  180.3 6.1 dynamic-slice.5
  191.6 8.8 %fusion.29 = f32[1,16,64,1024]{3,2,1,0:T(8,128)} fusion(f32[16,64,1024]{2,0,1:T(8,128)} %dynamic-slice.5, f32[1,16,64,1024]{3,2,1,0:T(8,128)} %get-tuple-element.426, f32[64]{0:T(128)S(1)} %multiply_bitcast_fusion.5, f32[16,1024]{1,0:T(8,128)S(1)} %broadcast_add_fusion.2, pred[]{:T(512)S(6)} %compare.4), kind=kLoop, calls=%fused_computation.10.clone.1 | loop fusion | flops 7340032 | bytes 12648705 | tf_op jit(solution)/shard_map/while/body/eval_jaxpr/add | solution.py:84
  204.2 6.1 dynamic-slice.5
  215.5 8.8 %fusion.29 = f32[1,16,64,1024]{3,2,1,0:T(8,128)} fusion(f32[16,64,1024]{2,0,1:T(8,128)} %dynamic-slice.5, f32[1,16,64,1024]{3,2,1,0:T(8,128)} %get-tuple-element.426, f32[64]{0:T(128)S(1)} %multiply_bitcast_fusion.5, f32[16,1024]{1,0:T(8,128)S(1)} %broadcast_add_fusion.2, pred[]{:T(512)S(6)} %compare.4), kind=kLoop, calls=%fused_computation.10.clone.1 | loop fusion | flops 7340032 | bytes 12648705 | tf_op jit(solution)/shard_map/while/body/eval_jaxpr/add | solution.py:84
  228.1 6.1 dynamic-slice.5
  239.3 8.8 %fusion.29 = f32[1,16,64,1024]{3,2,1,0:T(8,128)} fusion(f32[16,64,1024]{2,0,1:T(8,128)} %dynamic-slice.5, f32[1,16,64,1024]{3,2,1,0:T(8,128)} %get-tuple-element.426, f32[64]{0:T(128)S(1)} %multiply_bitcast_fusion.5, f32[16,1024]{1,0:T(8,128)S(1)} %broadcast_add_fusion.2, pred[]{:T(512)S(6)} %compare.4), kind=kLoop, calls=%fused_computation.10.clone.1 | loop fusion | flops 7340032 | bytes 12648705 | tf_op jit(solution)/shard_map/while/body/eval_jaxpr/add | solution.py:84
  252.0 6.1 dynamic-slice.5
  263.2 8.8 %fusion.29 = f32[1,16,64,1024]{3,2,1,0:T(8,128)} fusion(f32[16,64,1024]{2,0,1:T(8,128)} %dynamic-slice.5, f32[1,16,64,1024]{3,2,1,0:T(8,128)} %get-tuple-element.426, f32[64]{0:T(128)S(1)} %multiply_bitcast_fusion.5, f32[16,1024]{1,0:T(8,128)S(1)} %broadcast_add_fusion.2, pred[]{:T(512)S(6)} %compare.4), kind=kLoop, calls=%fused_computation.10.clone.1 | loop fusion | flops 7340032 | bytes 12648705 | tf_op jit(solution)/shard_map/while/body/eval_jaxpr/add | solution.py:84
  275.9 6.1 dynamic-slice.5
  287.1 8.8 %fusion.29 = f32[1,16,64,1024]{3,2,1,0:T(8,128)} fusion(f32[16,64,1024]{2,0,1:T(8,128)} %dynamic-slice.5, f32[1,16,64,1024]{3,2,1,0:T(8,128)} %get-tuple-element.426, f32[64]{0:T(128)S(1)} %multiply_bitcast_fusion.5, f32[16,1024]{1,0:T(8,128)S(1)} %broadcast_add_fusion.2, pred[]{:T(512)S(6)} %compare.4), kind=kLoop, calls=%fused_computation.10.clone.1 | loop fusion | flops 7340032 | bytes 12648705 | tf_op jit(solution)/shard_map/while/body/eval_jaxpr/add | solution.py:84
  299.7 6.1 dynamic-slice.5
  311.0 8.8 %fusion.29 = f32[1,16,64,1024]{3,2,1,0:T(8,128)} fusion(f32[16,64,1024]{2,0,1:T(8,128)} %dynamic-slice.5, f32[1,16,64,1024]{3,2,1,0:T(8,128)} %get-tuple-element.426, f32[64]{0:T(128)S(1)} %multiply_bitcast_fusion.5, f32[16,1024]{1,0:T(8,128)S(1)} %broadcast_add_fusion.2, pred[]{:T(512)S(6)} %compare.4), kind=kLoop, calls=%fused_computation.10.clone.1 | loop fusion | flops 7340032 | bytes 12648705 | tf_op jit(solution)/shard_map/while/body/eval_jaxpr/add | solution.py:84
  323.6 6.1 dynamic-slice.5
  334.9 8.8 %fusion.29 = f32[1,16,64,1024]{3,2,1,0:T(8,128)} fusion(f32[16,64,1024]{2,0,1:T(8,128)} %dynamic-slice.5, f32[1,16,64,1024]{3,2,1,0:T(8,128)} %get-tuple-element.426, f32[64]{0:T(128)S(1)} %multiply_bitcast_fusion.5, f32[16,1024]{1,0:T(8,128)S(1)} %broadcast_add_fusion.2, pred[]{:T(512)S(6)} %compare.4), kind=kLoop, calls=%fused_computation.10.clone.1 | loop fusion | flops 7340032 | bytes 12648705 | tf_op jit(solution)/shard_map/while/body/eval_jaxpr/add | solution.py:84
  347.5 6.1 dynamic-slice.5
  358.7 8.8 %fusion.29 = f32[1,16,64,1024]{3,2,1,0:T(8,128)} fusion(f32[16,64,1024]{2,0,1:T(8,128)} %dynamic-slice.5, f32[1,16,64,1024]{3,2,1,0:T(8,128)} %get-tuple-element.426, f32[64]{0:T(128)S(1)} %multiply_bitcast_fusion.5, f32[16,1024]{1,0:T(8,128)S(1)} %broadcast_add_fusion.2, pred[]{:T(512)S(6)} %compare.4), kind=kLoop, calls=%fused_computation.10.clone.1 | loop fusion | flops 7340032 | bytes 12648705 | tf_op jit(solution)/shard_map/while/body/eval_jaxpr/add | solution.py:84
  371.4 6.1 dynamic-slice.5
  382.6 8.8 %fusion.29 = f32[1,16,64,1024]{3,2,1,0:T(8,128)} fusion(f32[16,64,1024]{2,0,1:T(8,128)} %dynamic-slice.5, f32[1,16,64,1024]{3,2,1,0:T(8,128)} %get-tuple-element.426, f32[64]{0:T(128)S(1)} %multiply_bitcast_fusion.5, f32[16,1024]{1,0:T(8,128)S(1)} %broadcast_add_fusion.2, pred[]{:T(512)S(6)} %compare.4), kind=kLoop, calls=%fused_computation.10.clone.1 | loop fusion | flops 7340032 | bytes 12648705 | tf_op jit(solution)/shard_map/while/body/eval_jaxpr/add | solution.py:84
  395.3 6.1 dynamic-slice.5
  406.5 8.8 %fusion.29 = f32[1,16,64,1024]{3,2,1,0:T(8,128)} fusion(f32[16,64,1024]{2,0,1:T(8,128)} %dynamic-slice.5, f32[1,16,64,1024]{3,2,1,0:T(8,128)} %get-tuple-element.426, f32[64]{0:T(128)S(1)} %multiply_bitcast_fusion.5, f32[16,1024]{1,0:T(8,128)S(1)} %broadcast_add_fusion.2, pred[]{:T(512)S(6)} %compare.4), kind=kLoop, calls=%fused_computation.10.clone.1 | loop fusion | flops 7340032 | bytes 12648705 | tf_op jit(solution)/shard_map/while/body/eval_jaxpr/add | solution.py:84
  419.1 6.1 dynamic-slice.5
  430.4 8.8 %fusion.29 = f32[1,16,64,1024]{3,2,1,0:T(8,128)} fusion(f32[16,64,1024]{2,0,1:T(8,128)} %dynamic-slice.5, f32[1,16,64,1024]{3,2,1,0:T(8,128)} %get-tuple-element.426, f32[64]{0:T(128)S(1)} %multiply_bitcast_fusion.5, f32[16,1024]{1,0:T(8,128)S(1)} %broadcast_add_fusion.2, pred[]{:T(512)S(6)} %compare.4), kind=kLoop, calls=%fused_computation.10.clone.1 | loop fusion | flops 7340032 | bytes 12648705 | tf_op jit(solution)/shard_map/while/body/eval_jaxpr/add | solution.py:84
  443.0 6.1 dynamic-slice.5
  454.3 8.8 %fusion.29 = f32[1,16,64,1024]{3,2,1,0:T(8,128)} fusion(f32[16,64,1024]{2,0,1:T(8,128)} %dynamic-slice.5, f32[1,16,64,1024]{3,2,1,0:T(8,128)} %get-tuple-element.426, f32[64]{0:T(128)S(1)} %multiply_bitcast_fusion.5, f32[16,1024]{1,0:T(8,128)S(1)} %broadcast_add_fusion.2, pred[]{:T(512)S(6)} %compare.4), kind=kLoop, calls=%fused_computation.10.clone.1 | loop fusion | flops 7340032 | bytes 12648705 | tf_op jit(solution)/shard_map/while/body/eval_jaxpr/add | solution.py:84
  466.9 6.1 dynamic-slice.5
  478.2 8.8 %fusion.29 = f32[1,16,64,1024]{3,2,1,0:T(8,128)} fusion(f32[16,64,1024]{2,0,1:T(8,128)} %dynamic-slice.5, f32[1,16,64,1024]{3,2,1,0:T(8,128)} %get-tuple-element.426, f32[64]{0:T(128)S(1)} %multiply_bitcast_fusion.5, f32[16,1024]{1,0:T(8,128)S(1)} %broadcast_add_fusion.2, pred[]{:T(512)S(6)} %compare.4), kind=kLoop, calls=%fused_computation.10.clone.1 | loop fusion | flops 7340032 | bytes 12648705 | tf_op jit(solution)/shard_map/while/body/eval_jaxpr/add | solution.py:84
  490.8 6.1 dynamic-slice.5
  502.0 8.8 %fusion.29 = f32[1,16,64,1024]{3,2,1,0:T(8,128)} fusion(f32[16,64,1024]{2,0,1:T(8,128)} %dynamic-slice.5, f32[1,16,64,1024]{3,2,1,0:T(8,128)} %get-tuple-element.426, f32[64]{0:T(128)S(1)} %multiply_bitcast_fusion.5, f32[16,1024]{1,0:T(8,128)S(1)} %broadcast_add_fusion.2, pred[]{:T(512)S(6)} %compare.4), kind=kLoop, calls=%fused_computation.10.clone.1 | loop fusion | flops 7340032 | bytes 12648705 | tf_op jit(solution)/shard_map/while/body/eval_jaxpr/add | solution.py:84
  514.7 6.1 dynamic-slice.5
  525.9 8.8 %fusion.29 = f32[1,16,64,1024]{3,2,1,0:T(8,128)} fusion(f32[16,64,1024]{2,0,1:T(8,128)} %dynamic-slice.5, f32[1,16,64,1024]{3,2,1,0:T(8,128)} %get-tuple-element.426, f32[64]{0:T(128)S(1)} %multiply_bitcast_fusion.5, f32[16,1024]{1,0:T(8,128)S(1)} %broadcast_add_fusion.2, pred[]{:T(512)S(6)} %compare.4), kind=kLoop, calls=%fused_computation.10.clone.1 | loop fusion | flops 7340032 | bytes 12648705 | tf_op jit(solution)/shard_map/while/body/eval_jaxpr/add | solution.py:84
  534.7 5.0 multiply_bitcast_fusion.2
  539.8 94.9 %reduce-scatter.2.cloned.1.call-done = f32[16,32,1024]{2,1,0:T(8,128)} async-done(((f32[16,64,1024]{2,1,0:T(8,128)}), f32[16,32,1024]{2,1,0:T(8,128)}) %reduce-scatter.2.cloned.1.call-update) | async-done | bytes 2097168 | tf_op jit(solution)/shard_map/reduce_scatter | solution.py:90
  634.7 2.7 multiply_reduce_fusion
  637.4 39.5 %psum.7 = f32[]{:T(128)} all-reduce(f32[]{:T(128)} %multiply_reduce_fusion), channel_id=1, replica_groups=mesh['scen'=2,'grid'=16] {'scen','grid'}, use_global_device_ids=true, to_apply=%region_5.6 | all-reduce | flops 1 | bytes 8 | tf_op jit(solution)/shard_map/psum | solution.py:93
  677.6 3.3 multiply_subtract_fusion
  (156 shorter events, 40.4 us)
Async XLA Ops:
  6.5 61.8 %all-gather.2.cloned.1.call-start = ((), (), s32[]{:S(2)}) async-start(), calls=%async_computation.1 | async-start | bytes 6291456 | tf_op jit(solution)/shard_map/all_gather | solution.py:39
  7.3 70.1 %copy-start.2 = (s32[12,3]{0,1:T(4,128)S(1)}, s32[12,3]{0,1:T(4,128)}, u32[]{:S(2)}) copy-start(s32[12,3]{0,1:T(4,128)} %param.9) | copy-start | bytes 436
  7.3 627.4 %reduce-scatter.2.cloned.1.call-start = ((), (), s32[]{:S(2)}) async-start(), calls=%async_computation.2 | async-start | bytes 6291456 | tf_op jit(solution)/shard_map/reduce_scatter | solution.py:90
  72.4 7.8 %collective-permute-start = (f32[8,64,1024]{2,1,0:T(8,128)}, f32[8,64,1024]{2,1,0:T(8,128)}, u32[]{:S(2)}, u32[]{:S(2)}) collective-permute-start(f32[8,64,1024]{2,1,0:T(8,128)} %get-tuple-element.325), channel_id=1, source_target_pairs={{0,1},{1,2},{2,3},{3,4},{4,5},{5,6},{6,7},{7,8},{8,9},{9,10},{10,1... | collective-permute-start | bytes 6291464 | tf_op jit(solution)/shard_map/ppermute | solution.py:21
  75.4 6.2 collective-permute-start.1
  136.8 17.0 %copy-start = (f32[3]{0:T(128)S(1)}, f32[3]{0:T(128)}, u32[]{:S(2)}) copy-start(f32[3]{0:T(128)} %param.11) | copy-start | bytes 40
  136.8 17.0 %copy-start.1 = (s32[16,3]{0,1:T(4,128)S(1)}, s32[16,3]{0,1:T(4,128)}, u32[]{:S(2)}) copy-start(s32[16,3]{0,1:T(4,128)} %param.10) | copy-start | bytes 580
Sparse Core Ops, SparseCore 0:
  8.9 59.4 all-gather.1
  539.9 94.7 reduce-scatter.1
where the time goes:
time: 691 us; the launch traced here: 688 us
  local copies, waits for them, and re-layouts  181 us (26%)
  other arithmetic  176 us (25%)
  waiting for transfers between devices  158 us (23%)
  loops' own time  112 us (16%)
  blocking collectives  39.5 us (6%)
  between operations  16.7 us (2%)
    add x16, other arithmetic, add_release(): return running + jnp.exp(-(landed - benefit[None]) / softness)  139 us
    another operation x1, loops' own time, on_device(): running = lax.fori_loop(0, RELEASES, add_release, start_sums)  112 us
    while x16, local copies, waits for them, and re-layouts, one_scenario(): lax.dynamic_slice(extended, (first_index, third_index, second_index), (ro...  98.2 us
    reduce_scatter x1, waiting for transfers between devices, on_device(): lax.psum_scatter(partial_total, 'scen', scatter_dimension=1, tiled=True)  94.9 us
    all_gather x1, waiting for transfers between devices, on_device(): spread = lax.all_gather(value_next, 'scen', axis=1, tiled=True)  61.1 us
    psum x1, blocking collectives, on_device(): level_sum = lax.psum(jnp.sum(average), ('scen', 'grid'))  39.5 us
    concatenate x1, local copies, waits for them, and re-layouts, on_device(): jnp.pad(windowed, ((0, 0), (0, 0), (wide_pad, wide_pad)), mode='edge')  17 us
  transfers between devices with their start and end apart: 4, of which 3 were waited for; matrix products, arithmetic and copies ran while one was open for 0% of the time, Pallas kernels for 0%

commit v1 on v0

v1 whole, which is shorter than its diff:
```python
import functools

import jax
import jax.numpy as jnp
from jax import lax
from jax.experimental import pallas as pl
from jax.experimental.pallas import tpu as pltpu
from jax.sharding import PartitionSpec as P

H = 8
LOW, HIGH = H, 2 * H
SUB, LANES = 8, 128
softness = 0.5

SHIFT_A, OFFSET, TURN, CUT, SHIFT_C = range(5)
FIRST_ROW, LAST_ROW, FIRST_DEPTH, LAST_DEPTH, ROW0, DEPTH0 = range(6)


class Sizes:
    def __init__(self, rows, depth, width, scenarios, releases):
        self.rows, self.depth, self.width = rows, depth, width
        self.scenarios, self.releases = scenarios, releases
        self.blocks = width // LANES
        self.strips = depth // SUB
        self.lanes_ext = self.blocks + 2
        self.depth_ext = LOW + depth + HIGH
        self.row_size = self.lanes_ext * self.depth_ext


def put(weights, sizes, row, at, values):
    for strip in range(values.shape[0] // SUB):
        levels = slice(strip * SUB, strip * SUB + SUB)
        base = row * sizes.row_size + at + strip * SUB
        for block in range(sizes.blocks):
            e = jnp.exp(values[levels, block * LANES : block * LANES + LANES] * (-1.0 / softness))
            weights[pl.ds(base + (block + 1) * sizes.depth_ext, SUB), :] = e
            if block == 0:
                weights[pl.ds(base, SUB), :] = jnp.broadcast_to(e[:, :1], e.shape)
            if block == sizes.blocks - 1:
                end = base + (sizes.blocks + 1) * sizes.depth_ext
                weights[pl.ds(end, SUB), :] = jnp.broadcast_to(e[:, LANES - 1 :], e.shape)


def put_zeros(weights, sizes, row, at, count):
    zero = jnp.zeros((SUB, LANES), jnp.float32)
    for strip in range(count // SUB):
        for block in range(sizes.lanes_ext):
            weights[pl.ds(row * sizes.row_size + block * sizes.depth_ext + at + strip * SUB, SUB), :] = zero


def put_row(weights, sizes, pos, row, own, low, high):
    if own is None:
        put_zeros(weights, sizes, row, LOW, sizes.depth)
    else:
        put(weights, sizes, row, LOW, own)
    for is_end, at, count, beyond, edge in (
        (pos[FIRST_DEPTH] != 0, 0, LOW, low, None if own is None else own[:1]),
        (pos[LAST_DEPTH] != 0, LOW + sizes.depth, HIGH, high, None if own is None else own[-1:]),
    ):

        @pl.when(is_end)
        def _():
            if edge is None:
                put_zeros(weights, sizes, row, at, count)
            else:
                put(weights, sizes, row, at, jnp.broadcast_to(edge, (count, sizes.width)))

        @pl.when(jnp.logical_not(is_end))
        def _():
            if beyond is None:
                put_zeros(weights, sizes, row, at, count)
            else:
                put(weights, sizes, row, at, beyond())


def fill_gains(gains, sizes, rates):
    lane = lax.broadcasted_iota(jnp.int32, (SUB, LANES), 1)
    for release in range(sizes.releases):
        for block in range(sizes.blocks):
            level = (lane + (block * LANES + 1)).astype(jnp.float32)
            gains[pl.ds((release * sizes.blocks + block) * SUB, SUB), :] = jnp.exp(level * rates[release, 1])


def add_terms(sums, table, rates, pos, weights, gains, sizes, scenario, row, first, count, start, stop, source_row, wanted):
    lane = lax.broadcasted_iota(jnp.int32, (SUB, LANES), 1)
    level = lax.broadcasted_iota(jnp.int32, (SUB, LANES), 0)
    level = (level + (pos[DEPTH0] + first * SUB + 1)).astype(jnp.float32)
    height = (pos[ROW0] + row + 1).astype(jnp.float32)

    def term(release, sums):
        at = scenario * sizes.releases + release
        base = source_row(row + table[at, SHIFT_A]) * sizes.row_size + table[at, OFFSET] + first * SUB
        later = lane < table[at, CUT]
        turn = table[at, TURN]
        out = []
        rate = rates[release, 2]
        flat = rates[release, 0] * height
        factors = [jnp.exp((level + float(strip * SUB)) * rate + flat) for strip in range(count)]
        for block in range(sizes.blocks):
            gain = gains[pl.ds((release * sizes.blocks + block) * SUB, SUB), :]
            for strip in range(count):
                here = weights[pl.ds(base + block * sizes.depth_ext + strip * SUB, SUB), :]
                beyond = weights[pl.ds(base + (block + 1) * sizes.depth_ext + strip * SUB, SUB), :]
                landed = pltpu.roll(jnp.where(later, beyond, here), turn, 1)
                out.append(sums[block * count + strip] + landed * (gain * factors[strip]))
        return tuple(out)

    def step(release, sums):
        if wanted is None:
            return term(release, sums)
        return lax.cond(wanted(table[scenario * sizes.releases + release, SHIFT_C]), lambda s: term(release, s), lambda s: s, sums)

    return lax.fori_loop(start, stop, step, sums)


def load_sums(ref, sizes, scenario, row, first, count):
    return tuple(
        ref[scenario, row, pl.ds(pl.multiple_of((first + strip) * SUB, SUB), SUB), block * LANES : block * LANES + LANES]
        for block in range(sizes.blocks)
        for strip in range(count)
    )


def store_sums(ref, sizes, scenario, row, first, count, sums):
    for block in range(sizes.blocks):
        for strip in range(count):
            ref[
                scenario, row, pl.ds(pl.multiple_of((first + strip) * SUB, SUB), SUB), block * LANES : block * LANES + LANES
            ] = sums[block * count + strip]


def own_range(below, inflow, pos, sizes, scenario, row):
    top = row + inflow[scenario]
    start = jnp.where(pos[LAST_ROW] != 0, 0, below[jnp.clip(top - sizes.rows + 1, 0, H + 1)])
    stop = jnp.where(pos[FIRST_ROW] != 0, sizes.releases, below[jnp.clip(top + 1, 0, H + 1)])
    return start, stop


def own_kernel(sizes, table, rates, below, inflow, pos, values, sums_out, weights, gains):
    fill_gains(gains, sizes, rates)

    def fill(row, _):
        put_row(weights, sizes, pos, row, values[row], None, None)
        return 0

    lax.fori_loop(0, sizes.rows, fill, 0)
    zero = jnp.zeros((SUB, LANES), jnp.float32)

    def work(index, _):
        scenario, row = index // sizes.rows, index % sizes.rows
        start, stop = own_range(below, inflow, pos, sizes, scenario, row)
        sums = tuple(zero for _ in range(sizes.blocks * sizes.strips))
        sums = add_terms(
            sums, table, rates, pos, weights, gains, sizes, scenario, row, 0, sizes.strips, start, stop,
            lambda r: jnp.clip(r, 0, sizes.rows - 1), None,
        )
        store_sums(sums_out, sizes, scenario, row, 0, sizes.strips, sums)
        return 0

    lax.fori_loop(0, sizes.scenarios * sizes.rows, work, 0)


def beyond_levels(pair, pos, low_ref, high_ref, row):
    return lambda: low_ref[row, low_ref.shape[1] - LOW :], lambda: high_ref[row, :HIGH]


def edge_strips(sizes, pos, pair):
    count = min(HIGH // SUB, sizes.strips)
    if pair:
        return jnp.where(pos[FIRST_DEPTH] != 0, sizes.strips - count, 0), count
    return 0, sizes.strips


def reaches(sizes, pos, first, count):
    def test(shift):
        up = jnp.logical_and(pos[LAST_DEPTH] == 0, first * SUB + count * SUB + shift > sizes.depth)
        down = jnp.logical_and(pos[FIRST_DEPTH] == 0, first * SUB + shift < 0)
        return jnp.logical_or(up, down)

    return test


def outside_row(sizes):
    return lambda r: jnp.where(r < 0, r + H, r - sizes.rows + H)


def outside_terms(ref_in, ref_out, table, rates, below, inflow, pos, weights, gains, sizes, first, count, wanted):
    def work(index, _):
        scenario, row = index // sizes.rows, index % sizes.rows
        start, stop = own_range(below, inflow, pos, sizes, scenario, row)

        @pl.when(jnp.logical_or(start > 0, stop < sizes.releases))
        def _():
            sums = load_sums(ref_in, sizes, scenario, row, first, count)
            for lo, hi in ((0, start), (stop, sizes.releases)):
                sums = add_terms(
                    sums, table, rates, pos, weights, gains, sizes, scenario, row, first, count, lo, hi, outside_row(sizes), wanted
                )
            store_sums(ref_out, sizes, scenario, row, first, count, sums)

        return 0

    lax.fori_loop(0, sizes.scenarios * sizes.rows, work, 0)


def edge_kernel(sizes, pair, table, rates, below, inflow, pos, low, high, before, after, sums_in, sums_out, weights, gains):
    fill_gains(gains, sizes, rates)

    def fill_depth(row, _):
        put_row(weights, sizes, pos, row, None, *beyond_levels(pair, pos, low, high, row))
        return 0

    lax.fori_loop(0, sizes.rows, fill_depth, 0)
    first, count = edge_strips(sizes, pos, pair)
    wanted = reaches(sizes, pos, first, count)
    sums_out[...] = sums_in[...]

    def work(index, _):
        scenario, row = index // sizes.rows, index % sizes.rows
        start, stop = own_range(below, inflow, pos, sizes, scenario, row)
        sums = load_sums(sums_out, sizes, scenario, row, first, count)
        sums = add_terms(
            sums, table, rates, pos, weights, gains, sizes, scenario, row, first, count, start, stop,
            lambda r: jnp.clip(r, 0, sizes.rows - 1), wanted,
        )
        store_sums(sums_out, sizes, scenario, row, first, count, sums)
        return 0

    lax.fori_loop(0, sizes.scenarios * sizes.rows, work, 0)

    def fill_rows(row, _):
        put_row(weights, sizes, pos, row, before[row], None, None)
        put_row(weights, sizes, pos, row + H, after[row], None, None)
        return 0

    lax.fori_loop(0, H, fill_rows, 0)
    outside_terms(sums_out, sums_out, table, rates, below, inflow, pos, weights, gains, sizes, 0, sizes.strips, None)


def last_kernel(
    sizes, pair, scale, table, rates, below, inflow, pos, low_before, high_before, low_after, high_after, sums_in, average_out, total_out,
    sums, weights, gains,
):
    fill_gains(gains, sizes, rates)

    def fill_rows(row, _):
        put_row(weights, sizes, pos, row, None, *beyond_levels(pair, pos, low_before, high_before, row))
        put_row(weights, sizes, pos, row + H, None, *beyond_levels(pair, pos, low_after, high_after, row))
        return 0

    lax.fori_loop(0, H, fill_rows, 0)
    first, count = edge_strips(sizes, pos, pair)
    sums[...] = sums_in[...]
    outside_terms(sums, sums, table, rates, below, inflow, pos, weights, gains, sizes, first, count, reaches(sizes, pos, first, count))

    def finish(row, total):
        for strip in range(sizes.strips):
            for block in range(sizes.blocks):
                tile = (row, slice(strip * SUB, strip * SUB + SUB), slice(block * LANES, block * LANES + LANES))
                logs = None
                for scenario in range(0, sizes.scenarios, 2):
                    product = sums[(scenario, *tile)]
                    if scenario + 1 < sizes.scenarios:
                        product = product * sums[(scenario + 1, *tile)]
                    log = jnp.log(product)
                    logs = log if logs is None else logs + log
                average = logs * scale
                average_out[tile] = average
                total = total + average
        return total

    total = lax.fori_loop(0, sizes.rows, finish, jnp.zeros((SUB, LANES), jnp.float32))
    total_out[...] = jnp.sum(total, axis=0, keepdims=True)


def call(kernel, scalars, arrays, outs, scratch, aliases=None):
    smem, vmem = pl.BlockSpec(memory_space=pltpu.SMEM), pl.BlockSpec(memory_space=pltpu.VMEM)
    return pl.pallas_call(
        kernel,
        out_shape=outs,
        in_specs=[smem] * len(scalars) + [vmem] * len(arrays),
        out_specs=jax.tree.map(lambda _: vmem, outs),
        scratch_shapes=scratch,
        input_output_aliases=aliases or {},
        compiler_params=pltpu.CompilerParams(vmem_limit_bytes=56 * 2**20),
    )(*scalars, *arrays)


def from_above(cells, axis, hops=1):
    count = lax.axis_size(axis)
    return lax.ppermute(cells, axis, [(i + hops, i) for i in range(count - hops)])


def from_below(cells, axis, hops=1):
    count = lax.axis_size(axis)
    return lax.ppermute(cells, axis, [(i, i + hops) for i in range(count - hops)])


def on_device(value_next, scenario_ids, inflow_table, release_shifts, price):
    rows, depth, width = value_next.shape
    grid_count, scen_count = lax.axis_size("grid"), lax.axis_size("scen")
    grid, scen = lax.axis_index("grid"), lax.axis_index("scen")
    total_rows, total_depth = rows * grid_count, depth * scen_count
    releases = release_shifts.shape[0]
    pair = scen_count == 2 and depth >= HIGH

    ids = [scenario_ids]
    for hop in range(1, scen_count):
        ids.append(lax.ppermute(scenario_ids, "scen", [(i, (i + hop) % scen_count) for i in range(scen_count)]))
    ids = jnp.concatenate(ids)
    sizes = Sizes(rows, depth, width, ids.shape[0], releases)

    if pair:
        start = jnp.where(scen == 0, depth - HIGH, 0)
        sent = lax.dynamic_slice_in_dim(value_next, start, HIGH, axis=1)
        low = high = lax.ppermute(sent, "scen", [(0, 1), (1, 0)])
    else:
        low, high = [], []
        for hop in range(-(-LOW // depth), 0, -1):
            low.append(from_below(value_next, "scen", hop) if hop < scen_count else jnp.zeros_like(value_next))
        for hop in range(1, -(-HIGH // depth) + 1):
            high.append(from_above(value_next, "scen", hop) if hop < scen_count else jnp.zeros_like(value_next))
        low = jnp.concatenate(low, axis=1)[:, -LOW:]
        high = jnp.concatenate(high, axis=1)[:, :HIGH]
        last = value_next[:, -1:]
        for hop in range(1, -(-HIGH // depth)):
            past = jnp.where(scen + hop == scen_count - 1, 1, 0)
            fill = high[:, hop * depth - 1 : hop * depth]
            keep = lax.broadcasted_iota(jnp.int32, high.shape, 1) < hop * depth
            high = jnp.where(jnp.logical_or(past == 0, keep), high, fill)
        del last
    before = from_below(value_next[rows - H :], "grid")
    after = from_above(value_next[:H], "grid")

    shifts = release_shifts[:, 0]
    order = jnp.arange(releases, dtype=jnp.int32)
    ahead = jnp.logical_or(
        shifts[None, :] < shifts[:, None], jnp.logical_and(shifts[None, :] == shifts[:, None], order[None, :] < order[:, None])
    )
    rank = jnp.sum(ahead.astype(jnp.int32), axis=1)
    moved = (rank[None, :] == order[:, None]).astype(jnp.int32)
    sorted_shifts = jnp.sum(moved[:, :, None] * release_shifts[None, :, :], axis=1)
    below = jnp.sum((shifts[None, :] < jnp.arange(H + 2, dtype=jnp.int32)[:, None]).astype(jnp.int32), axis=1)
    one_hot = (ids[:, None] == jnp.arange(inflow_table.shape[0], dtype=jnp.int32)[None, :]).astype(jnp.int32)
    inflows = jnp.sum(one_hot[:, :, None] * inflow_table[None, :, :], axis=1)
    u1, u2, u3 = (sorted_shifts[None, :, i] for i in range(3))
    i1, i2, i3 = (inflows[:, None, i] for i in range(3))
    shift_b = i2 + u1 - u2
    shift_c = i3 + u2 - u3
    ahead_b = shift_b >= 0
    cut = jnp.where(ahead_b, shift_b, shift_b + LANES)
    table = jnp.stack(
        [i1 - u1, jnp.where(ahead_b, sizes.depth_ext, 0) + LOW + shift_c, (LANES - cut) % LANES, cut, shift_c], axis=-1
    ).reshape(-1, 5)
    spans = jnp.array([total_rows, width, total_depth], jnp.float32)
    rates = sorted_shifts.astype(jnp.float32) * (price / (spans * (H * softness)))[None, :]
    pos = jnp.stack(
        [grid == 0, grid == grid_count - 1, scen == 0, scen == scen_count - 1, grid * rows, scen * depth]
    ).astype(jnp.int32)
    scalars = (table, rates, below, inflows[:, 0], pos)

    sums_shape = jax.ShapeDtypeStruct((sizes.scenarios, rows, depth, width), jnp.float32)
    gains = pltpu.VMEM((releases * sizes.blocks * SUB, LANES), jnp.float32)
    ext = pltpu.VMEM((max(rows, 2 * H) * sizes.row_size, LANES), jnp.float32)
    sums = call(functools.partial(own_kernel, sizes), scalars, (value_next,), sums_shape, [ext, gains])

    sums = call(
        functools.partial(edge_kernel, sizes, pair), scalars, (low, high, before, after, sums), sums_shape, [ext, gains],
        {len(scalars) + 4: 0},
    )

    if pair:
        low_before = high_before = from_below(low[rows - H :], "grid")
        low_after = high_after = from_above(low[:H], "grid")
    else:
        both = jnp.concatenate([low, high], axis=1)
        both_before, both_after = from_below(both[rows - H :], "grid"), from_above(both[:H], "grid")
        low_before, high_before = both_before[:, :LOW], both_before[:, LOW:]
        low_after, high_after = both_after[:, :LOW], both_after[:, LOW:]

    scale = -softness / sizes.scenarios
    average, total = call(
        functools.partial(last_kernel, sizes, pair, scale), scalars, (low_before, high_before, low_after, high_after, sums),
        (jax.ShapeDtypeStruct(value_next.shape, jnp.float32), jax.ShapeDtypeStruct((1, LANES), jnp.float32)),
        [pltpu.VMEM(sums_shape.shape, jnp.float32), pltpu.VMEM((2 * H * sizes.row_size, LANES), jnp.float32), gains],
    )
    devices = grid_count * scen_count
    totals = lax.all_to_all(jnp.broadcast_to(total[None], (devices, 1, LANES)), ("scen", "grid"), 0, 0, tiled=True)
    return average - jnp.sum(totals) / float(total_rows * total_depth * width)


def solution(mesh):
    placed = (P("grid", "scen", None), P("scen"), P(), P(), P())
    return jax.shard_map(
        on_device, mesh=mesh, in_specs=placed, out_specs=P("grid", "scen", None), check_vma=False
    )
```

time: 691 us -> 191 us (0.28)
  local copies, waits for them, and re-layouts: 181 us -> 10.4 us
  other arithmetic: 176 us -> 6.4 us
  waiting for transfers between devices: 158 us -> 16.1 us
  Pallas kernels: 0 us -> 133 us
  loops' own time: 112 us -> 0 us
  blocking collectives: 39.5 us -> 14.9 us
  between operations: 16.7 us -> 1.35 us
    add x32 -> x0, other arithmetic: 141 us -> none  [the longest x16 139 us: add_release(): return running + jnp.exp(-(landed - benefit[None]) / softness)]
    pallas_call x0 -> x3, Pallas kernels: none -> 133 us  [call(): pl.pallas_call(kernel, out_shape=outs, in_specs=[smem] * len(scalars) + [...]
    another operation x1 -> x0, loops' own time: 112 us -> none  [on_device(): running = lax.fori_loop(0, RELEASES, add_release, start_sums)]
    while x16 -> x0, local copies, waits for them, and re-layouts: 98.2 us -> none  [one_scenario(): lax.dynamic_slice(extended, (first_index, third_index, second_index), (ro...]
    reduce_scatter x1 -> x0, waiting for transfers between devices: 94.9 us -> none  [on_device(): lax.psum_scatter(partial_total, 'scen', scatter_dimension=1, tiled=True)]
    all_gather x1 -> x0, waiting for transfers between devices: 61.1 us -> none  [on_device(): spread = lax.all_gather(value_next, 'scen', axis=1, tiled=True)]
    psum x1 -> x0, blocking collectives: 39.5 us -> none  [on_device(): level_sum = lax.psum(jnp.sum(average), ('scen', 'grid'))]
    slice x53 -> x3, local copies, waits for them, and re-layouts: 37 us -> 2.63 us  [the longest x1 1.49 us: on_device(): after = from_above(value_next[:H], 'grid')]
  transfers between devices with their start and end apart: 4 -> 6, of which waited for: 3 -> 1; matrix products, arithmetic and copies ran while one was open for 0% -> 5% of each run, Pallas kernels for 0% -> 60%
where the time goes in v1:
time: 191 us
  Pallas kernels  133 us (70%)
  waiting for transfers between devices  16.1 us (8%)
  blocking collectives  14.9 us (8%)
  local copies, waits for them, and re-layouts  10.4 us (5%)
  starting transfers between devices  8.63 us (5%)
  other arithmetic  6.4 us (3%)
    pallas_call x3, Pallas kernels, call(): pl.pallas_call(kernel, out_shape=outs, in_specs=[smem] * len(scalars) + [...  133 us
    ppermute x1, waiting for transfers between devices, on_device(): low = high = lax.ppermute(sent, 'scen', [(0, 1), (1, 0)])  16.1 us
    all_to_all x1, blocking collectives, on_device(): lax.all_to_all(jnp.broadcast_to(total[None], (devices, 1, LANES)), ('scen...  14.9 us
  transfers between devices with their start and end apart: 6, of which 1 were waited for; matrix products, arithmetic and copies ran while one was open for 5% of the time, Pallas kernels for 60%

profile of v1, /device:TPU:0, one launch (start us, length us, event | category | flops | bytes accessed | tf_op | source)
XLA Modules:
  0.0 191.0 jit_solution(565563758169811024)
XLA Ops:
  0.0 2.9 %collective-permute-start = (s32[1]{0:T(128)}, s32[1]{0:T(128)}, u32[]{:S(2)}, u32[]{:S(2)}) collective-permute-start(s32[1]{0:T(128)} %param.7), channel_id=1, source_target_pairs={{0,16},{16,0},{1,17},{17,1},{2,18},{18,2},{3,19},{19,3},{4,20},{20... | collective-permute-start | bytes 20 | tf_op jit(solution)/shard_map/ppermute | solution.py:309
  2.9 2.3 %constant_dynamic-slice_fusion = f32[16,16,1024]{2,1,0:T(8,128)} fusion(f32[16,32,1024]{2,1,0:T(8,128)} %values.1, s32[]{:T(128)S(6)} %select_n.52), kind=kLoop, calls=%fused_computation.31 | loop fusion | bytes 2097156 | tf_op jit(solution)/shard_map/dynamic_slice | solution.py:315
  5.3 0.2 collective-permute-start.1
  5.4 0.0 copy-done
  5.4 1.5 fusion.6
  6.9 1.6 collective-permute-start.4
  8.6 1.3 collective-permute-start.5
  9.9 0.0 copy-done.7
  9.9 0.2 convert_reduce_fusion.1
  10.7 0.1 multiply_reduce_fusion
  10.9 0.1 copy.37
  11.0 0.1 sub.102
  11.1 0.1 sub.105
  11.2 0.1 sub.99
  11.2 0.7 stack.52.pos
  11.9 0.7 convert_reduce_fusion.below
  12.6 0.6 convert_multiply_fusion.rates
  13.2 0.0 collective-permute-done
  13.2 0.8 pad_add_fusion
  14.0 0.1 compare_convert_fusion
  14.0 16.1 %collective-permute-done.1.low.high = f32[16,16,1024]{2,1,0:T(8,128)S(1)} collective-permute-done((f32[16,16,1024]{2,1,0:T(8,128)}, f32[16,16,1024]{2,1,0:T(8,128)S(1)}, u32[]{:S(2)}, u32[]{:S(2)}) %collective-permute-start.1) | collective-permute-done | bytes 1048608 | tf_op jit(solution)/shard_map/ppermute | solution.py:316
  30.1 1.1 fusion.7
  31.2 1.3 collective-permute-start.2
  32.5 1.3 collective-permute-start.3
  33.8 0.1 multiply_reduce_fusion.1
  34.0 0.0 copy-start.5
  34.0 0.1 sub.96
  34.1 0.1 sub.97
  34.2 0.1 add.118
  34.2 0.1 add.119
  34.3 0.1 add.124
  34.4 0.1 add.125
  34.5 0.7 copy.40.table
  35.2 0.0 copy-done.5
  35.2 51.5 %shard_map.64.sums_in = f32[2,16,32,1024]{3,2,1,0:T(8,128)} custom-call(s32[32,5]{1,0:T(8,128)} %copy.40.table, f32[16,3]{1,0:T(8,128)} %convert_multiply_fusion.rates, s32[10]{0:T(128)} %convert_reduce_fusion.below, s32[2]{0:T(128)} %copy-done.5, s32[6]{0:T(128)} %stack.52.pos, f32[16,32,1024]{2,1,0:T(8,128)} %values.1), custom_call_target="tpu_custom_call" | custom-call | tf_op jit(solution)/shard_map/pallas_call | solution.py:278
  86.8 0.0 collective-permute-done.4.before
  86.8 0.0 collective-permute-done.5.after
  86.8 1.0 copy-done.4
  87.8 64.0 %shard_map.65.sums_in = f32[2,16,32,1024]{3,2,1,0:T(8,128)} custom-call(s32[32,5]{1,0:T(8,128)} %copy.40.table, f32[16,3]{1,0:T(8,128)} %convert_multiply_fusion.rates, s32[10]{0:T(128)} %convert_reduce_fusion.below, s32[2]{0:T(128)} %copy-done.5, s32[6]{0:T(128)} %stack.52.pos, f32[16,16,1024]{2,1,0:T(8,128)} %copy-done.1, ...), custom_call_target="tpu_custom_call", output_to_operand_aliasing={{}: (9, {})} | custom-call | tf_op jit(solution)/shard_map/pallas_call | solution.py:278
  151.7 0.0 collective-permute-done.2.low_before.high_before
  151.7 0.0 collective-permute-done.3.low_after.high_after
  151.7 0.8 copy-done.2
  152.5 0.8 copy-done.3
  153.3 17.8 %shard_map.66 = (f32[16,32,1024]{2,1,0:T(8,128)}, f32[1,128]{1,0:T(1,128)}) custom-call(s32[32,5]{1,0:T(8,128)} %copy.40.table, f32[16,3]{1,0:T(8,128)} %convert_multiply_fusion.rates, s32[10]{0:T(128)} %convert_reduce_fusion.below, s32[2]{0:T(128)} %copy-done.5, s32[6]{0:T(128)} %stack.52.pos, f32[8,16,1024]{2,1,0:T(8,128)} %copy-done.2, ...), custom_call_target="tpu_custom_call" | custom-call | tf_op jit(solution)/shard_map/pallas_call | solution.py:278
  171.1 0.6 broadcast_in_dim.10
  171.8 14.9 %all_to_all.5 = f32[32,1,128]{2,1,0:T(1,128)S(1)} all-to-all(f32[32,1,128]{2,1,0:T(1,128)S(1)} %broadcast_in_dim.10), channel_id=1, replica_groups=mesh['scen'=2,'grid'=16] {'scen','grid'}, dimensions={0} | all-to-all | bytes 32768 | tf_op jit(solution)/shard_map/all_to_all | solution.py:388
  186.7 0.6 reduce_sum.49
  187.8 3.2 %broadcast_subtract_fusion = f32[16,32,1024]{2,1,0:T(8,128)} fusion(f32[16,32,1024]{2,1,0:T(8,128)} %get-tuple-element.7, f32[]{:T(128)S(6)} %div.7), kind=kLoop, calls=%fused_computation | loop fusion | flops 524288 | bytes 4194308 | tf_op jit(solution)/shard_map/sub | solution.py:389
  (23 shorter events, 0.1 us)
Async XLA Ops:
  0.0 5.4 %copy-start = (f32[16,32,1024]{2,1,0:T(8,128)S(1)}, f32[16,32,1024]{2,1,0:T(8,128)}, u32[]{:S(2)}) copy-start(f32[16,32,1024]{2,1,0:T(8,128)} %values.1) | copy-start | bytes 6291460
  0.0 13.2 %collective-permute-start = (s32[1]{0:T(128)}, s32[1]{0:T(128)}, u32[]{:S(2)}, u32[]{:S(2)}) collective-permute-start(s32[1]{0:T(128)} %param.7), channel_id=1, source_target_pairs={{0,16},{16,0},{1,17},{17,1},{2,18},{18,2},{3,19},{19,3},{4,20},{20... | collective-permute-start | bytes 20 | tf_op jit(solution)/shard_map/ppermute | solution.py:309
  5.2 4.6 %copy-start.7 = (s32[16,3]{0,1:T(4,128)S(1)}, s32[16,3]{0,1:T(4,128)}, u32[]{:S(2)}) copy-start(s32[16,3]{0,1:T(4,128)} %param.9) | copy-start | bytes 580
  5.3 6.0 %copy-start.8 = (f32[3]{0:T(128)S(1)}, f32[3]{0:T(128)}, u32[]{:S(2)}) copy-start(f32[3]{0:T(128)} %param.10) | copy-start | bytes 40
  5.3 6.0 %copy-start.9 = (f32[3]{0:T(128)S(1)}, f32[3]{0:T(128)}, u32[]{:S(2)}) copy-start(f32[3]{0:T(128)} %constant.52) | copy-start | bytes 40
  5.3 24.8 %collective-permute-start.1 = (f32[16,16,1024]{2,1,0:T(8,128)}, f32[16,16,1024]{2,1,0:T(8,128)S(1)}, u32[]{:S(2)}, u32[]{:S(2)}) collective-permute-start(f32[16,16,1024]{2,1,0:T(8,128)} %constant_dynamic-slice_fusion), channel_id=1, source_target_pairs={{0,16},{16,0},{1,17},{17,1},{2,18},{18,2},{3,19},{19,3},{4,20},{20... | collective-permute-start | bytes 3145736 | tf_op jit(solution)/shard_map/ppermute | solution.py:316
  6.9 26.9 %copy-start.6 = (s32[12,3]{0,1:T(4,128)S(1)}, s32[12,3]{0,1:T(4,128)}, u32[]{:S(2)}) copy-start(s32[12,3]{0,1:T(4,128)} %param.8) | copy-start | bytes 436
  6.9 79.8 %collective-permute-start.4 = (f32[8,32,1024]{2,1,0:T(8,128)}, f32[8,32,1024]{2,1,0:T(8,128)S(1)}, u32[]{:S(2)}, u32[]{:S(2)}) collective-permute-start(f32[8,32,1024]{2,1,0:T(8,128)} %get-tuple-element.14), channel_id=1, source_target_pairs={{0,1},{1,2},{2,3},{3,4},{4,5},{5,6},{6,7},{7,8},{8,9},{9,10},{10,1... | collective-permute-start | bytes 3145736 | tf_op jit(solution)/shard_map/ppermute | solution.py:296
  8.6 78.2 %collective-permute-start.5 = (f32[8,32,1024]{2,1,0:T(8,128)}, f32[8,32,1024]{2,1,0:T(8,128)}, u32[]{:S(2)}, u32[]{:S(2)}) collective-permute-start(f32[8,32,1024]{2,1,0:T(8,128)} %get-tuple-element.13), channel_id=1, source_target_pairs={{1,0},{2,1},{3,2},{4,3},{5,4},{6,5},{7,6},{8,7},{9,8},{10,9},{11,1... | collective-permute-start | bytes 3145736 | tf_op jit(solution)/shard_map/ppermute | solution.py:291
  30.1 56.7 %copy-start.1 = (f32[16,16,1024]{2,1,0:T(8,128)}, f32[16,16,1024]{2,1,0:T(8,128)S(1)}, u32[]{:S(2)}) copy-start(f32[16,16,1024]{2,1,0:T(8,128)S(1)} %collective-permute-done.1.low.high) | copy-start | bytes 3145732
  31.2 120.5 %collective-permute-start.2 = (f32[8,16,1024]{2,1,0:T(8,128)}, f32[8,16,1024]{2,1,0:T(8,128)S(1)}, u32[]{:S(2)}, u32[]{:S(2)}) collective-permute-start(f32[8,16,1024]{2,1,0:T(8,128)} %get-tuple-element.16), channel_id=1, source_target_pairs={{0,1},{1,2},{2,3},{3,4},{4,5},{5,6},{6,7},{7,8},{8,9},{9,10},{10,1... | collective-permute-start | bytes 1572872 | tf_op jit(solution)/shard_map/ppermute | solution.py:296
  32.5 119.2 %collective-permute-start.3 = (f32[8,16,1024]{2,1,0:T(8,128)}, f32[8,16,1024]{2,1,0:T(8,128)S(1)}, u32[]{:S(2)}, u32[]{:S(2)}) collective-permute-start(f32[8,16,1024]{2,1,0:T(8,128)} %get-tuple-element.15), channel_id=1, source_target_pairs={{1,0},{2,1},{3,2},{4,3},{5,4},{6,5},{7,6},{8,7},{9,8},{10,9},{11,1... | collective-permute-start | bytes 1572872 | tf_op jit(solution)/shard_map/ppermute | solution.py:291
  34.0 1.2 copy-start.5
  86.8 1.0 copy-start.4
  151.7 0.8 copy-start.2
  152.5 0.8 copy-start.3

commit v2 on v1

v2 whole, which is shorter than its diff:
```python
import functools

import jax
import jax.numpy as jnp
from jax import lax
from jax.experimental import pallas as pl
from jax.experimental.pallas import tpu as pltpu
from jax.sharding import PartitionSpec as P

H = 8
LOW, HIGH = H, 2 * H
SUB, LANES = 8, 128
softness = 0.5

SHIFT_A, OFFSET = range(2)
UNROLL = 2
FIRST_ROW, LAST_ROW, FIRST_DEPTH, LAST_DEPTH = range(4)


class Sizes:
    def __init__(self, rows, depth, width, scenarios, releases):
        self.rows, self.depth, self.width = rows, depth, width
        self.scenarios, self.releases = scenarios, releases
        self.listed = releases + UNROLL - 1
        self.planes = width // LANES
        self.group = LANES // self.planes
        self.strips = depth // SUB
        self.planes_ext = LOW + self.planes + HIGH
        self.depth_ext = LOW + depth + HIGH
        self.row_size = self.planes_ext * self.depth_ext

    def place(self, lane):
        return lane % self.planes * self.group + lane // self.planes

    def lane(self, place):
        return place % self.group * self.planes + place // self.group


def transpose(blocks):
    lane = lax.broadcasted_iota(jnp.int32, (SUB, LANES), 1)
    blocks = list(blocks)
    step = 1
    while step < len(blocks):
        odd = (lane // step) % 2 == 1
        for i in range(len(blocks)):
            if i // step % 2 == 0:
                first, second = blocks[i], blocks[i + step]
                blocks[i] = jnp.where(odd, pltpu.roll(second, step, 1), first)
                blocks[i + step] = jnp.where(odd, second, pltpu.roll(first, LANES - step, 1))
        step *= 2
    return blocks


def put(weights, sizes, row, at, values):
    lane = lax.broadcasted_iota(jnp.int32, (SUB, LANES), 1)
    for strip in range(values.shape[0] // SUB):
        levels = slice(strip * SUB, strip * SUB + SUB)
        base = row * sizes.row_size + at + strip * SUB
        planes = transpose(
            jnp.exp(values[levels, block * LANES : block * LANES + LANES] * (-1.0 / softness)) for block in range(sizes.planes)
        )

        def store(beyond, moved):
            for plane in range(sizes.planes):
                to = LOW + beyond * sizes.planes + plane
                if 0 <= to < sizes.planes_ext:
                    weights[pl.ds(base + to * sizes.depth_ext, SUB), :] = moved[plane]

        store(0, planes)
        for up in (False, True):
            turn = LANES - 1 if up else 1
            next_lane = [pltpu.roll(plane, turn, 1) for plane in planes]
            last = LANES - 1 if up else 0
            for beyond in range(1, -(-(HIGH if up else LOW) // sizes.planes) + 1):
                wrap = beyond * sizes.planes
                wrapped = lane < wrap if up else lane >= LANES - wrap
                moved = [
                    pltpu.roll(jnp.where(wrapped, there, plane), LANES - wrap if up else wrap, 1)
                    for plane, there in zip(planes, next_lane, strict=True)
                ]
                place = sizes.place(lane)
                past = place + beyond > last if up else place < beyond
                end = jnp.broadcast_to(planes[-1 if up else 0][:, last : last + 1], (SUB, LANES))
                store(beyond if up else -beyond, [jnp.where(past, end, plane) for plane in moved])


def repeat(weights, sizes, row, source, at, count):
    for plane in range(sizes.planes_ext):
        base = row * sizes.row_size + plane * sizes.depth_ext
        level = jnp.broadcast_to(weights[pl.ds(base + source, 1), :], (SUB, LANES))
        for strip in range(count // SUB):
            weights[pl.ds(base + at + strip * SUB, SUB), :] = level


def put_zeros(weights, sizes, row, at, count):
    zero = jnp.zeros((SUB, LANES), jnp.float32)
    for strip in range(count // SUB):
        for plane in range(sizes.planes_ext):
            weights[pl.ds(row * sizes.row_size + plane * sizes.depth_ext + at + strip * SUB, SUB), :] = zero


def put_row(weights, sizes, pos, row, own, low, high):
    if own is None:
        put_zeros(weights, sizes, row, LOW, sizes.depth)
    else:
        put(weights, sizes, row, LOW, own)
    for is_end, at, count, beyond, edge in (
        (pos[FIRST_DEPTH] != 0, 0, LOW, low, LOW),
        (pos[LAST_DEPTH] != 0, LOW + sizes.depth, HIGH, high, LOW + sizes.depth - 1),
    ):

        @pl.when(is_end)
        def _():
            if own is None:
                put_zeros(weights, sizes, row, at, count)
            else:
                repeat(weights, sizes, row, edge, at, count)

        @pl.when(jnp.logical_not(is_end))
        def _():
            if beyond is None:
                put_zeros(weights, sizes, row, at, count)
            else:
                put(weights, sizes, row, at, beyond())


def add_term(sums, table, heights, gains, depths, weights, sizes, scenario, row, first, count, release, source_row):
    at = scenario * sizes.listed + release
    base = source_row(row + table[at, SHIFT_A]) * sizes.row_size + table[at, OFFSET] + first * SUB
    height = heights[at, row]
    out = []
    factors = [
        depths[pl.ds(pl.multiple_of(release * sizes.depth + (first + strip) * SUB, SUB), SUB), :] * height for strip in range(count)
    ]
    for plane in range(sizes.planes):
        gain = gains[pl.ds(pl.multiple_of((release * sizes.planes + plane) * SUB, SUB), SUB), :]
        for strip in range(count):
            landed = weights[pl.ds(base + plane * sizes.depth_ext + strip * SUB, SUB), :]
            out.append(sums[plane * count + strip] + landed * (gain * factors[strip]))
    return out


def own_row(sizes):
    return lambda r: jnp.clip(r, 0, sizes.rows - 1)


def outside_row(sizes):
    return lambda r: jnp.clip(jnp.where(r < 0, r + H, r - sizes.rows + H), 0, 2 * H - 1)


def load_sums(ref, sizes, scenario, row, first, count):
    return tuple(
        ref[scenario, row, plane, pl.ds(pl.multiple_of((first + strip) * SUB, SUB), SUB), :]
        for plane in range(sizes.planes)
        for strip in range(count)
    )


def store_sums(ref, sizes, scenario, row, first, count, sums):
    for plane in range(sizes.planes):
        for strip in range(count):
            ref[scenario, row, plane, pl.ds(pl.multiple_of((first + strip) * SUB, SUB), SUB), :] = sums[plane * count + strip]


def own_range(below, inflow, pos, sizes, scenario, row):
    top = row + inflow[scenario]
    start = jnp.where(pos[LAST_ROW] != 0, 0, below[jnp.clip(top - sizes.rows + 1, 0, H + 1)])
    stop = jnp.where(pos[FIRST_ROW] != 0, sizes.releases, below[jnp.clip(top + 1, 0, H + 1)])
    return start, stop


def own_terms(load, store, table, heights, gains, depths, weights, sizes, first, count):
    def work(index, _):
        scenario, row = index // sizes.rows, index % sizes.rows
        sums = load(scenario, row, first, count)
        for release in range(sizes.releases):
            sums = add_term(sums, table, heights, gains, depths, weights, sizes, scenario, row, first, count, release, own_row(sizes))
        store(scenario, row, first, count, sums)
        return 0

    lax.fori_loop(0, sizes.scenarios * sizes.rows, work, 0)


def own_kernel(sizes, table, heights, below, inflow, pos, gains, depths, values, sums_out, weights):
    def fill(row, _):
        put_row(weights, sizes, pos, row, values[row], None, None)
        return 0

    lax.fori_loop(0, sizes.rows, fill, 0)
    zero = jnp.zeros((SUB, LANES), jnp.float32)

    def load(scenario, row, first, count):
        return [zero] * (sizes.planes * count)

    step = min(sizes.strips, 4)
    for first in range(0, sizes.strips, step):
        own_terms(
            load, functools.partial(store_sums, sums_out, sizes), table, heights, gains, depths, weights, sizes, first,
            min(step, sizes.strips - first),
        )


def beyond_levels(pair, pos, low_ref, high_ref, row):
    return lambda: low_ref[row, low_ref.shape[1] - LOW :], lambda: high_ref[row, :HIGH]


def edge_strips(sizes, pos, pair):
    count = min(HIGH // SUB, sizes.strips)
    if pair:
        return jnp.where(pos[FIRST_DEPTH] != 0, sizes.strips - count, 0), count
    return 0, sizes.strips


def outside_terms(ref_in, ref_out, table, heights, below, inflow, pos, gains, depths, weights, sizes, first, count):
    def work(index, _):
        scenario, row = index // sizes.rows, index % sizes.rows
        top = row + inflow[scenario]
        start = jnp.where(pos[LAST_ROW] != 0, 0, below[jnp.clip(top - sizes.rows + 1, 0, H + 1)])
        stop = jnp.where(pos[FIRST_ROW] != 0, sizes.releases, below[jnp.clip(top + 1, 0, H + 1)])

        def some(lo, hi):
            @pl.when(lo < hi)
            def _():
                def step(index, sums):
                    for k in range(UNROLL):
                        sums = add_term(
                            sums, table, heights, gains, depths, weights, sizes, scenario, row, first, count, lo + index * UNROLL + k,
                            outside_row(sizes),
                        )
                    return tuple(sums)

                sums = lax.fori_loop(0, (hi - lo + UNROLL - 1) // UNROLL, step, load_sums(ref_in, sizes, scenario, row, first, count))
                store_sums(ref_out, sizes, scenario, row, first, count, sums)

        some(0, start)
        some(stop, sizes.releases)
        return 0

    lax.fori_loop(0, sizes.scenarios * sizes.rows, work, 0)


def edge_kernel(
    sizes, pair, table, heights, outside, below, inflow, pos, gains, depths, low, high, before, after, sums_in, sums_out, weights
):
    def fill_depth(row, _):
        put_row(weights, sizes, pos, row, None, *beyond_levels(pair, pos, low, high, row))
        return 0

    lax.fori_loop(0, sizes.rows, fill_depth, 0)
    first, count = edge_strips(sizes, pos, pair)
    sums_out[...] = sums_in[...]
    own_terms(
        functools.partial(load_sums, sums_out, sizes), functools.partial(store_sums, sums_out, sizes), table, heights, gains, depths,
        weights, sizes, first, count,
    )

    def fill_rows(row, _):
        put_row(weights, sizes, pos, row, before[row], None, None)
        put_row(weights, sizes, pos, row + H, after[row], None, None)
        return 0

    lax.fori_loop(0, H, fill_rows, 0)
    step = min(sizes.strips, 4)
    for first in range(0, sizes.strips, step):
        outside_terms(
            sums_out, sums_out, table, outside, below, inflow, pos, gains, depths, weights, sizes, first, min(step, sizes.strips - first)
        )


def last_kernel(
    sizes, pair, scale, table, outside, below, inflow, pos, gains, depths, low_before, high_before, low_after, high_after, sums_in,
    average_out, total_out, sums, weights,
):
    def fill_rows(row, _):
        put_row(weights, sizes, pos, row, None, *beyond_levels(pair, pos, low_before, high_before, row))
        put_row(weights, sizes, pos, row + H, None, *beyond_levels(pair, pos, low_after, high_after, row))
        return 0

    lax.fori_loop(0, H, fill_rows, 0)
    first, count = edge_strips(sizes, pos, pair)
    sums[...] = sums_in[...]
    outside_terms(sums, sums, table, outside, below, inflow, pos, gains, depths, weights, sizes, first, count)

    def finish(row, total):
        for strip in range(sizes.strips):
            levels = slice(strip * SUB, strip * SUB + SUB)
            averages = []
            for plane in range(sizes.planes):
                logs = None
                for scenario in range(0, sizes.scenarios, 2):
                    product = sums[scenario, row, plane, levels, :]
                    if scenario + 1 < sizes.scenarios:
                        product = product * sums[scenario + 1, row, plane, levels, :]
                    log = jnp.log(product)
                    logs = log if logs is None else logs + log
                averages.append(logs * scale)
                total = total + averages[-1]
            for block, average in enumerate(transpose(averages)):
                average_out[row, levels, block * LANES : block * LANES + LANES] = average
        return total

    total = lax.fori_loop(0, sizes.rows, finish, jnp.zeros((SUB, LANES), jnp.float32))
    total_out[...] = jnp.sum(total, axis=0, keepdims=True)


def call(kernel, scalars, arrays, outs, scratch, aliases=None):
    smem, vmem = pl.BlockSpec(memory_space=pltpu.SMEM), pl.BlockSpec(memory_space=pltpu.VMEM)
    return pl.pallas_call(
        kernel,
        out_shape=outs,
        in_specs=[smem] * len(scalars) + [vmem] * len(arrays),
        out_specs=jax.tree.map(lambda _: vmem, outs),
        scratch_shapes=scratch,
        input_output_aliases=aliases or {},
        compiler_params=pltpu.CompilerParams(vmem_limit_bytes=32 * 2**20),
    )(*scalars, *arrays)


def from_above(cells, axis, hops=1):
    count = lax.axis_size(axis)
    return lax.ppermute(cells, axis, [(i + hops, i) for i in range(count - hops)])


def from_below(cells, axis, hops=1):
    count = lax.axis_size(axis)
    return lax.ppermute(cells, axis, [(i, i + hops) for i in range(count - hops)])


def on_device(value_next, scenario_ids, inflow_table, release_shifts, price):
    rows, depth, width = value_next.shape
    grid_count, scen_count = lax.axis_size("grid"), lax.axis_size("scen")
    grid, scen = lax.axis_index("grid"), lax.axis_index("scen")
    total_rows, total_depth = rows * grid_count, depth * scen_count
    releases = release_shifts.shape[0]
    pair = scen_count == 2 and depth >= HIGH

    ids = [scenario_ids]
    for hop in range(1, scen_count):
        ids.append(lax.ppermute(scenario_ids, "scen", [(i, (i + hop) % scen_count) for i in range(scen_count)]))
    ids = jnp.concatenate(ids)
    sizes = Sizes(rows, depth, width, ids.shape[0], releases)

    if pair:
        start = jnp.where(scen == 0, depth - HIGH, 0)
        sent = lax.dynamic_slice_in_dim(value_next, start, HIGH, axis=1)
        low = high = lax.ppermute(sent, "scen", [(0, 1), (1, 0)])
    else:
        low, high = [], []
        for hop in range(-(-LOW // depth), 0, -1):
            low.append(from_below(value_next, "scen", hop) if hop < scen_count else jnp.zeros_like(value_next))
        for hop in range(1, -(-HIGH // depth) + 1):
            high.append(from_above(value_next, "scen", hop) if hop < scen_count else jnp.zeros_like(value_next))
        low = jnp.concatenate(low, axis=1)[:, -LOW:]
        high = jnp.concatenate(high, axis=1)[:, :HIGH]
        last = value_next[:, -1:]
        for hop in range(1, -(-HIGH // depth)):
            past = jnp.where(scen + hop == scen_count - 1, 1, 0)
            fill = high[:, hop * depth - 1 : hop * depth]
            keep = lax.broadcasted_iota(jnp.int32, high.shape, 1) < hop * depth
            high = jnp.where(jnp.logical_or(past == 0, keep), high, fill)
        del last
    before = from_below(value_next[rows - H :], "grid")
    after = from_above(value_next[:H], "grid")

    shifts = release_shifts[:, 0]
    order = jnp.arange(releases, dtype=jnp.int32)
    ahead = jnp.logical_or(
        shifts[None, :] < shifts[:, None], jnp.logical_and(shifts[None, :] == shifts[:, None], order[None, :] < order[:, None])
    )
    rank = jnp.sum(ahead.astype(jnp.int32), axis=1)
    moved = (rank[None, :] == order[:, None]).astype(jnp.int32)
    sorted_shifts = jnp.sum(moved[:, :, None] * release_shifts[None, :, :], axis=1)
    below = jnp.sum((shifts[None, :] < jnp.arange(H + 2, dtype=jnp.int32)[:, None]).astype(jnp.int32), axis=1)
    one_hot = (ids[:, None] == jnp.arange(inflow_table.shape[0], dtype=jnp.int32)[None, :]).astype(jnp.int32)
    inflows = jnp.sum(one_hot[:, :, None] * inflow_table[None, :, :], axis=1)
    u1, u2, u3 = (sorted_shifts[None, :, i] for i in range(3))
    i1, i2, i3 = (inflows[:, None, i] for i in range(3))
    shift_b = i2 + u1 - u2
    shift_c = i3 + u2 - u3
    extra = ((0, 0), (0, sizes.listed - releases), (0, 0))
    table = jnp.stack([i1 - u1, (LOW + shift_b) * sizes.depth_ext + LOW + shift_c], axis=-1)
    table = jnp.pad(table, extra).reshape(-1, 2)
    spans = jnp.array([total_rows, width, total_depth], jnp.float32)
    rates = sorted_shifts.astype(jnp.float32) * (price / (spans * (H * softness)))[None, :]
    pos = jnp.stack([grid == 0, grid == grid_count - 1, scen == 0, scen == scen_count - 1]).astype(jnp.int32)
    row_heights = (grid * rows + 1 + jnp.arange(rows, dtype=jnp.int32)).astype(jnp.float32)
    heights = jnp.exp(rates[:, :1] * row_heights[None, :])[None]
    lands = (i1 - u1)[:, :, None] + jnp.arange(rows, dtype=jnp.int32)
    is_own = jnp.logical_and(jnp.logical_or(grid == 0, lands >= 0), jnp.logical_or(grid == grid_count - 1, lands < rows))
    outside = jnp.pad(jnp.where(is_own, 0.0, heights), extra).reshape(-1, rows)
    heights = jnp.pad(jnp.where(is_own, heights, 0.0), extra).reshape(-1, rows)
    listed = ((0, sizes.listed - releases), (0, 0), (0, 0))
    level = (scen * depth + 1 + jnp.arange(depth, dtype=jnp.int32)).astype(jnp.float32)
    depths = jnp.exp(jnp.broadcast_to(rates[:, 2][:, None, None] * level[None, :, None], (releases, depth, LANES)))
    place = sizes.place(jnp.arange(LANES, dtype=jnp.int32))
    level = (place[None, :] * sizes.planes + jnp.arange(sizes.planes, dtype=jnp.int32)[:, None] + 1).astype(jnp.float32)
    gains = jnp.exp(jnp.broadcast_to((rates[:, 1][:, None, None] * level[None])[:, :, None, :], (releases, sizes.planes, SUB, LANES)))
    factors = (
        jnp.pad(gains.reshape(releases, -1, LANES), listed).reshape(-1, LANES),
        jnp.pad(depths, listed).reshape(-1, LANES),
    )

    sums_shape = jax.ShapeDtypeStruct((sizes.scenarios, rows, sizes.planes, depth, LANES), jnp.float32)
    ext = pltpu.VMEM((max(rows, 2 * H) * sizes.row_size, LANES), jnp.float32)
    sums = call(functools.partial(own_kernel, sizes), (table, heights, below, inflows[:, 0], pos), (*factors, value_next), sums_shape, [ext])

    low, high, sums = lax.optimization_barrier((low, high, sums))

    if pair:
        low_before = high_before = from_below(low[rows - H :], "grid")
        low_after = high_after = from_above(low[:H], "grid")
    else:
        both = jnp.concatenate([low, high], axis=1)
        both_before, both_after = from_below(both[rows - H :], "grid"), from_above(both[:H], "grid")
        low_before, high_before = both_before[:, :LOW], both_before[:, LOW:]
        low_after, high_after = both_after[:, :LOW], both_after[:, LOW:]

    sums = call(
        functools.partial(edge_kernel, sizes, pair), (table, heights, outside, below, inflows[:, 0], pos), (*factors, low, high, before, after, sums), sums_shape, [ext],
        {12: 0},
    )

    scale = -softness / sizes.scenarios
    average, total = call(
        functools.partial(last_kernel, sizes, pair, scale), (table, outside, below, inflows[:, 0], pos), (*factors, low_before, high_before, low_after, high_after, sums),
        (jax.ShapeDtypeStruct(value_next.shape, jnp.float32), jax.ShapeDtypeStruct((1, LANES), jnp.float32)),
        [pltpu.VMEM(sums_shape.shape, jnp.float32), pltpu.VMEM((2 * H * sizes.row_size, LANES), jnp.float32)],
    )
    devices = grid_count * scen_count
    totals = lax.all_to_all(jnp.broadcast_to(total[None], (devices, 1, LANES)), ("scen", "grid"), 0, 0, tiled=True)
    return average - jnp.sum(totals) / float(total_rows * total_depth * width)


def solution(mesh):
    placed = (P("grid", "scen", None), P("scen"), P(), P(), P())
    return jax.shard_map(
        on_device, mesh=mesh, in_specs=placed, out_specs=P("grid", "scen", None), check_vma=False
    )
```

time: 191 us -> 116 us (0.61)
  Pallas kernels: 133 us -> 62.6 us
  waiting for transfers between devices: 16.1 us -> 0.02 us
  local copies, waits for them, and re-layouts: 10.4 us -> 17.2 us
  starting transfers between devices: 8.63 us -> 13 us
    pallas_call x3, Pallas kernels: 133 us -> 62.6 us  [call(): pl.pallas_call(kernel, out_shape=outs, in_specs=[smem] * len(scalars) + [...]
    ppermute x1, waiting for transfers between devices: 16.1 us -> 0.01 us  [on_device(): low = high = lax.ppermute(sent, 'scen', [(0, 1), (1, 0)])]
    unnamed x20 -> x24, local copies, waits for them, and re-layouts: 2.59 us -> 10.7 us
    ppermute x2, starting transfers between devices: 2.95 us -> 7.22 us  [from_below(): lax.ppermute(cells, axis, [(i, i + hops) for i in range(count - hops)])]
  transfers between devices with their start and end apart: 6 -> 6, of which waited for: 1 -> 0; matrix products, arithmetic and copies ran while one was open for 5% -> 7% of each run, Pallas kernels for 60% -> 41%
where the time goes in v2:
time: 116 us; the launch traced here: 115 us
  Pallas kernels  62.6 us (54%)
  local copies, waits for them, and re-layouts  17.2 us (15%)
  blocking collectives  14.8 us (13%)
  starting transfers between devices  13 us (11%)
  other arithmetic  5.83 us (5%)
  between operations  1.53 us (1%)
    pallas_call x3, Pallas kernels, call(): pl.pallas_call(kernel, out_shape=outs, in_specs=[smem] * len(scalars) + [...  62.6 us
    all_to_all x1, blocking collectives, on_device(): lax.all_to_all(jnp.broadcast_to(total[None], (devices, 1, LANES)), ('scen...  14.8 us
    unnamed x24, local copies, waits for them, and re-layouts  10.7 us
    ppermute x2, starting transfers between devices, from_below(): lax.ppermute(cells, axis, [(i, i + hops) for i in range(count - hops)])  7.22 us
    sub x1, other arithmetic, on_device(): return average - jnp.sum(totals) / float(total_rows * total_depth * width)  3.21 us
    ppermute x1, starting transfers between devices, on_device(): lax.ppermute(scenario_ids, 'scen', [(i, (i + hop) % scen_count) for i in...  2.94 us
    ppermute x2, starting transfers between devices, from_above(): lax.ppermute(cells, axis, [(i + hops, i) for i in range(count - hops)])  2.69 us
  transfers between devices with their start and end apart: 6, of which 0 were waited for; matrix products, arithmetic and copies ran while one was open for 7% of the time, Pallas kernels for 41%

profile of v2, /device:TPU:0, one launch (start us, length us, event | category | flops | bytes accessed | tf_op | source)
XLA Modules:
  0.0 114.9 jit_solution(15423492034735023980)
XLA Ops:
  0.0 2.9 %collective-permute-start = (s32[1]{0:T(128)}, s32[1]{0:T(128)}, u32[]{:S(2)}, u32[]{:S(2)}) collective-permute-start(s32[1]{0:T(128)} %param.7), channel_id=1, source_target_pairs={{0,16},{16,0},{1,17},{17,1},{2,18},{18,2},{3,19},{19,3},{4,20},{20... | collective-permute-start | bytes 20 | tf_op jit(solution)/shard_map/ppermute | solution.py:339
  2.9 2.3 %constant_dynamic-slice_fusion = f32[16,16,1024]{2,1,0:T(8,128)} fusion(f32[16,32,1024]{2,1,0:T(8,128)} %values.1, s32[]{:T(128)S(6)} %select_n.36), kind=kLoop, calls=%fused_computation.47 | loop fusion | bytes 2097156 | tf_op jit(solution)/shard_map/dynamic_slice | solution.py:345
  5.3 0.2 collective-permute-start.1
  5.4 1.5 %fusion.6 = (f32[8,32,1024]{2,1,0:T(8,128)}, f32[8,32,1024]{2,1,0:T(8,128)}) fusion(f32[16,32,1024]{2,1,0:T(8,128)S(1)} %copy-done.4), kind=kLoop, calls=%fused_computation.48 | loop fusion | bytes 4194304 | tf_op jit(solution)/shard_map/slice | solution.py:363
  6.9 1.4 %collective-permute-start.5 = (f32[8,32,1024]{2,1,0:T(8,128)}, f32[8,32,1024]{2,1,0:T(8,128)}, u32[]{:S(2)}, u32[]{:S(2)}) collective-permute-start(f32[8,32,1024]{2,1,0:T(8,128)} %get-tuple-element.15), channel_id=1, source_target_pairs={{1,0},{2,1},{3,2},{4,3},{5,4},{6,5},{7,6},{8,7},{9,8},{10,9},{11,1... | collective-permute-start | bytes 3145736 | tf_op jit(solution)/shard_map/ppermute | solution.py:321
  8.3 4.0 %collective-permute-start.4 = (f32[8,32,1024]{2,1,0:T(8,128)}, f32[8,32,1024]{2,1,0:T(8,128)}, u32[]{:S(2)}, u32[]{:S(2)}) collective-permute-start(f32[8,32,1024]{2,1,0:T(8,128)} %get-tuple-element.16), channel_id=1, source_target_pairs={{0,1},{1,2},{2,3},{3,4},{4,5},{5,6},{6,7},{7,8},{8,9},{9,10},{10,1... | collective-permute-start | bytes 3145736 | tf_op jit(solution)/shard_map/ppermute | solution.py:326
  13.0 0.1 convert_reduce_fusion.below
  13.1 0.2 convert_reduce_fusion.1
  13.4 0.1 multiply_reduce_fusion
  13.6 0.1 convert_multiply_fusion
  13.6 0.1 multiply_exponential_fusion
  13.8 0.1 multiply_exponential_fusion.1
  13.9 0.1 broadcast_in_dim.27
  14.0 0.9 pad.21
  14.9 0.1 multiply_exponential_fusion.2
  15.0 0.1 add_convert_fusion.1.pos
  15.1 0.0 collective-permute-done
  15.1 0.7 pad_add_fusion.1
  15.8 0.1 compare_convert_fusion
  15.8 0.1 multiply_reduce_fusion.1
  16.0 0.1 broadcast_subtract_fusion.1
  16.1 0.1 broadcast_subtract_fusion.2
  16.2 0.1 reshape.418
  16.2 0.1 copy.34.table
  16.4 0.1 reshape.423
  16.5 0.1 copy.30.heights
  16.6 1.1 copy-done.5
  17.6 21.2 %shard_map.64.sums_in = f32[2,16,8,32,128]{4,3,2,1,0:T(8,128)S(1)} custom-call(s32[34,2]{1,0:T(8,128)S(1)} %copy.34.table, f32[34,16]{1,0:T(8,128)S(1)} %copy.30.heights, s32[10]{0:T(128)S(1)} %convert_reduce_fusion.below, s32[2]{0:T(128)S(1)} %get-tuple-element.24.inflow, s32[4]{0:T(128)S(1)} %add_convert_fusion.1.pos, f32[1088,128]{1,0:T(8,128)S(1)} %bitcast.36, ...), custom_call_target="tpu_custom_call" | custom-call | tf_op jit(solution)/shard_map/pallas_call | solution.py:308
  38.9 1.9 %copy-done = f32[2,16,8,32,128]{4,3,2,1,0:T(8,128)} copy-done((f32[2,16,8,32,128]{4,3,2,1,0:T(8,128)}, f32[2,16,8,32,128]{4,3,2,1,0:T(8,128)S(1)}, u32[]{:S(2)}) %copy-start) | copy-done | bytes 4194328
  40.8 0.0 collective-permute-done.1.low.high
  40.8 1.1 fusion.7
  41.9 1.3 %collective-permute-start.3 = (f32[8,16,1024]{2,1,0:T(8,128)}, f32[8,16,1024]{2,1,0:T(8,128)S(1)}, u32[]{:S(2)}, u32[]{:S(2)}) collective-permute-start(f32[8,16,1024]{2,1,0:T(8,128)} %get-tuple-element.17), channel_id=1, source_target_pairs={{1,0},{2,1},{3,2},{4,3},{5,4},{6,5},{7,6},{8,7},{9,8},{10,9},{11,1... | collective-permute-start | bytes 1572872 | tf_op jit(solution)/shard_map/ppermute | solution.py:321
  43.2 3.2 %collective-permute-start.2 = (f32[8,16,1024]{2,1,0:T(8,128)}, f32[8,16,1024]{2,1,0:T(8,128)S(1)}, u32[]{:S(2)}, u32[]{:S(2)}) collective-permute-start(f32[8,16,1024]{2,1,0:T(8,128)} %get-tuple-element.18), channel_id=1, source_target_pairs={{0,1},{1,2},{2,3},{3,4},{4,5},{5,6},{6,7},{7,8},{8,9},{9,10},{10,1... | collective-permute-start | bytes 1572872 | tf_op jit(solution)/shard_map/ppermute | solution.py:326
  46.4 0.1 reshape.419
  46.5 0.1 copy.35.outside
  46.6 0.0 collective-permute-done.5.after
  46.6 0.0 collective-permute-done.4.before
  46.6 2.2 %copy-done.1 = f32[2,16,8,32,128]{4,3,2,1,0:T(8,128)S(1)} copy-done((f32[2,16,8,32,128]{4,3,2,1,0:T(8,128)S(1)}, f32[2,16,8,32,128]{4,3,2,1,0:T(8,128)}, u32[]{:S(2)}) %copy-start.1) | copy-done | bytes 4194328
  48.8 25.9 %shard_map.65.sums_in = f32[2,16,8,32,128]{4,3,2,1,0:T(8,128)S(1)} custom-call(s32[34,2]{1,0:T(8,128)S(1)} %copy.34.table, f32[34,16]{1,0:T(8,128)S(1)} %copy.30.heights, f32[34,16]{1,0:T(8,128)S(1)} %copy.35.outside, s32[10]{0:T(128)S(1)} %convert_reduce_fusion.below, s32[2]{0:T(128)S(1)} %get-tuple-element.24.inflow, ...), custom_call_target="tpu_custom_call", output_to_operand_aliasing={{}: (12, {})} | custom-call | tf_op jit(solution)/shard_map/pallas_call | solution.py:308
  74.7 1.9 %copy-done.2 = f32[2,16,8,32,128]{4,3,2,1,0:T(8,128)} copy-done((f32[2,16,8,32,128]{4,3,2,1,0:T(8,128)}, f32[2,16,8,32,128]{4,3,2,1,0:T(8,128)S(1)}, u32[]{:S(2)}) %copy-start.2) | copy-done | bytes 4194328
  76.7 0.0 collective-permute-done.3.low_after.high_after
  76.7 2.2 %copy-done.3 = f32[2,16,8,32,128]{4,3,2,1,0:T(8,128)S(1)} copy-done((f32[2,16,8,32,128]{4,3,2,1,0:T(8,128)S(1)}, f32[2,16,8,32,128]{4,3,2,1,0:T(8,128)}, u32[]{:S(2)}) %copy-start.3) | copy-done | bytes 4194328
  78.9 15.4 %shard_map.66 = (f32[16,32,1024]{2,1,0:T(8,128)S(1)}, f32[1,128]{1,0:T(1,128)S(1)}) custom-call(s32[34,2]{1,0:T(8,128)S(1)} %copy.34.table, f32[34,16]{1,0:T(8,128)S(1)} %copy.35.outside, s32[10]{0:T(128)S(1)} %convert_reduce_fusion.below, s32[2]{0:T(128)S(1)} %get-tuple-element.24.inflow, s32[4]{0:T(128)S(1)} %add_convert_fusion.1.pos, ...), custom_call_target="tpu_custom_call" | custom-call | tf_op jit(solution)/shard_map/pallas_call | solution.py:308
  94.3 0.0 copy-start.7
  94.3 1.3 %copy-done.7 = f32[16,32,1024]{2,1,0:T(8,128)} copy-done((f32[16,32,1024]{2,1,0:T(8,128)}, f32[16,32,1024]{2,1,0:T(8,128)S(1)}, u32[]{:S(2)}) %copy-start.7) | copy-done | bytes 2097176
  95.6 14.8 %all_to_all.5 = f32[32,1,128]{2,1,0:T(1,128)S(1)} all-to-all(f32[32,1,128]{2,1,0:T(1,128)S(1)} %broadcast_in_dim.33), channel_id=1, replica_groups=mesh['scen'=2,'grid'=16] {'scen','grid'}, dimensions={0} | all-to-all | bytes 32768 | tf_op jit(solution)/shard_map/all_to_all | solution.py:430
  110.4 0.7 reduce_sum.49
  111.7 3.2 %broadcast_subtract_fusion = f32[16,32,1024]{2,1,0:T(8,128)} fusion(f32[16,32,1024]{2,1,0:T(8,128)} %copy-done.7, f32[]{:T(128)S(6)} %div.17), kind=kLoop, calls=%fused_computation | loop fusion | flops 524288 | bytes 4194308 | tf_op jit(solution)/shard_map/sub | solution.py:431
  (36 shorter events, 0.2 us)
Async XLA Ops:
  0.0 5.4 %copy-start.4 = (f32[16,32,1024]{2,1,0:T(8,128)S(1)}, f32[16,32,1024]{2,1,0:T(8,128)}, u32[]{:S(2)}) copy-start(f32[16,32,1024]{2,1,0:T(8,128)} %values.1) | copy-start | bytes 6291460
  0.0 15.1 %collective-permute-start = (s32[1]{0:T(128)}, s32[1]{0:T(128)}, u32[]{:S(2)}, u32[]{:S(2)}) collective-permute-start(s32[1]{0:T(128)} %param.7), channel_id=1, source_target_pairs={{0,16},{16,0},{1,17},{17,1},{2,18},{18,2},{3,19},{19,3},{4,20},{20... | collective-permute-start | bytes 20 | tf_op jit(solution)/shard_map/ppermute | solution.py:339
  5.2 7.7 %copy-start.9 = (s32[16,3]{0,1:T(4,128)S(1)}, s32[16,3]{0,1:T(4,128)}, u32[]{:S(2)}) copy-start(s32[16,3]{0,1:T(4,128)} %param.9) | copy-start | bytes 580
  5.3 8.3 %copy-start.10 = (f32[3]{0:T(128)S(1)}, f32[3]{0:T(128)}, u32[]{:S(2)}) copy-start(f32[3]{0:T(128)} %param.10) | copy-start | bytes 40
  5.3 8.3 %copy-start.11 = (f32[3]{0:T(128)S(1)}, f32[3]{0:T(128)}, u32[]{:S(2)}) copy-start(f32[3]{0:T(128)} %constant.80) | copy-start | bytes 40
  5.3 35.5 %collective-permute-start.1 = (f32[16,16,1024]{2,1,0:T(8,128)}, f32[16,16,1024]{2,1,0:T(8,128)S(1)}, u32[]{:S(2)}, u32[]{:S(2)}) collective-permute-start(f32[16,16,1024]{2,1,0:T(8,128)} %constant_dynamic-slice_fusion), channel_id=1, source_target_pairs={{0,16},{16,0},{1,17},{17,1},{2,18},{18,2},{3,19},{19,3},{4,20},{20... | collective-permute-start | bytes 3145736 | tf_op jit(solution)/shard_map/ppermute | solution.py:346
  6.9 8.9 %copy-start.8 = (s32[12,3]{0,1:T(4,128)S(1)}, s32[12,3]{0,1:T(4,128)}, u32[]{:S(2)}) copy-start(s32[12,3]{0,1:T(4,128)} %param.8) | copy-start | bytes 436
  6.9 39.7 %collective-permute-start.5 = (f32[8,32,1024]{2,1,0:T(8,128)}, f32[8,32,1024]{2,1,0:T(8,128)}, u32[]{:S(2)}, u32[]{:S(2)}) collective-permute-start(f32[8,32,1024]{2,1,0:T(8,128)} %get-tuple-element.15), channel_id=1, source_target_pairs={{1,0},{2,1},{3,2},{4,3},{5,4},{6,5},{7,6},{8,7},{9,8},{10,9},{11,1... | collective-permute-start | bytes 3145736 | tf_op jit(solution)/shard_map/ppermute | solution.py:321
  8.3 38.3 %collective-permute-start.4 = (f32[8,32,1024]{2,1,0:T(8,128)}, f32[8,32,1024]{2,1,0:T(8,128)}, u32[]{:S(2)}, u32[]{:S(2)}) collective-permute-start(f32[8,32,1024]{2,1,0:T(8,128)} %get-tuple-element.16), channel_id=1, source_target_pairs={{0,1},{1,2},{2,3},{3,4},{4,5},{5,6},{6,7},{7,8},{8,9},{9,10},{10,1... | collective-permute-start | bytes 3145736 | tf_op jit(solution)/shard_map/ppermute | solution.py:326
  16.6 1.1 copy-start.5
  38.8 2.0 %copy-start = (f32[2,16,8,32,128]{4,3,2,1,0:T(8,128)}, f32[2,16,8,32,128]{4,3,2,1,0:T(8,128)S(1)}, u32[]{:S(2)}) copy-start(f32[2,16,8,32,128]{4,3,2,1,0:T(8,128)S(1)} %shard_map.64.sums_in) | copy-start | bytes 12582916
  40.8 5.8 %copy-start.6 = (f32[17,64,128]{2,1,0:T(8,128)S(1)}, f32[17,64,128]{2,1,0:T(8,128)}, u32[]{:S(2)}) copy-start(f32[17,64,128]{2,1,0:T(8,128)} %pad.21) | copy-start | bytes 1671172
  41.9 34.8 %collective-permute-start.3 = (f32[8,16,1024]{2,1,0:T(8,128)}, f32[8,16,1024]{2,1,0:T(8,128)S(1)}, u32[]{:S(2)}, u32[]{:S(2)}) collective-permute-start(f32[8,16,1024]{2,1,0:T(8,128)} %get-tuple-element.17), channel_id=1, source_target_pairs={{1,0},{2,1},{3,2},{4,3},{5,4},{6,5},{7,6},{8,7},{9,8},{10,9},{11,1... | collective-permute-start | bytes 1572872 | tf_op jit(solution)/shard_map/ppermute | solution.py:321
  43.2 33.5 %collective-permute-start.2 = (f32[8,16,1024]{2,1,0:T(8,128)}, f32[8,16,1024]{2,1,0:T(8,128)S(1)}, u32[]{:S(2)}, u32[]{:S(2)}) collective-permute-start(f32[8,16,1024]{2,1,0:T(8,128)} %get-tuple-element.18), channel_id=1, source_target_pairs={{0,1},{1,2},{2,3},{3,4},{4,5},{5,6},{6,7},{7,8},{8,9},{9,10},{10,1... | collective-permute-start | bytes 1572872 | tf_op jit(solution)/shard_map/ppermute | solution.py:326
  46.6 2.2 %copy-start.1 = (f32[2,16,8,32,128]{4,3,2,1,0:T(8,128)S(1)}, f32[2,16,8,32,128]{4,3,2,1,0:T(8,128)}, u32[]{:S(2)}) copy-start(f32[2,16,8,32,128]{4,3,2,1,0:T(8,128)} %copy-done) | copy-start | bytes 12582916
  74.7 2.0 %copy-start.2 = (f32[2,16,8,32,128]{4,3,2,1,0:T(8,128)}, f32[2,16,8,32,128]{4,3,2,1,0:T(8,128)S(1)}, u32[]{:S(2)}) copy-start(f32[2,16,8,32,128]{4,3,2,1,0:T(8,128)S(1)} %shard_map.65.sums_in) | copy-start | bytes 12582916
  76.7 2.2 %copy-start.3 = (f32[2,16,8,32,128]{4,3,2,1,0:T(8,128)S(1)}, f32[2,16,8,32,128]{4,3,2,1,0:T(8,128)}, u32[]{:S(2)}) copy-start(f32[2,16,8,32,128]{4,3,2,1,0:T(8,128)} %copy-done.2) | copy-start | bytes 12582916
  94.3 1.3 %copy-start.7 = (f32[16,32,1024]{2,1,0:T(8,128)}, f32[16,32,1024]{2,1,0:T(8,128)S(1)}, u32[]{:S(2)}) copy-start(f32[16,32,1024]{2,1,0:T(8,128)S(1)} %get-tuple-element.13) | copy-start | bytes 6291460

commit v3 on v0

v3 whole, which is shorter than its diff:
```python
import functools

import jax
import jax.numpy as jnp
from jax import lax
from jax.experimental import pallas as pl
from jax.experimental.pallas import tpu as pltpu
from jax.sharding import PartitionSpec as P

H = 8
LOW, HIGH = H, 2 * H
SUB, LANES = 8, 128
TILE = 1
UNROLL = 2
softness = 0.5

SHIFT_A, OFFSET, EDGE_OFFSET = range(3)


class Sizes:
    def __init__(self, rows, depth, width, scenarios, releases, grid_count, scen_count):
        self.rows, self.depth, self.width = rows, depth, width
        self.grid_count, self.scen_count = grid_count, scen_count
        self.scenarios, self.releases = scenarios, releases
        self.listed = releases + UNROLL - 1
        self.planes = width // LANES
        self.group = LANES // self.planes
        self.strips = depth // SUB
        self.planes_ext = LOW + self.planes + HIGH
        self.depth_ext = LOW + depth + HIGH
        self.row_size = self.planes_ext * self.depth_ext
        self.pair = scen_count == 2 and depth >= HIGH
        self.edge_strips = HIGH // SUB if self.pair else self.strips
        self.edge_ext = 2 * HIGH if self.pair else self.depth_ext
        self.edge_size = self.planes_ext * self.edge_ext

    def place(self, lane):
        return lane % self.planes * self.group + lane // self.planes

    def lane(self, place):
        return place % self.group * self.planes + place // self.group


def transpose(blocks):
    lane = lax.broadcasted_iota(jnp.int32, (SUB, LANES), 1)
    blocks = list(blocks)
    step = 1
    while step < len(blocks):
        odd = (lane // step) % 2 == 1
        for i in range(len(blocks)):
            if i // step % 2 == 0:
                first, second = blocks[i], blocks[i + step]
                blocks[i] = jnp.where(odd, pltpu.roll(second, step, 1), first)
                blocks[i + step] = jnp.where(odd, second, pltpu.roll(first, LANES - step, 1))
        step *= 2
    return blocks


def turns(sizes):
    return [*range(-(-(-LOW // sizes.planes)), 0), *range(1, -(-HIGH // sizes.planes) + 1)]


def fill_turns(matrix, sizes):
    shape = (2 * LANES, LANES)
    source = lax.broadcasted_iota(jnp.int32, shape, 0) % LANES
    place = sizes.place(lax.broadcasted_iota(jnp.int32, shape, 1))
    for i, turn in enumerate(turns(sizes)):
        there = jnp.clip(place + turn, 0, LANES - 1)
        matrix[:, i * LANES : i * LANES + LANES] = (sizes.lane(there) == source).astype(jnp.float32).astype(jnp.bfloat16)


def put(weights, sizes, matrix, row_bases, depth_ext, at, rows):
    place = sizes.place(lax.broadcasted_iota(jnp.int32, (SUB, LANES), 1))
    levels = rows[0].shape[1]
    both = jnp.concatenate([row.reshape(sizes.planes * levels, LANES) for row in rows], axis=0)
    upper = both.astype(jnp.bfloat16)
    lower = (both - upper.astype(jnp.float32)).astype(jnp.bfloat16)
    turned = jnp.dot(jnp.concatenate([upper, lower], axis=1), matrix[...], preferred_element_type=jnp.float32)
    for row, row_base in enumerate(row_bases):
        for strip in range(levels // SUB):
            base = row_base + at + strip * SUB

            def part(array, plane):
                first = (row * sizes.planes + plane) * levels + strip * SUB
                return array[first : first + SUB]

            for plane in range(sizes.planes):
                weights[pl.ds(base + (LOW + plane) * depth_ext, SUB), :] = part(both, plane)
            for i, turn in enumerate(turns(sizes)):
                moved = turned[:, i * LANES : i * LANES + LANES]
                end = part(moved, sizes.planes - 1 if turn > 0 else 0)
                past = place + turn > LANES - 1 if turn > 0 else place + turn < 0
                for plane in range(sizes.planes):
                    to = LOW + turn * sizes.planes + plane
                    if 0 <= to < sizes.planes_ext:
                        weights[pl.ds(base + to * depth_ext, SUB), :] = jnp.where(past, end, part(moved, plane))


def put_zeros(weights, sizes, row_base, depth_ext, at, count):
    zero = jnp.zeros((SUB, LANES), jnp.float32)
    for strip in range(count // SUB):
        for plane in range(sizes.planes_ext):
            weights[pl.ds(row_base + plane * depth_ext + at + strip * SUB, SUB), :] = zero


def repeat(weights, sizes, row_base, depth_ext, source, at, count):
    for plane in range(sizes.planes_ext):
        base = row_base + plane * depth_ext
        level = jnp.broadcast_to(weights[pl.ds(base + source, 1), :], (SUB, LANES))
        for strip in range(count // SUB):
            weights[pl.ds(base + at + strip * SUB, SUB), :] = level


class Plan:
    def __init__(self, sizes, release, inflow, price, ids, below, order, table, gains, depths, heights, matrix):
        self.sizes, self.matrix = sizes, matrix
        fill_turns(matrix, sizes)
        self.below, self.table, self.gains, self.depths, self.heights = below, table, gains, depths, heights
        self.grid, self.scen = lax.axis_index("grid"), lax.axis_index("scen")
        self.first_row, self.last_row = self.grid == 0, self.grid == sizes.grid_count - 1
        self.first_depth, self.last_depth = self.scen == 0, self.scen == sizes.scen_count - 1
        for value in range(H + 2):
            count = jnp.int32(0)
            for r in range(sizes.releases):
                count = count + (release[0, r] < value).astype(jnp.int32)
            below[value] = count
            below[H + 2 + value] = count
        for r in range(sizes.releases):
            value = release[0, r]
            to = below[H + 2 + value]
            below[H + 2 + value] = to + 1
            order[to] = r
        for extra in range(sizes.releases, sizes.listed):
            order[extra] = 0
        self.inflow_a = [inflow[0, ids[w][0]] for w in range(sizes.scenarios)]
        inflow_b = [inflow[1, ids[w][0]] for w in range(sizes.scenarios)]
        inflow_c = [inflow[2, ids[w][0]] for w in range(sizes.scenarios)]
        sublane = lax.broadcasted_iota(jnp.int32, (SUB, LANES), 0)
        place = sizes.place(lax.broadcasted_iota(jnp.int32, (SUB, LANES), 1))
        row0, depth0 = self.grid * sizes.rows, self.scen * sizes.depth
        spans = (sizes.rows * sizes.grid_count, sizes.width, sizes.depth * sizes.scen_count)
        prices = [price[i] * (1.0 / (spans[i] * H * softness)) for i in range(3)]

        def step(listed, _):
            r = order[listed]
            u1, u2, u3 = release[0, r], release[1, r], release[2, r]
            for w in range(sizes.scenarios):
                at = w * sizes.listed + listed
                plane = LOW + inflow_b[w] + u1 - u2
                shift = inflow_c[w] + u2 - u3
                table[at, SHIFT_A] = self.inflow_a[w] - u1
                table[at, OFFSET] = plane * sizes.depth_ext + LOW + shift
                if sizes.pair:
                    shift = jnp.where(self.first_depth, jnp.maximum(shift, 0), HIGH + jnp.minimum(shift, 0))
                    table[at, EDGE_OFFSET] = plane * sizes.edge_ext + shift
                else:
                    table[at, EDGE_OFFSET] = plane * sizes.edge_ext + LOW + shift
            rate = [prices[i] * u.astype(jnp.float32) for i, u in enumerate((u1, u2, u3))]
            for plane in range(sizes.planes):
                level = (place * sizes.planes + (plane + 1)).astype(jnp.float32)
                gains[pl.ds(pl.multiple_of((listed * sizes.planes + plane) * SUB, SUB), SUB), :] = jnp.exp(level * rate[1])
            listens = jnp.where(listed < sizes.releases, 1.0, 0.0)
            for refs, start, count, which in ((heights, row0, sizes.rows, 0), (depths, depth0, sizes.depth, 2)):
                for strip in range(count // SUB):
                    level = (sublane + (start + strip * SUB + 1)).astype(jnp.float32)
                    refs[pl.ds(pl.multiple_of(listed * count + strip * SUB, SUB), SUB), :] = jnp.exp(level * rate[which]) * listens
            return 0

        lax.fori_loop(0, sizes.listed, step, 0)

    def edge_first(self):
        if self.sizes.pair:
            return jnp.where(self.first_depth, self.sizes.strips - self.sizes.edge_strips, 0)
        return 0

    def put_rows(self, weights, rows, values):
        sizes = self.sizes
        ext = sizes.depth_ext
        bases = [row * sizes.row_size for row in rows]
        put(weights, sizes, self.matrix, bases, ext, LOW, values)
        for is_end, at, count, edge in (
            (self.first_depth, 0, LOW, LOW),
            (self.last_depth, LOW + sizes.depth, HIGH, LOW + sizes.depth - 1),
        ):

            @pl.when(is_end)
            def _():
                for base in bases:
                    repeat(weights, sizes, base, ext, edge, at, count)

            @pl.when(jnp.logical_not(is_end))
            def _():
                for base in bases:
                    put_zeros(weights, sizes, base, ext, at, count)

    def put_edges(self, weights, rows, beyond):
        sizes = self.sizes
        ext = sizes.edge_ext
        bases = [row * sizes.edge_size for row in rows]
        if sizes.pair:
            put(weights, sizes, self.matrix, bases, ext, jnp.where(self.first_depth, HIGH, 0), beyond)
            for base in bases:
                put_zeros(weights, sizes, base, ext, jnp.where(self.first_depth, 0, HIGH), HIGH)
            return
        for base in bases:
            put_zeros(weights, sizes, base, ext, 0, ext)

        @pl.when(jnp.logical_not(self.first_depth))
        def _():
            put(weights, sizes, self.matrix, bases, ext, 0, [row[:, :LOW] for row in beyond])

        @pl.when(jnp.logical_not(self.last_depth))
        def _():
            put(weights, sizes, self.matrix, bases, ext, LOW + sizes.depth, [row[:, LOW:] for row in beyond])

    def gain(self, listed, plane):
        return self.gains[pl.ds(pl.multiple_of((listed * self.sizes.planes + plane) * SUB, SUB), SUB), :]

    def factors(self, row, first, count, listed):
        height = self.heights[pl.ds(listed * self.sizes.rows + row, 1), :]
        return [
            self.depths[pl.ds(pl.multiple_of(listed * self.sizes.depth + (first + strip) * SUB, SUB), SUB), :] * height
            for strip in range(count)
        ]

    def base(self, edge, scenario, source, first, listed):
        at = scenario * self.sizes.listed + listed
        if edge:
            return source * self.sizes.edge_size + self.table[at, EDGE_OFFSET], self.sizes.edge_ext
        return source * self.sizes.row_size + self.table[at, OFFSET] + first * SUB, self.sizes.depth_ext

    def fill_beyond(self, weights, row_size):
        rows = self.sizes.rows
        unroll = 4

        def fill(index, _):
            for k in range(unroll):
                at = pl.multiple_of((index * unroll + k) * SUB, SUB)
                for is_end, to, source in ((self.first_row, 0, 1), (self.last_row, rows + 1, rows)):
                    end = weights[pl.ds(source * row_size + at, SUB), :]
                    weights[pl.ds(to * row_size + at, SUB), :] = end * is_end.astype(jnp.float32)
            return 0

        lax.fori_loop(0, row_size // (SUB * unroll), fill, 0)

    def own_terms(self, load, store, weights, edge, first, strips):
        sizes = self.sizes
        together = 2 if sizes.scenarios % 2 == 0 else 1

        def work(index, _):
            row = index % sizes.rows
            scenarios = [index // sizes.rows * together + i for i in range(together)]
            bases = []
            for listed in range(sizes.releases):
                bases.append([])
                for scenario in scenarios:
                    source = jnp.clip(row + 1 + self.table[scenario * sizes.listed + listed, SHIFT_A], 0, sizes.rows + 1)
                    bases[-1].append(self.base(edge, scenario, source, first, listed))
            for from_strip, count in strip_sets(strips, TILE):
                sums = [load(scenario, row, first + from_strip, count) for scenario in scenarios]
                for listed in range(sizes.releases):
                    factors = self.factors(row, first + from_strip, count, listed)
                    for plane in range(sizes.planes):
                        gain = self.gain(listed, plane)
                        for strip in range(count):
                            weight = gain * factors[strip]
                            at = plane * count + strip
                            for i, (base, ext) in enumerate(bases[listed]):
                                landed = weights[pl.ds(base + plane * ext + (from_strip + strip) * SUB, SUB), :]
                                sums[i][at] = sums[i][at] + landed * weight
                for i, scenario in enumerate(scenarios):
                    store(scenario, row, first + from_strip, count, sums[i], from_strip + count == strips)
            return 0

        lax.fori_loop(0, sizes.scenarios // together * sizes.rows, work, 0)

    def add_outside(self, sums, weights, edge, scenario, row, first, count, listed, shift):
        sizes = self.sizes
        source = jnp.clip(row + self.table[scenario * sizes.listed + listed, SHIFT_A] + shift, 0, 2 * H - 1)
        base, ext = self.base(edge, scenario, source, first, listed)
        factors = self.factors(row, first, count, listed)
        out = []
        for plane in range(sizes.planes):
            gain = self.gain(listed, plane)
            for strip in range(count):
                landed = weights[pl.ds(base + plane * ext + strip * SUB, SUB), :]
                out.append(sums[plane * count + strip] + landed * (gain * factors[strip]))
        return out

    def outside_terms(self, sums_ref, weights, edge, first, count, done=None):
        sizes = self.sizes

        def work(index, _):
            scenario, row = index // sizes.rows, index % sizes.rows
            top = row + self.inflow_a[0]
            for w in range(1, sizes.scenarios):
                top = jnp.where(scenario == w, row + self.inflow_a[w], top)
            start = jnp.where(self.last_row, 0, self.below[jnp.clip(top - sizes.rows + 1, 0, H + 1)])
            stop = jnp.where(self.first_row, sizes.releases, self.below[jnp.clip(top + 1, 0, H + 1)])

            def some(lo, hi, shift):
                @pl.when(lo < hi)
                def _():
                    def step(index, sums):
                        for k in range(UNROLL):
                            listed = lo + index * UNROLL + k
                            listed = jnp.where(listed < hi, listed, sizes.releases)
                            sums = self.add_outside(sums, weights, edge, scenario, row, first, count, listed, shift)
                        return tuple(sums)

                    sums = tuple(load_sums(sums_ref, sizes, scenario, row, first, count))
                    sums = lax.fori_loop(0, (hi - lo + UNROLL - 1) // UNROLL, step, sums)
                    store_sums(sums_ref, sizes, scenario, row, first, count, sums)

            some(0, start, H - sizes.rows)
            some(stop, sizes.releases, H)
            if done is not None:
                done(scenario, row)
            return 0

        lax.fori_loop(0, sizes.scenarios * sizes.rows, work, 0)


def load_sums(ref, sizes, scenario, row, first, count):
    return [
        ref[scenario, row, plane, pl.ds(pl.multiple_of((first + strip) * SUB, SUB), SUB), :]
        for plane in range(sizes.planes)
        for strip in range(count)
    ]


def store_sums(ref, sizes, scenario, row, first, count, sums):
    for plane in range(sizes.planes):
        for strip in range(count):
            ref[scenario, row, plane, pl.ds(pl.multiple_of((first + strip) * SUB, SUB), SUB), :] = sums[plane * count + strip]


def strip_sets(strips, most=4):
    return [(first, min(most, strips - first)) for first in range(0, strips, most)]


def fill_pairs(count, held, fill):
    def step(index, _):
        rows = [2 * index, 2 * index + 1]
        fill(rows, [held[row] for row in rows])
        return 0

    lax.fori_loop(0, count // 2, step, 0)


def planes_kernel(sizes, values, planes_out):
    def step(row, _):
        for strip in range(sizes.strips):
            levels = slice(strip * SUB, strip * SUB + SUB)
            blocks = (
                jnp.exp(values[row, levels, block * LANES : block * LANES + LANES] * (-1.0 / softness))
                for block in range(sizes.planes)
            )
            for plane, each in enumerate(transpose(blocks)):
                planes_out[row, plane, levels, :] = each
        return 0

    lax.fori_loop(0, sizes.rows, step, 0)


def own_kernel(sizes, own, sums_out, release, inflow, price, ids, plan, weights, sums, held, sems):
    copy = pltpu.make_async_copy(own, held, sems.at[0])
    copy.start()
    plan = Plan(sizes, release, inflow, price, ids, *plan)
    copy.wait()
    fill_pairs(sizes.rows, held, lambda rows, values: plan.put_rows(weights, [row + 1 for row in rows], values))
    plan.fill_beyond(weights, sizes.row_size)
    zero = jnp.zeros((SUB, LANES), jnp.float32)

    def store(scenario, row, first, count, values, is_last):
        store_sums(sums, sizes, scenario, row, first, count, values)
        if is_last:
            pltpu.make_async_copy(sums.at[scenario, row], sums_out.at[scenario, row], sems.at[1]).start()

    plan.own_terms(lambda scenario, row, first, count: [zero] * (sizes.planes * count), store, weights, False, 0, sizes.strips)
    pltpu.make_async_copy(sums, sums_out, sems.at[1]).wait()


def edge_kernel(sizes, beyond, before, after, sums_in, sums_out, release, inflow, price, ids, plan, weights, edges, sums, held, rows_held, sems):
    copies = [
        pltpu.make_async_copy(beyond, held, sems.at[0]),
        pltpu.make_async_copy(sums_in, sums, sems.at[1]),
        pltpu.make_async_copy(before, rows_held.at[pl.ds(0, H)], sems.at[2]),
        pltpu.make_async_copy(after, rows_held.at[pl.ds(H, H)], sems.at[3]),
    ]
    for copy in copies:
        copy.start()
    plan = Plan(sizes, release, inflow, price, ids, *plan)
    copies[0].wait()
    fill_pairs(sizes.rows, held, lambda rows, values: plan.put_edges(edges, [row + 1 for row in rows], values))
    plan.fill_beyond(edges, sizes.edge_size)
    copies[1].wait()

    def store(scenario, row, first, count, values, is_last):
        store_sums(sums, sizes, scenario, row, first, count, values)

    plan.own_terms(functools.partial(load_sums, sums, sizes), store, edges, True, plan.edge_first(), sizes.edge_strips)
    copies[2].wait()
    copies[3].wait()
    fill_pairs(2 * H, rows_held, functools.partial(plan.put_rows, weights))
    sets = strip_sets(sizes.strips)

    def done(scenario, row):
        pltpu.make_async_copy(sums.at[scenario, row], sums_out.at[scenario, row], sems.at[4]).start()

    for index, (first, count) in enumerate(sets):
        plan.outside_terms(sums, weights, False, first, count, done if index == len(sets) - 1 else None)
    pltpu.make_async_copy(sums, sums_out, sems.at[4]).wait()


def last_kernel(sizes, scale, before, after, sums_in, average_out, totals_out, release, inflow, price, ids, plan, edges, sums, held, average, sems):
    copies = [
        pltpu.make_async_copy(before, held.at[pl.ds(0, H)], sems.at[0]),
        pltpu.make_async_copy(after, held.at[pl.ds(H, H)], sems.at[1]),
        pltpu.make_async_copy(sums_in, sums, sems.at[2]),
    ]
    for copy in copies:
        copy.start()
    plan = Plan(sizes, release, inflow, price, ids, *plan)
    copies[0].wait()
    copies[1].wait()

    fill_pairs(2 * H, held, functools.partial(plan.put_edges, edges))
    copies[2].wait()
    for first, count in strip_sets(sizes.edge_strips):
        plan.outside_terms(sums, edges, True, plan.edge_first() + first, count)

    def finish(row, total):
        for strip in range(sizes.strips):
            levels = slice(strip * SUB, strip * SUB + SUB)
            averages = []
            for plane in range(sizes.planes):
                logs = None
                for scenario in range(0, sizes.scenarios, 2):
                    product = sums[scenario, row, plane, levels, :]
                    if scenario + 1 < sizes.scenarios:
                        product = product * sums[scenario + 1, row, plane, levels, :]
                    log = jnp.log(product)
                    logs = log if logs is None else logs + log
                averages.append(logs * scale)
                total = total + averages[-1]
            for block, values in enumerate(transpose(averages)):
                average[row, levels, block * LANES : block * LANES + LANES] = values
        pltpu.make_async_copy(average.at[row], average_out.at[row], sems.at[3]).start()
        return total

    total = lax.fori_loop(0, sizes.rows, finish, jnp.zeros((SUB, LANES), jnp.float32))
    total = jnp.sum(total, axis=0, keepdims=True)
    totals_out[...] = jnp.broadcast_to(total[None], totals_out.shape)
    pltpu.make_async_copy(average, average_out, sems.at[3]).wait()


def mean_kernel(sizes, cells, totals, average, out, held, sems):
    chunks = min(4, sizes.rows)
    step = sizes.rows // chunks
    copies = [
        pltpu.make_async_copy(average.at[pl.ds(i * step, step)], held.at[pl.ds(i * step, step)], sems.at[i]) for i in range(chunks)
    ]
    back = [
        pltpu.make_async_copy(held.at[pl.ds(i * step, step)], out.at[pl.ds(i * step, step)], sems.at[chunks + i]) for i in range(chunks)
    ]
    for copy in copies:
        copy.start()
    total = jnp.sum(totals[...], axis=0)
    mean = jnp.sum(total, axis=1, keepdims=True) * (1.0 / cells)
    mean = jnp.broadcast_to(mean, (sizes.depth, sizes.width))
    for i in range(chunks):
        copies[i].wait()
        for row in range(i * step, i * step + step):
            held[row] = held[row] - mean
        back[i].start()
    for copy in back:
        copy.wait()


def call(kernel, sizes, arrays, outs, in_hbm, out_hbm, scalars, scratch):
    smem, vmem, hbm = (pl.BlockSpec(memory_space=space) for space in (pltpu.SMEM, pltpu.VMEM, pl.ANY))
    release, inflow, price, ids = scalars
    count, listed = sizes.scenarios, sizes.listed
    plan = [
        pltpu.SMEM((2 * (H + 2),), jnp.int32),
        pltpu.SMEM((listed,), jnp.int32),
        pltpu.SMEM((count * listed, 3), jnp.int32),
        pltpu.VMEM((listed * sizes.planes * SUB, LANES), jnp.float32),
        pltpu.VMEM((listed * sizes.depth, LANES), jnp.float32),
        pltpu.VMEM((listed * sizes.rows, LANES), jnp.float32),
        pltpu.VMEM((2 * LANES, len(turns(sizes)) * LANES), jnp.bfloat16),
    ]

    def body(*refs):
        ins, refs = refs[: len(arrays)], refs[len(arrays) :]
        scalar_refs, refs = refs[: 3 + count], refs[3 + count :]
        out_refs, refs = refs[: len(outs)], refs[len(outs) :]
        kernel(*ins, *out_refs, *scalar_refs[:3], scalar_refs[3:], refs[: len(plan)], *refs[len(plan) :])

    return pl.pallas_call(
        body,
        out_shape=outs,
        in_specs=[hbm if is_hbm else vmem for is_hbm in in_hbm] + [smem] * (3 + count),
        out_specs=[hbm if is_hbm else vmem for is_hbm in out_hbm],
        scratch_shapes=plan + scratch,
        compiler_params=pltpu.CompilerParams(vmem_limit_bytes=48 * 2**20),
    )(*arrays, release, inflow, price, *ids)


def from_above(cells, axis, hops=1):
    count = lax.axis_size(axis)
    return lax.ppermute(cells, axis, [(i + hops, i) for i in range(count - hops)])


def from_below(cells, axis, hops=1):
    count = lax.axis_size(axis)
    return lax.ppermute(cells, axis, [(i, i + hops) for i in range(count - hops)])


def beyond_levels(own):
    depth = own.shape[2]
    scen_count, scen = lax.axis_size("scen"), lax.axis_index("scen")
    low, high = [], []
    for hop in range(-(-LOW // depth), 0, -1):
        low.append(from_below(own, "scen", hop) if hop < scen_count else jnp.zeros_like(own))
    for hop in range(1, -(-HIGH // depth) + 1):
        high.append(from_above(own, "scen", hop) if hop < scen_count else jnp.zeros_like(own))
    low = jnp.concatenate(low, axis=2)[:, :, -LOW:]
    high = jnp.concatenate(high, axis=2)[:, :, :HIGH]
    for hop in range(1, -(-HIGH // depth)):
        fill = high[:, :, hop * depth - 1 : hop * depth]
        keep = lax.broadcasted_iota(jnp.int32, high.shape, 2) < hop * depth
        high = jnp.where(jnp.logical_or(scen + hop != scen_count - 1, keep), high, fill)
    return jnp.concatenate([low, high], axis=2)


def on_device(value_next, scenario_ids, inflow_table, release_shifts, price):
    rows, depth, width = value_next.shape
    grid_count, scen_count = lax.axis_size("grid"), lax.axis_size("scen")
    scen = lax.axis_index("scen")
    scenarios = scenario_ids.shape[0] * scen_count
    sizes = Sizes(rows, depth, width, scenarios, release_shifts.shape[0], grid_count, scen_count)

    ids = [scenario_ids]
    for hop in range(1, scen_count):
        ids.append(lax.ppermute(scenario_ids, "scen", [(i, (i + hop) % scen_count) for i in range(scen_count)]))
    ids = [each[i : i + 1] for each in ids for i in range(scenario_ids.shape[0])]

    own = pl.pallas_call(
        functools.partial(planes_kernel, sizes),
        out_shape=jax.ShapeDtypeStruct((rows, sizes.planes, depth, LANES), jnp.float32),
        in_specs=[pl.BlockSpec(memory_space=pltpu.VMEM)],
        out_specs=pl.BlockSpec(memory_space=pltpu.VMEM),
    )(value_next)
    own, ids = lax.optimization_barrier((own, ids))
    scalars = (release_shifts.T, inflow_table.T, price, ids)
    if sizes.pair:
        sent = jnp.where(scen == 0, own[:, :, depth - HIGH :], own[:, :, :HIGH])
        beyond = lax.ppermute(sent, "scen", [(0, 1), (1, 0)])
    else:
        beyond = beyond_levels(own)
    before = from_below(own[rows - H :], "grid")
    after = from_above(own[:H], "grid")

    shape = (scenarios, rows, sizes.planes, depth, LANES)
    sums_shape = jax.ShapeDtypeStruct(shape, jnp.float32)
    sums_held = pltpu.VMEM(shape, jnp.float32)
    inside, outside = rows + 2, 2 * H
    (sums,) = call(
        functools.partial(own_kernel, sizes), sizes, (own,), [sums_shape], [True], [True], scalars,
        [
            pltpu.VMEM((inside * sizes.row_size, LANES), jnp.float32), sums_held, pltpu.VMEM(own.shape, jnp.float32),
            pltpu.SemaphoreType.DMA((2,)),
        ],
    )
    beyond, sums = lax.optimization_barrier((beyond, sums))
    corner_before = from_below(beyond[rows - H :], "grid")
    corner_after = from_above(beyond[:H], "grid")
    (sums,) = call(
        functools.partial(edge_kernel, sizes), sizes, (beyond, before, after, sums), [sums_shape], [True] * 4, [True], scalars,
        [
            pltpu.VMEM((outside * sizes.row_size, LANES), jnp.float32), pltpu.VMEM((inside * sizes.edge_size, LANES), jnp.float32),
            sums_held, pltpu.VMEM(beyond.shape, jnp.float32), pltpu.VMEM((2 * H, *own.shape[1:]), jnp.float32),
            pltpu.SemaphoreType.DMA((5,)),
        ],
    )
    scale = -softness / scenarios
    devices = grid_count * scen_count
    average, totals = call(
        functools.partial(last_kernel, sizes, scale), sizes, (corner_before, corner_after, sums),
        [jax.ShapeDtypeStruct(value_next.shape, jnp.float32), jax.ShapeDtypeStruct((devices, 1, LANES), jnp.float32)],
        [True] * 3, [True, False], scalars,
        [
            pltpu.VMEM((outside * sizes.edge_size, LANES), jnp.float32), sums_held, pltpu.VMEM((2 * H, *beyond.shape[1:]), jnp.float32), pltpu.VMEM(value_next.shape, jnp.float32),
            pltpu.SemaphoreType.DMA((4,)),
        ],
    )
    totals = lax.all_to_all(totals, ("scen", "grid"), 0, 0, tiled=True)
    cells = rows * grid_count * depth * scen_count * width
    return pl.pallas_call(
        functools.partial(mean_kernel, sizes, cells),
        out_shape=jax.ShapeDtypeStruct(value_next.shape, jnp.float32),
        in_specs=[pl.BlockSpec(memory_space=pltpu.VMEM), pl.BlockSpec(memory_space=pl.ANY)],
        out_specs=pl.BlockSpec(memory_space=pl.ANY),
        scratch_shapes=[pltpu.VMEM(value_next.shape, jnp.float32), pltpu.SemaphoreType.DMA((8,))],
    )(totals, average)


def solution(mesh):
    placed = (P("grid", "scen", None), P("scen"), P(), P(), P())
    return jax.shard_map(
        on_device, mesh=mesh, in_specs=placed, out_specs=P("grid", "scen", None), check_vma=False
    )
```

time: 691 us -> 93.2 us (0.13)
  local copies, waits for them, and re-layouts: 181 us -> 1.88 us
  other arithmetic: 176 us -> 1.86 us
  waiting for transfers between devices: 158 us -> 0.9 us
  loops' own time: 112 us -> 0 us
  Pallas kernels: 0 us -> 60.6 us
  blocking collectives: 39.5 us -> 15 us
  between operations: 16.7 us -> 0.83 us
  starting transfers between devices: 4.37 us -> 11.8 us
    add x32 -> x0, other arithmetic: 141 us -> none  [the longest x16 139 us: add_release(): return running + jnp.exp(-(landed - benefit[None]) / softness)]
    another operation x1 -> x0, loops' own time: 112 us -> none  [on_device(): running = lax.fori_loop(0, RELEASES, add_release, start_sums)]
    while x16 -> x0, local copies, waits for them, and re-layouts: 98.2 us -> none  [one_scenario(): lax.dynamic_slice(extended, (first_index, third_index, second_index), (ro...]
    reduce_scatter x1 -> x0, waiting for transfers between devices: 94.9 us -> none  [on_device(): lax.psum_scatter(partial_total, 'scen', scatter_dimension=1, tiled=True)]
    all_gather x1 -> x0, waiting for transfers between devices: 61.1 us -> none  [on_device(): spread = lax.all_gather(value_next, 'scen', axis=1, tiled=True)]
    pallas_call x0 -> x5, Pallas kernels: none -> 60.6 us  [the longest x3 50.6 us: call(): pl.pallas_call(body, out_shape=outs, in_specs=[hbm if is_hbm else vmem fo...]
    psum x1 -> x0, blocking collectives: 39.5 us -> none  [on_device(): level_sum = lax.psum(jnp.sum(average), ('scen', 'grid'))]
    slice x53 -> x2, local copies, waits for them, and re-layouts: 37 us -> 0.29 us  [the longest x1 0.2 us: on_device(): after = from_above(own[:H], 'grid')]
  transfers between devices with their start and end apart: 4 -> 6, of which waited for: 3 -> 1; matrix products, arithmetic and copies ran while one was open for 0% -> 0% of each run, Pallas kernels for 0% -> 48%
where the time goes in v3:
time: 93.2 us; the launch traced here: 92.9 us
  Pallas kernels  60.6 us (65%)
  blocking collectives  15 us (16%)
  starting transfers between devices  11.8 us (13%)
  local copies, waits for them, and re-layouts  1.88 us (2%)
  other arithmetic  1.86 us (2%)
    pallas_call x3, Pallas kernels, call(): pl.pallas_call(body, out_shape=outs, in_specs=[hbm if is_hbm else vmem fo...  50.6 us
    all_to_all x1, blocking collectives, on_device(): totals = lax.all_to_all(totals, ('scen', 'grid'), 0, 0, tiled=True)  15 us
    pallas_call x1, Pallas kernels, on_device(): pl.pallas_call(functools.partial(planes_kernel, sizes), out_shape=jax.Sha...  6.93 us
    ppermute x2, starting transfers between devices, from_below(): lax.ppermute(cells, axis, [(i, i + hops) for i in range(count - hops)])  6.16 us
    pallas_call x1, Pallas kernels, on_device(): pl.pallas_call(functools.partial(mean_kernel, sizes, cells), out_shape=ja...  3.17 us
    ppermute x1, starting transfers between devices, on_device(): lax.ppermute(scenario_ids, 'scen', [(i, (i + hop) % scen_count) for i in...  2.94 us
    ppermute x2, starting transfers between devices, from_above(): lax.ppermute(cells, axis, [(i + hops, i) for i in range(count - hops)])  2.58 us
  transfers between devices with their start and end apart: 6, of which 1 were waited for; matrix products, arithmetic and copies ran while one was open for 0% of the time, Pallas kernels for 48%

profile of v3, /device:TPU:0, one launch (start us, length us, event | category | flops | bytes accessed | tf_op | source)
XLA Modules:
  0.0 92.9 jit_solution(3964238891812670031)
XLA Ops:
  0.0 2.9 %collective-permute-start = (s32[1]{0:T(128)}, s32[1]{0:T(128)}, u32[]{:S(2)}, u32[]{:S(2)}) collective-permute-start(s32[1]{0:T(128)} %param.6), channel_id=1, source_target_pairs={{0,16},{16,0},{1,17},{17,1},{2,18},{18,2},{3,19},{19,3},{4,20},{20... | collective-permute-start | bytes 20 | tf_op jit(solution)/shard_map/ppermute | solution.py:547
  2.9 6.9 %shard_map.55.refs_0_ = f32[16,8,32,128]{3,2,1,0:T(8,128)} custom-call(f32[16,32,1024]{2,1,0:T(8,128)} %values.1), custom_call_target="tpu_custom_call" | custom-call | tf_op jit(solution)/shard_map/pallas_call | solution.py:550
  9.9 0.0 copy-start
  9.9 0.0 collective-permute-done.refs_5_.refs_8_.refs_7_
  9.9 1.9 %slice_select_fusion = f32[16,8,16,128]{3,2,1,0:T(8,128)S(1)} fusion(f32[16,8,32,128]{3,2,1,0:T(8,128)} %shard_map.55.refs_0_, pred[]{:T(512)S(6)} %eq.3), kind=kLoop, calls=%fused_computation | loop fusion | flops 262144 | bytes 3145729 | tf_op jit(solution)/shard_map/jit(_where)/select_n | solution.py:559
  11.7 0.0 copy-start.2
  11.8 0.0 copy-start.3
  11.8 0.0 copy-start.4
  11.8 0.1 collective-permute-start.1
  11.9 0.2 copy-done
  12.1 0.2 fusion
  12.3 1.3 %collective-permute-start.5 = (f32[8,8,32,128]{3,2,1,0:T(8,128)S(1)}, f32[8,8,32,128]{3,2,1,0:T(8,128)S(1)}, u32[]{:S(2)}, u32[]{:S(2)}) collective-permute-start(f32[8,8,32,128]{3,2,1,0:T(8,128)S(1)} %get-tuple-element.19), channel_id=1, source_target_pairs={{1,0},{2,1},{3,2},{4,3},{5,4},{6,5},{7,6},{8,7},{9,8},{10,9},{11,1... | collective-permute-start | bytes 3145736 | tf_op jit(solution)/shard_map/ppermute | solution.py:513
  13.6 3.1 %collective-permute-start.4 = (f32[8,8,32,128]{3,2,1,0:T(8,128)S(1)}, f32[8,8,32,128]{3,2,1,0:T(8,128)S(1)}, u32[]{:S(2)}, u32[]{:S(2)}) collective-permute-start(f32[8,8,32,128]{3,2,1,0:T(8,128)S(1)} %get-tuple-element.20), channel_id=1, source_target_pairs={{0,1},{1,2},{2,3},{3,4},{4,5},{5,6},{6,7},{7,8},{8,9},{9,10},{10,1... | collective-permute-start | bytes 3145736 | tf_op jit(solution)/shard_map/ppermute | solution.py:518
  17.4 0.0 copy-done.2
  17.4 0.0 copy-done.3
  17.4 0.0 copy-done.4
  17.4 18.2 %shard_map.56.refs_3_ = f32[2,16,8,32,128]{4,3,2,1,0:T(8,128)} custom-call(f32[16,8,32,128]{3,2,1,0:T(8,128)S(1)} %copy-done, s32[3,16]{1,0:T(4,128)S(1)} %bitcast.2, s32[3,12]{1,0:T(4,128)S(1)} %bitcast.5, f32[3]{0:T(128)S(1)} %copy-done.4, s32[1]{0:T(128)S(6)} %copy.6.refs_4_.refs_7_.refs_6_, s32[1]{0:T(128)} %collective-permute-done.refs_5_.refs_8_.refs_7_), custom_call_target="tpu_custom_call" | custom-call | tf_op jit(solution)/shard_map/pallas_call | solution.py:501
  35.6 0.9 collective-permute-done.1.refs_0_
  36.5 0.1 fusion.1
  36.6 1.3 %collective-permute-start.3 = (f32[8,8,16,128]{3,2,1,0:T(8,128)S(1)}, f32[8,8,16,128]{3,2,1,0:T(8,128)S(1)}, u32[]{:S(2)}, u32[]{:S(2)}) collective-permute-start(f32[8,8,16,128]{3,2,1,0:T(8,128)S(1)} %get-tuple-element.21), channel_id=1, source_target_pairs={{1,0},{2,1},{3,2},{4,3},{5,4},{6,5},{7,6},{8,7},{9,8},{10,9},{11,1... | collective-permute-start | bytes 1572872 | tf_op jit(solution)/shard_map/ppermute | solution.py:513
  37.9 3.1 %collective-permute-start.2 = (f32[8,8,16,128]{3,2,1,0:T(8,128)S(1)}, f32[8,8,16,128]{3,2,1,0:T(8,128)S(1)}, u32[]{:S(2)}, u32[]{:S(2)}) collective-permute-start(f32[8,8,16,128]{3,2,1,0:T(8,128)S(1)} %get-tuple-element.22), channel_id=1, source_target_pairs={{0,1},{1,2},{2,3},{3,4},{4,5},{5,6},{6,7},{7,8},{8,9},{9,10},{10,1... | collective-permute-start | bytes 1572872 | tf_op jit(solution)/shard_map/ppermute | solution.py:518
  40.9 0.0 collective-permute-done.5.refs_2_
  40.9 0.0 collective-permute-done.4.refs_1_
  41.0 19.2 %shard_map.57.refs_2_ = f32[2,16,8,32,128]{4,3,2,1,0:T(8,128)} custom-call(f32[16,8,16,128]{3,2,1,0:T(8,128)S(1)} %collective-permute-done.1.refs_0_, f32[8,8,32,128]{3,2,1,0:T(8,128)S(1)} %collective-permute-done.4.refs_1_, f32[8,8,32,128]{3,2,1,0:T(8,128)S(1)} %collective-permute-done.5.refs_2_, f32[2,16,8,32,128]{4,3,2,1,0:T(8,128)} %shard_map.56.refs_3_, ...), custom_call_target="tpu_custom_call" | custom-call | tf_op jit(solution)/shard_map/pallas_call | solution.py:501
  60.1 0.0 collective-permute-done.3.refs_1_
  60.1 0.0 collective-permute-done.2.refs_0_
  60.2 13.2 %shard_map.58 = (f32[16,32,1024]{2,1,0:T(8,128)S(1)}, f32[32,1,128]{2,1,0:T(1,128)S(1)}) custom-call(f32[8,8,16,128]{3,2,1,0:T(8,128)S(1)} %collective-permute-done.2.refs_0_, f32[8,8,16,128]{3,2,1,0:T(8,128)S(1)} %collective-permute-done.3.refs_1_, f32[2,16,8,32,128]{4,3,2,1,0:T(8,128)} %shard_map.57.refs_2_, s32[3,16]{1,0:T(4,128)S(1)} %bitcast.4, ...), custom_call_target="tpu_custom_call" | custom-call | tf_op jit(solution)/shard_map/pallas_call | solution.py:501
  73.4 0.0 copy-start.1
  73.4 1.3 %copy-done.1 = f32[16,32,1024]{2,1,0:T(8,128)} copy-done((f32[16,32,1024]{2,1,0:T(8,128)}, f32[16,32,1024]{2,1,0:T(8,128)S(1)}, u32[]{:S(2)}) %copy-start.1) | copy-done | bytes 2097176
  74.7 15.0 %all_to_all.5.totals = f32[32,1,128]{2,1,0:T(1,128)} all-to-all(f32[32,1,128]{2,1,0:T(1,128)S(1)} %get-tuple-element.17), channel_id=1, replica_groups=mesh['scen'=2,'grid'=16] {'scen','grid'}, dimensions={0} | all-to-all | bytes 32768 | tf_op jit(solution)/shard_map/all_to_all | solution.py:599
  89.7 3.2 %shard_map.59 = f32[16,32,1024]{2,1,0:T(8,128)} custom-call(f32[32,1,128]{2,1,0:T(1,128)} %all_to_all.5.totals, f32[16,32,1024]{2,1,0:T(8,128)} %copy-done.1), custom_call_target="tpu_custom_call" | custom-call | tf_op jit(solution)/shard_map/pallas_call | solution.py:601
Async XLA Ops:
  0.0 9.9 %collective-permute-start = (s32[1]{0:T(128)}, s32[1]{0:T(128)}, u32[]{:S(2)}, u32[]{:S(2)}) collective-permute-start(s32[1]{0:T(128)} %param.6), channel_id=1, source_target_pairs={{0,16},{16,0},{1,17},{17,1},{2,18},{18,2},{3,19},{19,3},{4,20},{20... | collective-permute-start | bytes 20 | tf_op jit(solution)/shard_map/ppermute | solution.py:547
  9.9 2.2 %copy-start = (f32[16,8,32,128]{3,2,1,0:T(8,128)S(1)}, f32[16,8,32,128]{3,2,1,0:T(8,128)}, u32[]{:S(2)}) copy-start(f32[16,8,32,128]{3,2,1,0:T(8,128)} %shard_map.55.refs_0_) | copy-start | bytes 6291460
  11.7 5.6 %copy-start.2 = (s32[16,3]{0,1:T(4,128)S(1)}, s32[16,3]{0,1:T(4,128)}, u32[]{:S(2)}) copy-start(s32[16,3]{0,1:T(4,128)} %param.8) | copy-start | bytes 580
  11.8 5.6 %copy-start.3 = (s32[12,3]{0,1:T(4,128)S(1)}, s32[12,3]{0,1:T(4,128)}, u32[]{:S(2)}) copy-start(s32[12,3]{0,1:T(4,128)} %param.7) | copy-start | bytes 436
  11.8 5.6 %copy-start.4 = (f32[3]{0:T(128)S(1)}, f32[3]{0:T(128)}, u32[]{:S(2)}) copy-start(f32[3]{0:T(128)} %refs_5_.1) | copy-start | bytes 40
  11.8 24.7 %collective-permute-start.1 = (f32[16,8,16,128]{3,2,1,0:T(8,128)S(1)}, f32[16,8,16,128]{3,2,1,0:T(8,128)S(1)}, u32[]{:S(2)}, u32[]{:S(2)}) collective-permute-start(f32[16,8,16,128]{3,2,1,0:T(8,128)S(1)} %slice_select_fusion), channel_id=1, source_target_pairs={{0,16},{16,0},{1,17},{17,1},{2,18},{18,2},{3,19},{19,3},{4,20},{20... | collective-permute-start | bytes 3145736 | tf_op jit(solution)/shard_map/ppermute | solution.py:560
  12.3 28.6 %collective-permute-start.5 = (f32[8,8,32,128]{3,2,1,0:T(8,128)S(1)}, f32[8,8,32,128]{3,2,1,0:T(8,128)S(1)}, u32[]{:S(2)}, u32[]{:S(2)}) collective-permute-start(f32[8,8,32,128]{3,2,1,0:T(8,128)S(1)} %get-tuple-element.19), channel_id=1, source_target_pairs={{1,0},{2,1},{3,2},{4,3},{5,4},{6,5},{7,6},{8,7},{9,8},{10,9},{11,1... | collective-permute-start | bytes 3145736 | tf_op jit(solution)/shard_map/ppermute | solution.py:513
  13.6 27.3 %collective-permute-start.4 = (f32[8,8,32,128]{3,2,1,0:T(8,128)S(1)}, f32[8,8,32,128]{3,2,1,0:T(8,128)S(1)}, u32[]{:S(2)}, u32[]{:S(2)}) collective-permute-start(f32[8,8,32,128]{3,2,1,0:T(8,128)S(1)} %get-tuple-element.20), channel_id=1, source_target_pairs={{0,1},{1,2},{2,3},{3,4},{4,5},{5,6},{6,7},{7,8},{8,9},{9,10},{10,1... | collective-permute-start | bytes 3145736 | tf_op jit(solution)/shard_map/ppermute | solution.py:518
  36.6 23.6 %collective-permute-start.3 = (f32[8,8,16,128]{3,2,1,0:T(8,128)S(1)}, f32[8,8,16,128]{3,2,1,0:T(8,128)S(1)}, u32[]{:S(2)}, u32[]{:S(2)}) collective-permute-start(f32[8,8,16,128]{3,2,1,0:T(8,128)S(1)} %get-tuple-element.21), channel_id=1, source_target_pairs={{1,0},{2,1},{3,2},{4,3},{5,4},{6,5},{7,6},{8,7},{9,8},{10,9},{11,1... | collective-permute-start | bytes 1572872 | tf_op jit(solution)/shard_map/ppermute | solution.py:513
  37.9 22.3 %collective-permute-start.2 = (f32[8,8,16,128]{3,2,1,0:T(8,128)S(1)}, f32[8,8,16,128]{3,2,1,0:T(8,128)S(1)}, u32[]{:S(2)}, u32[]{:S(2)}) collective-permute-start(f32[8,8,16,128]{3,2,1,0:T(8,128)S(1)} %get-tuple-element.22), channel_id=1, source_target_pairs={{0,1},{1,2},{2,3},{3,4},{4,5},{5,6},{6,7},{7,8},{8,9},{9,10},{10,1... | collective-permute-start | bytes 1572872 | tf_op jit(solution)/shard_map/ppermute | solution.py:518
  73.4 1.3 %copy-start.1 = (f32[16,32,1024]{2,1,0:T(8,128)}, f32[16,32,1024]{2,1,0:T(8,128)S(1)}, u32[]{:S(2)}) copy-start(f32[16,32,1024]{2,1,0:T(8,128)S(1)} %get-tuple-element.18.average) | copy-start | bytes 6291460

commit v4 on v3

v4 whole, which is shorter than its diff:
```python
import functools

import jax
import jax.numpy as jnp
from jax import lax
from jax.experimental import pallas as pl
from jax.experimental.pallas import tpu as pltpu
from jax.sharding import PartitionSpec as P

H = 8
LOW, HIGH = H, 2 * H
SUB, LANES = 8, 128
TILE = 2
CHUNK = 4
UNROLL = 2
softness = 0.5

ORDER = 0
SHIFT_A, OFFSET, EDGE_OFFSET = range(3)


class Sizes:
    def __init__(self, rows, depth, width, scenarios, releases, grid_count, scen_count):
        self.rows, self.depth, self.width = rows, depth, width
        self.grid_count, self.scen_count = grid_count, scen_count
        self.scenarios, self.releases = scenarios, releases
        self.listed = releases + UNROLL - 1
        self.columns = 1 + 3 * scenarios
        self.far_size = releases + 1 + UNROLL
        self.pieces = [(0, H), (H, rows - 2 * H), (rows - H, H)] if rows > 2 * H else [(0, H), (H, H)] if rows == 2 * H else [(0, rows)]
        self.planes = width // LANES
        self.group = LANES // self.planes
        self.strips = depth // SUB
        self.planes_ext = LOW + self.planes + HIGH
        self.depth_ext = LOW + depth + HIGH
        self.row_size = self.planes_ext * self.depth_ext
        self.pair = scen_count == 2 and depth >= HIGH
        self.edge_strips = HIGH // SUB if self.pair else self.strips
        self.edge_ext = 2 * HIGH if self.pair else self.depth_ext
        self.edge_size = self.planes_ext * self.edge_ext

    def place(self, lane):
        return lane % self.planes * self.group + lane // self.planes

    def lane(self, place):
        return place % self.group * self.planes + place // self.group


def transpose(blocks):
    lane = lax.broadcasted_iota(jnp.int32, (SUB, LANES), 1)
    blocks = [pltpu.roll(block, k, 1) if k else block for k, block in enumerate(blocks)]
    count = len(blocks)
    step = 1
    while step < count:
        odd = (lane // step) % 2 == 1
        blocks = [jnp.where(odd, blocks[(i + step) % count], blocks[i]) for i in range(count)]
        step *= 2
    return [pltpu.roll(blocks[-j % count], LANES - j, 1) if j else blocks[0] for j in range(count)]


def turns(sizes):
    return [*range(-(-(-LOW // sizes.planes)), 0), *range(1, -(-HIGH // sizes.planes) + 1)]


def fill_turns(matrix, sizes):
    shape = (2 * LANES, LANES)
    source = lax.broadcasted_iota(jnp.int32, shape, 0) % LANES
    place = sizes.place(lax.broadcasted_iota(jnp.int32, shape, 1))
    for i, turn in enumerate(turns(sizes)):
        there = jnp.clip(place + turn, 0, LANES - 1)
        matrix[:, i * LANES : i * LANES + LANES] = (sizes.lane(there) == source).astype(jnp.float32).astype(jnp.bfloat16)


def put(weights, sizes, matrix, row_bases, depth_ext, at, rows):
    place = sizes.place(lax.broadcasted_iota(jnp.int32, (SUB, LANES), 1))
    levels = rows[0].shape[1]
    both = jnp.concatenate([row.reshape(sizes.planes * levels, LANES) for row in rows], axis=0)
    upper = both.astype(jnp.bfloat16)
    lower = (both - upper.astype(jnp.float32)).astype(jnp.bfloat16)
    turned = jnp.dot(jnp.concatenate([upper, lower], axis=1), matrix[...], preferred_element_type=jnp.float32)
    for row, row_base in enumerate(row_bases):
        for strip in range(levels // SUB):
            base = row_base + at + strip * SUB

            def part(array, plane):
                first = (row * sizes.planes + plane) * levels + strip * SUB
                return array[first : first + SUB]

            for plane in range(sizes.planes):
                weights[pl.ds(base + (LOW + plane) * depth_ext, SUB), :] = part(both, plane)
            for i, turn in enumerate(turns(sizes)):
                moved = turned[:, i * LANES : i * LANES + LANES]
                end = part(moved, sizes.planes - 1 if turn > 0 else 0)
                past = place + turn > LANES - 1 if turn > 0 else place + turn < 0
                for plane in range(sizes.planes):
                    to = LOW + turn * sizes.planes + plane
                    if 0 <= to < sizes.planes_ext:
                        weights[pl.ds(base + to * depth_ext, SUB), :] = jnp.where(past, end, part(moved, plane))


def put_zeros(weights, sizes, row_base, depth_ext, at, count):
    zero = jnp.zeros((SUB, LANES), jnp.float32)
    for strip in range(count // SUB):
        for plane in range(sizes.planes_ext):
            weights[pl.ds(row_base + plane * depth_ext + at + strip * SUB, SUB), :] = zero


def repeat(weights, sizes, row_base, depth_ext, source, at, count):
    for plane in range(sizes.planes_ext):
        base = row_base + plane * depth_ext
        level = jnp.broadcast_to(weights[pl.ds(base + source, 1), :], (SUB, LANES))
        for strip in range(count // SUB):
            weights[pl.ds(base + at + strip * SUB, SUB), :] = level


def make_lists(sizes, release, inflow, ids, below, table, far):
    first_depth = lax.axis_index("scen") == 0
    inflow_a, inflow_b, inflow_c = ([inflow[i, ids[w][0]] for w in range(sizes.scenarios)] for i in range(3))
    for value in range(H + 2):
        count = jnp.int32(0)
        for r in range(sizes.releases):
            count = count + (release[0, r] < value).astype(jnp.int32)
        below[value] = count
        below[H + 2 + value] = count
    for w in range(sizes.scenarios):
        below[2 * (H + 2) + w] = inflow_a[w]
    for r in range(sizes.releases):
        value = release[0, r]
        to = below[H + 2 + value]
        below[H + 2 + value] = to + 1
        table[sizes.columns * to + ORDER] = r
    for extra in range(sizes.releases, sizes.listed):
        table[sizes.columns * extra + ORDER] = 0

    def step(listed, counts):
        r = table[sizes.columns * listed + ORDER]
        u1, u2, u3 = release[0, r], release[1, r], release[2, r]
        out = []
        for w in range(sizes.scenarios):
            at = sizes.columns * listed + 1 + 3 * w
            plane = LOW + inflow_b[w] + u1 - u2
            shift = inflow_c[w] + u2 - u3
            table[at + SHIFT_A] = inflow_a[w] - u1
            table[at + OFFSET] = plane * sizes.depth_ext + LOW + shift
            far[w * sizes.far_size + 1 + counts[w]] = listed
            reaches = jnp.logical_and(jnp.logical_and(first_depth, shift > SUB), listed < sizes.releases)
            out.append(counts[w] + reaches.astype(jnp.int32))
            if sizes.pair:
                shift = jnp.where(first_depth, jnp.maximum(shift, 0), HIGH + jnp.minimum(shift, 0))
                table[at + EDGE_OFFSET] = plane * sizes.edge_ext + shift
            else:
                table[at + EDGE_OFFSET] = plane * sizes.edge_ext + LOW + shift
        return tuple(out)

    counts = lax.fori_loop(0, sizes.listed, step, tuple(jnp.int32(0) for _ in range(sizes.scenarios)))
    for w in range(sizes.scenarios):
        far[w * sizes.far_size] = counts[w]
        far[w * sizes.far_size + 1 + counts[w]] = sizes.releases


def make_factors(sizes, release, price, table, gains, depths, heights):
    sublane = lax.broadcasted_iota(jnp.int32, (SUB, LANES), 0)
    place = sizes.place(lax.broadcasted_iota(jnp.int32, (SUB, LANES), 1))
    row0, depth0 = lax.axis_index("grid") * sizes.rows, lax.axis_index("scen") * sizes.depth
    spans = (sizes.rows * sizes.grid_count, sizes.width, sizes.depth * sizes.scen_count)
    prices = [price[i] * (1.0 / (spans[i] * H * softness)) for i in range(3)]

    def step(listed, _):
        r = table[sizes.columns * listed + ORDER]
        rate = [prices[i] * release[i, r].astype(jnp.float32) for i in range(3)]
        for plane in range(sizes.planes):
            level = (place * sizes.planes + (plane + 1)).astype(jnp.float32)
            gains[pl.ds(pl.multiple_of((listed * sizes.planes + plane) * SUB, SUB), SUB), :] = jnp.exp(level * rate[1])
        listens = jnp.where(listed < sizes.releases, 1.0, 0.0)
        for refs, start, count, which in ((heights, row0, sizes.rows, 0), (depths, depth0, sizes.depth, 2)):
            for strip in range(count // SUB):
                level = (sublane + (start + strip * SUB + 1)).astype(jnp.float32)
                refs[pl.ds(pl.multiple_of(listed * count + strip * SUB, SUB), SUB), :] = jnp.exp(level * rate[which]) * listens
        return 0

    lax.fori_loop(0, sizes.listed, step, 0)


class Plan:
    def __init__(self, sizes, below, table, far, factors, matrix):
        self.sizes, self.below, self.table, self.far, self.matrix = sizes, below, table, far, matrix
        self.gains, self.depths, self.heights = factors
        grid, scen = lax.axis_index("grid"), lax.axis_index("scen")
        self.first_row, self.last_row = grid == 0, grid == sizes.grid_count - 1
        self.first_depth, self.last_depth = scen == 0, scen == sizes.scen_count - 1
        fill_turns(matrix, sizes)

    def entry(self, scenario, listed, column):
        return self.table[self.sizes.columns * listed + 1 + 3 * scenario + column]

    def edge_first(self):
        if self.sizes.pair:
            return jnp.where(self.first_depth, self.sizes.strips - self.sizes.edge_strips, 0)
        return 0

    def put_rows(self, weights, rows, values):
        sizes = self.sizes
        ext = sizes.depth_ext
        bases = [row * sizes.row_size for row in rows]
        put(weights, sizes, self.matrix, bases, ext, LOW, values)
        for is_end, at, count, edge in (
            (self.first_depth, 0, LOW, LOW),
            (self.last_depth, LOW + sizes.depth, HIGH, LOW + sizes.depth - 1),
        ):

            @pl.when(is_end)
            def _():
                for base in bases:
                    repeat(weights, sizes, base, ext, edge, at, count)

            @pl.when(jnp.logical_not(is_end))
            def _():
                for base in bases:
                    put_zeros(weights, sizes, base, ext, at, count)

    def put_edges(self, weights, rows, beyond):
        sizes = self.sizes
        ext = sizes.edge_ext
        bases = [row * sizes.edge_size for row in rows]
        if sizes.pair:
            put(weights, sizes, self.matrix, bases, ext, jnp.where(self.first_depth, HIGH, 0), beyond)
            for base in bases:
                put_zeros(weights, sizes, base, ext, jnp.where(self.first_depth, 0, HIGH), HIGH)
            return
        for base in bases:
            put_zeros(weights, sizes, base, ext, 0, ext)

        @pl.when(jnp.logical_not(self.first_depth))
        def _():
            put(weights, sizes, self.matrix, bases, ext, 0, [row[:, :LOW] for row in beyond])

        @pl.when(jnp.logical_not(self.last_depth))
        def _():
            put(weights, sizes, self.matrix, bases, ext, LOW + sizes.depth, [row[:, LOW:] for row in beyond])

    def gain(self, listed, plane):
        return self.gains[pl.ds(pl.multiple_of((listed * self.sizes.planes + plane) * SUB, SUB), SUB), :]

    def factors(self, row, first, count, listed):
        height = self.heights[pl.ds(listed * self.sizes.rows + row, 1), :]
        return [
            self.depths[pl.ds(pl.multiple_of(listed * self.sizes.depth + (first + strip) * SUB, SUB), SUB), :] * height
            for strip in range(count)
        ]

    def base(self, edge, scenario, source, first, listed):
        if edge:
            return source * self.sizes.edge_size + self.entry(scenario, listed, EDGE_OFFSET), self.sizes.edge_ext
        return source * self.sizes.row_size + self.entry(scenario, listed, OFFSET) + first * SUB, self.sizes.depth_ext

    def fill_beyond(self, weights, row_size):
        rows = self.sizes.rows
        unroll = 4

        def fill(index, _):
            for k in range(unroll):
                at = pl.multiple_of((index * unroll + k) * SUB, SUB)
                for is_end, to, source in ((self.first_row, 0, 1), (self.last_row, rows + 1, rows)):
                    end = weights[pl.ds(source * row_size + at, SUB), :]
                    weights[pl.ds(to * row_size + at, SUB), :] = end * is_end.astype(jnp.float32)
            return 0

        lax.fori_loop(0, row_size // (SUB * unroll), fill, 0)

    def far_terms(self, sums_ref, edges):
        sizes = self.sizes
        strip = sizes.strips - 2
        together = 2 if sizes.rows % 2 == 0 else 1

        def scenario_terms(scenario, _):
            count = self.far[scenario * sizes.far_size]

            def work(index, _):
                rows = [index * together + i for i in range(together)]

                def step(index, sums):
                    sums = [list(each) for each in sums]
                    for k in range(UNROLL):
                        listed = self.far[scenario * sizes.far_size + 1 + index * UNROLL + k]
                        lands = self.entry(scenario, listed, SHIFT_A) + 1
                        for i, row in enumerate(rows):
                            source = jnp.clip(row + lands, 0, sizes.rows + 1)
                            sums[i] = self.add_release(sums[i], edges, True, scenario, row, strip, 1, listed, source)
                    return tuple(tuple(each) for each in sums)

                sums = tuple(tuple(load_sums(sums_ref, sizes, scenario, row, strip, 1)) for row in rows)
                sums = lax.fori_loop(0, (count + UNROLL - 1) // UNROLL, step, sums)
                for row, each in zip(rows, sums, strict=True):
                    store_sums(sums_ref, sizes, scenario, row, strip, 1, each)
                return 0

            @pl.when(count > 0)
            def _():
                lax.fori_loop(0, sizes.rows // together, work, 0)

            return 0

        lax.fori_loop(0, sizes.scenarios, scenario_terms, 0)

    def own_terms(self, load, store, weights, edge, first, strips, shift=0, chunk=None):
        sizes = self.sizes
        together = 2 if sizes.scenarios % 2 == 0 else 1

        def work(index, _):
            row = index % sizes.rows
            scenarios = [index // sizes.rows * together + i for i in range(together)]

            def find(listed):
                found = []
                for scenario in scenarios:
                    source = jnp.clip(row + 1 + self.entry(scenario, listed, SHIFT_A), 0, sizes.rows + 1)
                    base, ext = self.base(edge, scenario, source, first, listed)
                    found.append((base + shift, ext))
                return found

            def add(sums, from_strip, count, listed, bases):
                factors = self.factors(row, first + from_strip, count, listed)
                for plane in range(sizes.planes):
                    gain = self.gain(listed, plane)
                    for strip in range(count):
                        weight = gain * factors[strip]
                        at = plane * count + strip
                        for i, (base, ext) in enumerate(bases):
                            landed = weights[pl.ds(base + plane * ext + (from_strip + strip) * SUB, SUB), :]
                            sums[i][at] = sums[i][at] + landed * weight

            bases = None if chunk else [find(listed) for listed in range(sizes.releases)]
            for from_strip, count in strip_sets(strips, TILE):
                sums = [load(scenario, row, first + from_strip, count) for scenario in scenarios]
                if chunk:

                    def step(index, sums):
                        sums = [list(each) for each in sums]
                        for k in range(chunk):
                            add(sums, from_strip, count, index * chunk + k, find(index * chunk + k))
                        return tuple(tuple(each) for each in sums)

                    sums = lax.fori_loop(0, sizes.releases // chunk, step, tuple(tuple(each) for each in sums))
                else:
                    for listed in range(sizes.releases):
                        add(sums, from_strip, count, listed, bases[listed])
                for i, scenario in enumerate(scenarios):
                    store(scenario, row, first + from_strip, count, sums[i], from_strip + count == strips)
            return 0

        lax.fori_loop(0, sizes.scenarios // together * sizes.rows, work, 0)

    def add_release(self, sums, weights, edge, scenario, row, first, count, listed, source):
        sizes = self.sizes
        base, ext = self.base(edge, scenario, source, first, listed)
        factors = self.factors(row, first, count, listed)
        out = []
        for plane in range(sizes.planes):
            gain = self.gain(listed, plane)
            for strip in range(count):
                landed = weights[pl.ds(base + plane * ext + strip * SUB, SUB), :]
                out.append(sums[plane * count + strip] + landed * (gain * factors[strip]))
        return out

    def outside_terms(self, sums_ref, weights, edge, first, count, done=None):
        sizes = self.sizes

        def work(index, _):
            scenario, row = index // sizes.rows, index % sizes.rows
            top = row + self.below[2 * (H + 2) + scenario]
            start = jnp.where(self.last_row, 0, self.below[jnp.clip(top - sizes.rows + 1, 0, H + 1)])
            stop = jnp.where(self.first_row, sizes.releases, self.below[jnp.clip(top + 1, 0, H + 1)])

            def some(lo, hi, shift):
                @pl.when(lo < hi)
                def _():
                    def step(index, sums):
                        for k in range(UNROLL):
                            listed = lo + index * UNROLL + k
                            listed = jnp.where(listed < hi, listed, sizes.releases)
                            source = row + self.entry(scenario, listed, SHIFT_A) + shift
                            source = jnp.clip(source, 0, 2 * H - 1)
                            sums = self.add_release(sums, weights, edge, scenario, row, first, count, listed, source)
                        return tuple(sums)

                    sums = tuple(load_sums(sums_ref, sizes, scenario, row, first, count))
                    sums = lax.fori_loop(0, (hi - lo + UNROLL - 1) // UNROLL, step, sums)
                    store_sums(sums_ref, sizes, scenario, row, first, count, sums)

            if sizes.rows >= 2 * H:
                low = row < H
                some(jnp.where(low, stop, 0), jnp.where(low, sizes.releases, start), jnp.where(low, H, H - sizes.rows))
            else:
                some(0, start, H - sizes.rows)
                some(stop, sizes.releases, H)
            if done is not None:
                done(scenario, row)
            return 0

        lax.fori_loop(0, sizes.scenarios * sizes.rows, work, 0)


def load_sums(ref, sizes, scenario, row, first, count):
    return [
        ref[scenario, row, plane, pl.ds(pl.multiple_of((first + strip) * SUB, SUB), SUB), :]
        for plane in range(sizes.planes)
        for strip in range(count)
    ]


def store_sums(ref, sizes, scenario, row, first, count, sums):
    for plane in range(sizes.planes):
        for strip in range(count):
            ref[scenario, row, plane, pl.ds(pl.multiple_of((first + strip) * SUB, SUB), SUB), :] = sums[plane * count + strip]


def strip_sets(strips, most=4):
    return [(first, min(most, strips - first)) for first in range(0, strips, most)]


def fill_pairs(count, held, fill):
    def step(index, _):
        rows = [2 * index, 2 * index + 1]
        fill(rows, [held[row] for row in rows])
        return 0

    lax.fori_loop(0, count // 2, step, 0)


def planes_kernel(sizes, values, *refs):
    outs, (held, planes_held, sems) = refs[:-3], refs[-3:]
    size = 4 if all(count % 4 == 0 for _, count in sizes.pieces) else 1
    copies = [
        pltpu.make_async_copy(values.at[pl.ds(row, size)], held.at[pl.ds(row, size)], sems.at[i])
        for i, row in enumerate(range(0, sizes.rows, size))
    ]
    for copy in copies:
        copy.start()
    start = pl.multiple_of(jnp.where(lax.axis_index("scen") == 0, sizes.depth - HIGH, 0), SUB) if sizes.pair else None
    sent_sem, first_sem = sems.at[len(copies)], len(copies) + 1

    def step(row, _):
        for strip in range(sizes.strips):
            levels = slice(strip * SUB, strip * SUB + SUB)
            blocks = (
                jnp.exp(held[row, levels, block * LANES : block * LANES + LANES] * (-1.0 / softness))
                for block in range(sizes.planes)
            )
            for plane, each in enumerate(transpose(blocks)):
                planes_held[row, plane, levels, :] = each
        if sizes.pair:
            pltpu.make_async_copy(planes_held.at[row, :, pl.ds(start, HIGH)], outs[-1].at[row], sent_sem).start()
        return 0

    pieces = []
    for i, (first, count) in enumerate(sizes.pieces):
        for row in range(first, first + count, size):
            copies[row // size].wait()
            lax.fori_loop(row, row + size, step, 0)
        pieces.append(pltpu.make_async_copy(planes_held.at[pl.ds(first, count)], outs[i], sems.at[first_sem + i]))
        pieces[-1].start()
    if sizes.pair:
        pltpu.make_async_copy(planes_held.at[:, :, pl.ds(start, HIGH)], outs[-1], sent_sem).wait()
    for piece in pieces:
        piece.wait()


def own_kernel(sizes, *refs):
    own, refs = refs[: len(sizes.pieces)], refs[len(sizes.pieces) :]
    release, inflow, price, ids, sums_out, gains_out, depths_out, heights_out, below, table, far, factors, matrix, *refs = refs
    weights, sums, held, sems = refs
    copies = [
        pltpu.make_async_copy(piece, held.at[pl.ds(first, count)], sems.at[5 + i])
        for i, (piece, (first, count)) in enumerate(zip(own, sizes.pieces, strict=True))
    ]
    for copy in copies:
        copy.start()
    make_lists(sizes, release, inflow, ids, below, table, far)
    make_factors(sizes, release, price, table, *factors)
    backs = [
        pltpu.make_async_copy(ref, out, sems.at[2 + i])
        for i, (ref, out) in enumerate(zip(factors, (gains_out, depths_out, heights_out), strict=True))
    ]
    for back in backs:
        back.start()
    plan = Plan(sizes, below, table, far, factors, matrix)
    for copy in copies:
        copy.wait()
    fill_pairs(sizes.rows, held, lambda rows, values: plan.put_rows(weights, [row + 1 for row in rows], values))
    plan.fill_beyond(weights, sizes.row_size)
    zero = jnp.zeros((SUB, LANES), jnp.float32)

    def store(scenario, row, first, count, values, is_last):
        store_sums(sums, sizes, scenario, row, first, count, values)
        if is_last:
            pltpu.make_async_copy(sums.at[scenario, row], sums_out.at[scenario, row], sems.at[1]).start()

    chunk = CHUNK if sizes.releases % CHUNK == 0 else None
    plan.own_terms(lambda scenario, row, first, count: [zero] * (sizes.planes * count), store, weights, False, 0, sizes.strips, 0, chunk)
    for back in backs:
        back.wait()
    pltpu.make_async_copy(sums, sums_out, sems.at[1]).wait()


def start_copies(refs, held, sems):
    copies = [pltpu.make_async_copy(ref, to, sems.at[i]) for i, (ref, to) in enumerate(zip(refs, held, strict=True))]
    for copy in copies:
        copy.start()
    return copies


def edge_kernel(
    sizes, beyond, before, after, sums_in, gains, depths, heights, below, table, far, sums_out, factors, matrix, weights, edges, sums, held,
    rows_held, sems,
):
    copies = [
        pltpu.make_async_copy(beyond, held, sems.at[0]),
        pltpu.make_async_copy(sums_in, sums, sems.at[1]),
        pltpu.make_async_copy(before, rows_held.at[pl.ds(0, H)], sems.at[2]),
        pltpu.make_async_copy(after, rows_held.at[pl.ds(H, H)], sems.at[3]),
    ]
    for copy in copies:
        copy.start()
    copies += start_copies((gains, depths, heights), factors, sems.at[pl.ds(5, 3)])
    plan = Plan(sizes, below, table, far, factors, matrix)
    copies[0].wait()
    fill_pairs(sizes.rows, held, lambda rows, values: plan.put_edges(edges, [row + 1 for row in rows], values))
    plan.fill_beyond(edges, sizes.edge_size)
    for copy in (copies[1], *copies[4:]):
        copy.wait()

    def store(scenario, row, first, count, values, is_last):
        store_sums(sums, sizes, scenario, row, first, count, values)

    load = functools.partial(load_sums, sums, sizes)
    if sizes.pair:
        near = jnp.where(plan.first_depth, sizes.strips - 1, 0)
        shift = jnp.where(plan.first_depth, HIGH - SUB, 0)
        plan.own_terms(load, store, edges, True, near, 1, shift, CHUNK if sizes.releases % CHUNK == 0 else None)
        plan.far_terms(sums, edges)
    else:
        plan.own_terms(load, store, edges, True, 0, sizes.edge_strips)
    copies[2].wait()
    copies[3].wait()
    fill_pairs(2 * H, rows_held, functools.partial(plan.put_rows, weights))
    sets = strip_sets(sizes.strips)

    def done(scenario, row):
        pltpu.make_async_copy(sums.at[scenario, row], sums_out.at[scenario, row], sems.at[4]).start()

    for index, (first, count) in enumerate(sets):
        plan.outside_terms(sums, weights, False, first, count, done if index == len(sets) - 1 else None)
    pltpu.make_async_copy(sums, sums_out, sems.at[4]).wait()


def last_kernel(
    sizes, scale, before, after, sums_in, gains, depths, heights, below, table, far, average_out, totals_out, factors, matrix, edges, sums,
    held, average, sems,
):
    copies = [
        pltpu.make_async_copy(before, held.at[pl.ds(0, H)], sems.at[0]),
        pltpu.make_async_copy(after, held.at[pl.ds(H, H)], sems.at[1]),
        pltpu.make_async_copy(sums_in, sums, sems.at[2]),
    ]
    for copy in copies:
        copy.start()
    copies += start_copies((gains, depths, heights), factors, sems.at[pl.ds(4, 3)])
    plan = Plan(sizes, below, table, far, factors, matrix)
    copies[0].wait()
    copies[1].wait()

    fill_pairs(2 * H, held, functools.partial(plan.put_edges, edges))
    for copy in copies[2:]:
        copy.wait()
    for first, count in strip_sets(sizes.edge_strips):
        plan.outside_terms(sums, edges, True, plan.edge_first() + first, count)

    def finish(index, total):
        for row in (2 * index, 2 * index + 1):
            for strip in range(sizes.strips):
                levels = slice(strip * SUB, strip * SUB + SUB)
                averages = []
                for plane in range(sizes.planes):
                    logs = None
                    for scenario in range(0, sizes.scenarios, 2):
                        product = sums[scenario, row, plane, levels, :]
                        if scenario + 1 < sizes.scenarios:
                            product = product * sums[scenario + 1, row, plane, levels, :]
                        log = jnp.log(product)
                        logs = log if logs is None else logs + log
                    averages.append(logs * scale)
                    total = total + averages[-1]
                for block, values in enumerate(transpose(averages)):
                    average[row, levels, block * LANES : block * LANES + LANES] = values
            pltpu.make_async_copy(average.at[row], average_out.at[row], sems.at[3]).start()
        return total

    total = lax.fori_loop(0, sizes.rows // 2, finish, jnp.zeros((SUB, LANES), jnp.float32))
    total = jnp.sum(total, axis=0, keepdims=True)
    totals_out[...] = jnp.broadcast_to(total[None], totals_out.shape)
    pltpu.make_async_copy(average, average_out, sems.at[3]).wait()


def mean_kernel(sizes, cells, totals, average, out, held, sems):
    chunks = min(8, sizes.rows)
    step = sizes.rows // chunks
    copies = [
        pltpu.make_async_copy(average.at[pl.ds(i * step, step)], held.at[pl.ds(i * step, step)], sems.at[i]) for i in range(chunks)
    ]
    back = [
        pltpu.make_async_copy(held.at[pl.ds(i * step, step)], out.at[pl.ds(i * step, step)], sems.at[chunks + i]) for i in range(chunks)
    ]
    for copy in copies:
        copy.start()
    total = jnp.sum(totals[...], axis=0)
    mean = jnp.sum(total, axis=1, keepdims=True) * (1.0 / cells)
    mean = jnp.broadcast_to(mean, (sizes.depth, sizes.width))
    for i in range(chunks):
        copies[i].wait()
        for row in range(i * step, i * step + step):
            held[row] = held[row] - mean
        back[i].start()
    for copy in back:
        copy.wait()


SMEM, VMEM, HBM, ANY = (pl.BlockSpec(memory_space=space) for space in (pltpu.SMEM, pltpu.VMEM, pltpu.HBM, pl.ANY))


def call(kernel, sizes, arrays, scalars, outs, out_specs, scratch):
    listed = sizes.listed
    factors = [(listed * sizes.planes * SUB, LANES), (listed * sizes.depth, LANES), (listed * sizes.rows, LANES)]
    factors = [pltpu.VMEM(shape, jnp.float32) for shape in factors]
    matrix = pltpu.VMEM((2 * LANES, len(turns(sizes)) * LANES), jnp.bfloat16)
    flat, tree = jax.tree.flatten(scalars)

    def body(*refs):
        ins, refs = refs[: len(arrays)], refs[len(arrays) :]
        scalar_refs, refs = jax.tree.unflatten(tree, refs[: len(flat)]), refs[len(flat) :]
        out_refs, refs = refs[: len(outs)], refs[len(outs) :]
        kernel(*ins, *scalar_refs, *out_refs, refs[: len(factors)], *refs[len(factors) :])

    return pl.pallas_call(
        body,
        out_shape=outs,
        in_specs=[ANY] * len(arrays) + [SMEM] * len(flat),
        out_specs=out_specs,
        scratch_shapes=[*factors, matrix, *scratch],
        compiler_params=pltpu.CompilerParams(vmem_limit_bytes=61 * 2**20),
    )(*arrays, *flat)


def from_above(cells, axis, hops=1):
    count = lax.axis_size(axis)
    return lax.ppermute(cells, axis, [(i + hops, i) for i in range(count - hops)])


def from_below(cells, axis, hops=1):
    count = lax.axis_size(axis)
    return lax.ppermute(cells, axis, [(i, i + hops) for i in range(count - hops)])


def beyond_levels(own):
    depth = own.shape[2]
    scen_count, scen = lax.axis_size("scen"), lax.axis_index("scen")
    low, high = [], []
    for hop in range(-(-LOW // depth), 0, -1):
        low.append(from_below(own, "scen", hop) if hop < scen_count else jnp.zeros_like(own))
    for hop in range(1, -(-HIGH // depth) + 1):
        high.append(from_above(own, "scen", hop) if hop < scen_count else jnp.zeros_like(own))
    low = jnp.concatenate(low, axis=2)[:, :, -LOW:]
    high = jnp.concatenate(high, axis=2)[:, :, :HIGH]
    for hop in range(1, -(-HIGH // depth)):
        fill = high[:, :, hop * depth - 1 : hop * depth]
        keep = lax.broadcasted_iota(jnp.int32, high.shape, 2) < hop * depth
        high = jnp.where(jnp.logical_or(scen + hop != scen_count - 1, keep), high, fill)
    return jnp.concatenate([low, high], axis=2)


def on_device(value_next, scenario_ids, inflow_table, release_shifts, price):
    rows, depth, width = value_next.shape
    grid_count, scen_count = lax.axis_size("grid"), lax.axis_size("scen")
    scenarios = scenario_ids.shape[0] * scen_count
    sizes = Sizes(rows, depth, width, scenarios, release_shifts.shape[0], grid_count, scen_count)

    ids = [scenario_ids]
    for hop in range(1, scen_count):
        ids.append(lax.ppermute(scenario_ids, "scen", [(i, (i + hop) % scen_count) for i in range(scen_count)]))
    ids = [each[i : i + 1] for each in ids for i in range(scenario_ids.shape[0])]

    def like(*shape, kind=jnp.float32):
        return jax.ShapeDtypeStruct(shape, kind)

    planes = sizes.planes
    made = [like(count, planes, depth, LANES) for _, count in sizes.pieces]
    if sizes.pair:
        made.append(like(rows, planes, HIGH, LANES))
    made = pl.pallas_call(
        functools.partial(planes_kernel, sizes),
        out_shape=made,
        in_specs=[HBM],
        out_specs=[HBM] * len(made),
        scratch_shapes=[
            pltpu.VMEM(value_next.shape, jnp.float32), pltpu.VMEM((rows, planes, depth, LANES), jnp.float32),
            pltpu.SemaphoreType.DMA((rows + 4,)),
        ],
        compiler_params=pltpu.CompilerParams(vmem_limit_bytes=61 * 2**20),
    )(value_next)
    made, ids = lax.optimization_barrier((made, ids))
    pieces = made[: len(sizes.pieces)]
    scalars = (release_shifts.T, inflow_table.T, price, ids)
    if sizes.pair:
        beyond = lax.ppermute(made[-1], "scen", [(0, 1), (1, 0)])
    else:
        beyond = beyond_levels(jnp.concatenate(pieces, axis=0))
    before = from_below(pieces[-1][-H:], "grid")
    after = from_above(pieces[0][:H], "grid")

    shape = (scenarios, rows, sizes.planes, depth, LANES)
    sums_shape = jax.ShapeDtypeStruct(shape, jnp.float32)
    sums_held = pltpu.VMEM(shape, jnp.float32)
    inside, outside = rows + 2, 2 * H
    listed = sizes.listed
    factors = [like(listed * planes * SUB, LANES), like(listed * depth, LANES), like(listed * rows, LANES)]
    lists = [2 * (H + 2) + scenarios, listed * sizes.columns, scenarios * sizes.far_size]
    lists = [like(size, kind=jnp.int32) for size in lists]
    sums, *factors = call(
        functools.partial(own_kernel, sizes), sizes, pieces, scalars, [sums_shape, *factors, *lists], [HBM] * 4 + [SMEM] * 3,
        [
            pltpu.VMEM((inside * sizes.row_size, LANES), jnp.float32), sums_held,
            pltpu.VMEM((rows, planes, depth, LANES), jnp.float32), pltpu.SemaphoreType.DMA((8,)),
        ],
    )
    factors, lists = factors[:3], factors[3:]
    beyond, sums = lax.optimization_barrier((beyond, sums))
    corner_before = from_below(beyond[rows - H :], "grid")
    corner_after = from_above(beyond[:H], "grid")
    (sums,) = call(
        functools.partial(edge_kernel, sizes), sizes, (beyond, before, after, sums, *factors), lists, [sums_shape], [HBM],
        [
            pltpu.VMEM((outside * sizes.row_size, LANES), jnp.float32), pltpu.VMEM((inside * sizes.edge_size, LANES), jnp.float32),
            sums_held, pltpu.VMEM(beyond.shape, jnp.float32), pltpu.VMEM((2 * H, planes, depth, LANES), jnp.float32),
            pltpu.SemaphoreType.DMA((8,)),
        ],
    )
    scale = -softness / scenarios
    devices = grid_count * scen_count
    average, totals = call(
        functools.partial(last_kernel, sizes, scale), sizes, (corner_before, corner_after, sums, *factors), lists,
        [jax.ShapeDtypeStruct(value_next.shape, jnp.float32), jax.ShapeDtypeStruct((devices, 1, LANES), jnp.float32)],
        [HBM, VMEM],
        [
            pltpu.VMEM((outside * sizes.edge_size, LANES), jnp.float32), sums_held, pltpu.VMEM((2 * H, *beyond.shape[1:]), jnp.float32), pltpu.VMEM(value_next.shape, jnp.float32),
            pltpu.SemaphoreType.DMA((7,)),
        ],
    )
    totals = lax.all_to_all(totals, ("scen", "grid"), 0, 0, tiled=True)
    cells = rows * grid_count * depth * scen_count * width
    return pl.pallas_call(
        functools.partial(mean_kernel, sizes, cells),
        out_shape=jax.ShapeDtypeStruct(value_next.shape, jnp.float32),
        in_specs=[VMEM, HBM],
        out_specs=HBM,
        scratch_shapes=[pltpu.VMEM(value_next.shape, jnp.float32), pltpu.SemaphoreType.DMA((16,))],
        compiler_params=pltpu.CompilerParams(vmem_limit_bytes=61 * 2**20),
    )(totals, average)


def solution(mesh):
    placed = (P("grid", "scen", None), P("scen"), P(), P(), P())
    return jax.shard_map(
        on_device, mesh=mesh, in_specs=placed, out_specs=P("grid", "scen", None), check_vma=False
    )
```

time: 93.2 us -> 82.6 us (0.89)
  Pallas kernels: 60.6 us -> 46.4 us
  waiting for transfers between devices: 0.9 us -> 2.91 us
  blocking collectives: 15 us -> 16.9 us
  other arithmetic: 1.86 us -> 0 us
  starting transfers between devices: 11.8 us -> 13.5 us
    pallas_call x4, Pallas kernels: 57.5 us -> 43.3 us  [the longest x3 38.2 us: call(): pl.pallas_call(body, out_shape=outs, in_specs=[ANY] * len(arrays) + [SMEM...]
    ppermute x1, waiting for transfers between devices: 0.88 us -> 2.9 us  [on_device(): beyond = lax.ppermute(made[-1], 'scen', [(0, 1), (1, 0)])]
    all_to_all x1, blocking collectives: 15 us -> 16.9 us  [on_device(): totals = lax.all_to_all(totals, ('scen', 'grid'), 0, 0, tiled=True)]
    select_n x1 -> x0, other arithmetic: 1.86 us -> none  [on_device(): sent = jnp.where(scen == 0, own[:, :, depth - HIGH:], own[:, :, :HIGH])]
    ppermute x2, starting transfers between devices: 6.16 us -> 7.93 us  [from_below(): lax.ppermute(cells, axis, [(i, i + hops) for i in range(count - hops)])]
  transfers between devices with their start and end apart: 6 -> 6, of which waited for: 1 -> 1; matrix products, arithmetic and copies ran while one was open for 0% -> 1% of each run, Pallas kernels for 48% -> 43%
where the time goes in v4:
time: 82.6 us; the launch traced here: 82.5 us
  Pallas kernels  46.4 us (56%)
  blocking collectives  16.9 us (20%)
  starting transfers between devices  13.5 us (16%)
  waiting for transfers between devices  2.91 us (4%)
  local copies, waits for them, and re-layouts  1.96 us (2%)
    pallas_call x3, Pallas kernels, call(): pl.pallas_call(body, out_shape=outs, in_specs=[ANY] * len(arrays) + [SMEM...  38.2 us
    all_to_all x1, blocking collectives, on_device(): totals = lax.all_to_all(totals, ('scen', 'grid'), 0, 0, tiled=True)  16.9 us
    ppermute x2, starting transfers between devices, from_below(): lax.ppermute(cells, axis, [(i, i + hops) for i in range(count - hops)])  7.93 us
    pallas_call x1, Pallas kernels, on_device(): pl.pallas_call(functools.partial(planes_kernel, sizes), out_shape=made, i...  5.09 us
    pallas_call x1, Pallas kernels, on_device(): pl.pallas_call(functools.partial(mean_kernel, sizes, cells), out_shape=ja...  3.13 us
    ppermute x1, starting transfers between devices, on_device(): lax.ppermute(scenario_ids, 'scen', [(i, (i + hop) % scen_count) for i in...  2.94 us
    ppermute x1, waiting for transfers between devices, on_device(): beyond = lax.ppermute(made[-1], 'scen', [(0, 1), (1, 0)])  2.9 us
    ppermute x2, starting transfers between devices, from_above(): lax.ppermute(cells, axis, [(i + hops, i) for i in range(count - hops)])  2.57 us
  transfers between devices with their start and end apart: 6, of which 1 were waited for; matrix products, arithmetic and copies ran while one was open for 1% of the time, Pallas kernels for 43%

profile of v4, /device:TPU:0, one launch (start us, length us, event | category | flops | bytes accessed | tf_op | source)
XLA Modules:
  0.0 82.5 jit_solution(15595743989970959595)
XLA Ops:
  0.0 2.9 %collective-permute-start = (s32[1]{0:T(128)}, s32[1]{0:T(128)}, u32[]{:S(2)}, u32[]{:S(2)}) collective-permute-start(s32[1]{0:T(128)} %param.6), channel_id=1, source_target_pairs={{0,16},{16,0},{1,17},{17,1},{2,18},{18,2},{3,19},{19,3},{4,20},{20... | collective-permute-start | bytes 20 | tf_op jit(solution)/shard_map/ppermute | solution.py:688
  2.9 5.1 %shard_map.55 = (f32[8,8,32,128]{3,2,1,0:T(8,128)}, f32[8,8,32,128]{3,2,1,0:T(8,128)}, f32[16,8,16,128]{3,2,1,0:T(8,128)}) custom-call(f32[16,32,1024]{2,1,0:T(8,128)} %values.1), custom_call_target="tpu_custom_call" | custom-call | tf_op jit(solution)/shard_map/pallas_call | solution.py:698
  8.0 0.0 collective-permute-done.refs_6_
  8.1 0.1 collective-permute-start.1
  8.1 1.3 %collective-permute-start.5 = (f32[8,8,32,128]{3,2,1,0:T(8,128)}, f32[8,8,32,128]{3,2,1,0:T(8,128)S(1)}, u32[]{:S(2)}, u32[]{:S(2)}) collective-permute-start(f32[8,8,32,128]{3,2,1,0:T(8,128)} %get-tuple-element.28.refs_0_), channel_id=1, source_target_pairs={{1,0},{2,1},{3,2},{4,3},{5,4},{6,5},{7,6},{8,7},{9,8},{10,9},{11,1... | collective-permute-start | bytes 3145736 | tf_op jit(solution)/shard_map/ppermute | solution.py:655
  9.4 4.1 %collective-permute-start.4 = (f32[8,8,32,128]{3,2,1,0:T(8,128)}, f32[8,8,32,128]{3,2,1,0:T(8,128)}, u32[]{:S(2)}, u32[]{:S(2)}) collective-permute-start(f32[8,8,32,128]{3,2,1,0:T(8,128)} %get-tuple-element.29.refs_1_), channel_id=1, source_target_pairs={{0,1},{1,2},{2,3},{3,4},{4,5},{5,6},{6,7},{7,8},{8,9},{9,10},{10,1... | collective-permute-start | bytes 3145736 | tf_op jit(solution)/shard_map/ppermute | solution.py:660
  14.2 15.9 %shard_map.56 = (f32[2,16,8,32,128]{4,3,2,1,0:T(8,128)}, f32[1088,128]{1,0:T(8,128)}, f32[544,128]{1,0:T(8,128)}, f32[272,128]{1,0:T(8,128)}, s32[22]{0:T(128)}, /*index=5*/s32[119]{0:T(128)}, s32[38]{0:T(128)}) custom-call(f32[8,8,32,128]{3,2,1,0:T(8,128)} %get-tuple-element.28.refs_0_, f32[8,8,32,128]{3,2,1,0:T(8,128)} %get-tuple-element.29.refs_1_, ...), custom_call_target="tpu_custom_call" | custom-call | tf_op jit(solution)/shard_map/pallas_call | solution.py:643
  30.0 2.9 %collective-permute-done.1.refs_0_ = f32[16,8,16,128]{3,2,1,0:T(8,128)S(1)} collective-permute-done((f32[16,8,16,128]{3,2,1,0:T(8,128)}, f32[16,8,16,128]{3,2,1,0:T(8,128)S(1)}, u32[]{:S(2)}, u32[]{:S(2)}) %collective-permute-start.1) | collective-permute-done | bytes 1048608 | tf_op jit(solution)/shard_map/ppermute | solution.py:713
  32.9 0.0 copy-start
  32.9 1.0 %fusion = (f32[8,8,16,128]{3,2,1,0:T(8,128)}, f32[8,8,16,128]{3,2,1,0:T(8,128)S(1)}) fusion(f32[16,8,16,128]{3,2,1,0:T(8,128)S(1)} %collective-permute-done.1.refs_0_), kind=kLoop, calls=%fused_computation | loop fusion | bytes 2097152 | tf_op jit(solution)/shard_map/slice | solution.py:737
  33.9 1.3 %collective-permute-start.3 = (f32[8,8,16,128]{3,2,1,0:T(8,128)}, f32[8,8,16,128]{3,2,1,0:T(8,128)}, u32[]{:S(2)}, u32[]{:S(2)}) collective-permute-start(f32[8,8,16,128]{3,2,1,0:T(8,128)} %get-tuple-element.43), channel_id=1, source_target_pairs={{1,0},{2,1},{3,2},{4,3},{5,4},{6,5},{7,6},{8,7},{9,8},{10,9},{11,1... | collective-permute-start | bytes 1572872 | tf_op jit(solution)/shard_map/ppermute | solution.py:655
  35.2 3.8 %collective-permute-start.2 = (f32[8,8,16,128]{3,2,1,0:T(8,128)S(1)}, f32[8,8,16,128]{3,2,1,0:T(8,128)}, u32[]{:S(2)}, u32[]{:S(2)}) collective-permute-start(f32[8,8,16,128]{3,2,1,0:T(8,128)S(1)} %get-tuple-element.44), channel_id=1, source_target_pairs={{0,1},{1,2},{2,3},{3,4},{4,5},{5,6},{6,7},{7,8},{8,9},{9,10},{10,1... | collective-permute-start | bytes 1572872 | tf_op jit(solution)/shard_map/ppermute | solution.py:660
  39.1 0.0 collective-permute-done.5.refs_2_
  39.1 0.0 copy-start.1
  39.1 0.0 collective-permute-done.4.refs_1_
  39.1 0.0 copy-done
  39.1 1.0 %copy-done.1 = f32[8,8,32,128]{3,2,1,0:T(8,128)} copy-done((f32[8,8,32,128]{3,2,1,0:T(8,128)}, f32[8,8,32,128]{3,2,1,0:T(8,128)S(1)}, u32[]{:S(2)}) %copy-start.1) | copy-done | bytes 1048600
  40.0 14.1 %shard_map.57.refs_2_ = f32[2,16,8,32,128]{4,3,2,1,0:T(8,128)} custom-call(f32[16,8,16,128]{3,2,1,0:T(8,128)} %copy-done, f32[8,8,32,128]{3,2,1,0:T(8,128)} %collective-permute-done.4.refs_1_, f32[8,8,32,128]{3,2,1,0:T(8,128)} %copy-done.1, f32[2,16,8,32,128]{4,3,2,1,0:T(8,128)} %get-tuple-element.34.refs_3_, f32[1088,128]{1,0:T(8,128)} %get-tuple-element.35.refs_4_.refs_3_, ...), custom_call_target="tpu_custom_call" | custom-call | tf_op jit(solution)/shard_map/pallas_call | solution.py:643
  54.2 0.0 collective-permute-done.3.refs_1_
  54.2 0.0 collective-permute-done.2.refs_0_
  54.2 8.2 %shard_map.58 = (f32[16,32,1024]{2,1,0:T(8,128)}, f32[32,1,128]{2,1,0:T(1,128)}) custom-call(f32[8,8,16,128]{3,2,1,0:T(8,128)} %collective-permute-done.2.refs_0_, f32[8,8,16,128]{3,2,1,0:T(8,128)} %collective-permute-done.3.refs_1_, f32[2,16,8,32,128]{4,3,2,1,0:T(8,128)} %shard_map.57.refs_2_, f32[1088,128]{1,0:T(8,128)} %get-tuple-element.35.refs_4_.refs_3_, ...), custom_call_target="tpu_custom_call" | custom-call | tf_op jit(solution)/shard_map/pallas_call | solution.py:643
  62.4 16.9 %all_to_all.5.totals = f32[32,1,128]{2,1,0:T(1,128)} all-to-all(f32[32,1,128]{2,1,0:T(1,128)} %get-tuple-element.41), channel_id=1, replica_groups=mesh['scen'=2,'grid'=16] {'scen','grid'}, dimensions={0} | all-to-all | bytes 32768 | tf_op jit(solution)/shard_map/all_to_all | solution.py:757
  79.3 3.1 %shard_map.59 = f32[16,32,1024]{2,1,0:T(8,128)} custom-call(f32[32,1,128]{2,1,0:T(1,128)} %all_to_all.5.totals, f32[16,32,1024]{2,1,0:T(8,128)} %get-tuple-element.42.average), custom_call_target="tpu_custom_call" | custom-call | tf_op jit(solution)/shard_map/pallas_call | solution.py:759
Async XLA Ops:
  0.0 8.0 %collective-permute-start = (s32[1]{0:T(128)}, s32[1]{0:T(128)}, u32[]{:S(2)}, u32[]{:S(2)}) collective-permute-start(s32[1]{0:T(128)} %param.6), channel_id=1, source_target_pairs={{0,16},{16,0},{1,17},{17,1},{2,18},{18,2},{3,19},{19,3},{4,20},{20... | collective-permute-start | bytes 20 | tf_op jit(solution)/shard_map/ppermute | solution.py:688
  8.1 24.9 %collective-permute-start.1 = (f32[16,8,16,128]{3,2,1,0:T(8,128)}, f32[16,8,16,128]{3,2,1,0:T(8,128)S(1)}, u32[]{:S(2)}, u32[]{:S(2)}) collective-permute-start(f32[16,8,16,128]{3,2,1,0:T(8,128)} %get-tuple-element.27), channel_id=1, source_target_pairs={{0,16},{16,0},{1,17},{17,1},{2,18},{18,2},{3,19},{19,3},{4,20},{20... | collective-permute-start | bytes 3145736 | tf_op jit(solution)/shard_map/ppermute | solution.py:713
  8.1 30.9 %collective-permute-start.5 = (f32[8,8,32,128]{3,2,1,0:T(8,128)}, f32[8,8,32,128]{3,2,1,0:T(8,128)S(1)}, u32[]{:S(2)}, u32[]{:S(2)}) collective-permute-start(f32[8,8,32,128]{3,2,1,0:T(8,128)} %get-tuple-element.28.refs_0_), channel_id=1, source_target_pairs={{1,0},{2,1},{3,2},{4,3},{5,4},{6,5},{7,6},{8,7},{9,8},{10,9},{11,1... | collective-permute-start | bytes 3145736 | tf_op jit(solution)/shard_map/ppermute | solution.py:655
  9.4 29.6 %collective-permute-start.4 = (f32[8,8,32,128]{3,2,1,0:T(8,128)}, f32[8,8,32,128]{3,2,1,0:T(8,128)}, u32[]{:S(2)}, u32[]{:S(2)}) collective-permute-start(f32[8,8,32,128]{3,2,1,0:T(8,128)} %get-tuple-element.29.refs_1_), channel_id=1, source_target_pairs={{0,1},{1,2},{2,3},{3,4},{4,5},{5,6},{6,7},{7,8},{8,9},{9,10},{10,1... | collective-permute-start | bytes 3145736 | tf_op jit(solution)/shard_map/ppermute | solution.py:660
  32.9 6.1 %copy-start = (f32[16,8,16,128]{3,2,1,0:T(8,128)}, f32[16,8,16,128]{3,2,1,0:T(8,128)S(1)}, u32[]{:S(2)}) copy-start(f32[16,8,16,128]{3,2,1,0:T(8,128)S(1)} %collective-permute-done.1.refs_0_) | copy-start | bytes 3145732
  33.9 20.2 %collective-permute-start.3 = (f32[8,8,16,128]{3,2,1,0:T(8,128)}, f32[8,8,16,128]{3,2,1,0:T(8,128)}, u32[]{:S(2)}, u32[]{:S(2)}) collective-permute-start(f32[8,8,16,128]{3,2,1,0:T(8,128)} %get-tuple-element.43), channel_id=1, source_target_pairs={{1,0},{2,1},{3,2},{4,3},{5,4},{6,5},{7,6},{8,7},{9,8},{10,9},{11,1... | collective-permute-start | bytes 1572872 | tf_op jit(solution)/shard_map/ppermute | solution.py:655
  35.2 19.0 %collective-permute-start.2 = (f32[8,8,16,128]{3,2,1,0:T(8,128)S(1)}, f32[8,8,16,128]{3,2,1,0:T(8,128)}, u32[]{:S(2)}, u32[]{:S(2)}) collective-permute-start(f32[8,8,16,128]{3,2,1,0:T(8,128)S(1)} %get-tuple-element.44), channel_id=1, source_target_pairs={{0,1},{1,2},{2,3},{3,4},{4,5},{5,6},{6,7},{7,8},{8,9},{9,10},{10,1... | collective-permute-start | bytes 1572872 | tf_op jit(solution)/shard_map/ppermute | solution.py:660
  39.1 1.0 %copy-start.1 = (f32[8,8,32,128]{3,2,1,0:T(8,128)}, f32[8,8,32,128]{3,2,1,0:T(8,128)S(1)}, u32[]{:S(2)}) copy-start(f32[8,8,32,128]{3,2,1,0:T(8,128)S(1)} %collective-permute-done.5.refs_2_) | copy-start | bytes 3145732

commit v5 on v4

--- a/solution.py
+++ b/solution.py
@@ -12,6 +12,7 @@
 SUB, LANES = 8, 128
 TILE = 2
 CHUNK = 4
+FILL = 8
 UNROLL = 2
 softness = 0.5
 
@@ -418,13 +419,15 @@
     return [(first, min(most, strips - first)) for first in range(0, strips, most)]
 
 
-def fill_pairs(count, held, fill):
+def fill_rows(count, held, fill):
+    together = FILL if count % FILL == 0 else 1
+
     def step(index, _):
-        rows = [2 * index, 2 * index + 1]
+        rows = [together * index + i for i in range(together)]
         fill(rows, [held[row] for row in rows])
         return 0
 
-    lax.fori_loop(0, count // 2, step, 0)
+    lax.fori_loop(0, count // together, step, 0)
 
 
 def planes_kernel(sizes, values, *refs):
@@ -486,7 +489,7 @@
     plan = Plan(sizes, below, table, far, factors, matrix)
     for copy in copies:
         copy.wait()
-    fill_pairs(sizes.rows, held, lambda rows, values: plan.put_rows(weights, [row + 1 for row in rows], values))
+    fill_rows(sizes.rows, held, lambda rows, values: plan.put_rows(weights, [row + 1 for row in rows], values))
     plan.fill_beyond(weights, sizes.row_size)
     zero = jnp.zeros((SUB, LANES), jnp.float32)
 
@@ -510,7 +513,7 @@
 
 
 def edge_kernel(
-    sizes, beyond, before, after, sums_in, gains, depths, heights, below, table, far, sums_out, factors, matrix, weights, edges, sums, held,
+    sizes, beyond, before, after, sums_in, gains, depths, heights, below, table, far, sums, factors, matrix, weights, edges, held,
     rows_held, sems,
 ):
     copies = [
@@ -524,7 +527,7 @@
     copies += start_copies((gains, depths, heights), factors, sems.at[pl.ds(5, 3)])
     plan = Plan(sizes, below, table, far, factors, matrix)
     copies[0].wait()
-    fill_pairs(sizes.rows, held, lambda rows, values: plan.put_edges(edges, [row + 1 for row in rows], values))
+    fill_rows(sizes.rows, held, lambda rows, values: plan.put_edges(edges, [row + 1 for row in rows], values))
     plan.fill_beyond(edges, sizes.edge_size)
     for copy in (copies[1], *copies[4:]):
         copy.wait()
@@ -542,20 +545,16 @@
         plan.own_terms(load, store, edges, True, 0, sizes.edge_strips)
     copies[2].wait()
     copies[3].wait()
-    fill_pairs(2 * H, rows_held, functools.partial(plan.put_rows, weights))
+    fill_rows(2 * H, rows_held, functools.partial(plan.put_rows, weights))
     sets = strip_sets(sizes.strips)
 
-    def done(scenario, row):
-        pltpu.make_async_copy(sums.at[scenario, row], sums_out.at[scenario, row], sems.at[4]).start()
-
-    for index, (first, count) in enumerate(sets):
-        plan.outside_terms(sums, weights, False, first, count, done if index == len(sets) - 1 else None)
-    pltpu.make_async_copy(sums, sums_out, sems.at[4]).wait()
+    for first, count in sets:
+        plan.outside_terms(sums, weights, False, first, count)
 
 
 def last_kernel(
-    sizes, scale, before, after, sums_in, gains, depths, heights, below, table, far, average_out, totals_out, factors, matrix, edges, sums,
-    held, average, sems,
+    sizes, scale, before, after, sums_in, gains, depths, heights, below, table, far, average, totals_out, factors, matrix, edges, sums,
+    held, sems,
 ):
     copies = [
         pltpu.make_async_copy(before, held.at[pl.ds(0, H)], sems.at[0]),
@@ -569,7 +568,7 @@
     copies[0].wait()
     copies[1].wait()
 
-    fill_pairs(2 * H, held, functools.partial(plan.put_edges, edges))
+    fill_rows(2 * H, held, functools.partial(plan.put_edges, edges))
     for copy in copies[2:]:
         copy.wait()
     for first, count in strip_sets(sizes.edge_strips):
@@ -592,33 +591,25 @@
                     total = total + averages[-1]
                 for block, values in enumerate(transpose(averages)):
                     average[row, levels, block * LANES : block * LANES + LANES] = values
-            pltpu.make_async_copy(average.at[row], average_out.at[row], sems.at[3]).start()
         return total
 
     total = lax.fori_loop(0, sizes.rows // 2, finish, jnp.zeros((SUB, LANES), jnp.float32))
     total = jnp.sum(total, axis=0, keepdims=True)
     totals_out[...] = jnp.broadcast_to(total[None], totals_out.shape)
-    pltpu.make_async_copy(average, average_out, sems.at[3]).wait()
 
 
 def mean_kernel(sizes, cells, totals, average, out, held, sems):
     chunks = min(8, sizes.rows)
     step = sizes.rows // chunks
-    copies = [
-        pltpu.make_async_copy(average.at[pl.ds(i * step, step)], held.at[pl.ds(i * step, step)], sems.at[i]) for i in range(chunks)
-    ]
     back = [
         pltpu.make_async_copy(held.at[pl.ds(i * step, step)], out.at[pl.ds(i * step, step)], sems.at[chunks + i]) for i in range(chunks)
     ]
-    for copy in copies:
-        copy.start()
     total = jnp.sum(totals[...], axis=0)
     mean = jnp.sum(total, axis=1, keepdims=True) * (1.0 / cells)
     mean = jnp.broadcast_to(mean, (sizes.depth, sizes.width))
     for i in range(chunks):
-        copies[i].wait()
         for row in range(i * step, i * step + step):
-            held[row] = held[row] - mean
+            held[row] = average[row] - mean
         back[i].start()
     for copy in back:
         copy.wait()
@@ -627,7 +618,7 @@
 SMEM, VMEM, HBM, ANY = (pl.BlockSpec(memory_space=space) for space in (pltpu.SMEM, pltpu.VMEM, pltpu.HBM, pl.ANY))
 
 
-def call(kernel, sizes, arrays, scalars, outs, out_specs, scratch):
+def call(kernel, sizes, arrays, scalars, outs, out_specs, scratch, limit=61):
     listed = sizes.listed
     factors = [(listed * sizes.planes * SUB, LANES), (listed * sizes.depth, LANES), (listed * sizes.rows, LANES)]
     factors = [pltpu.VMEM(shape, jnp.float32) for shape in factors]
@@ -646,7 +637,7 @@
         in_specs=[ANY] * len(arrays) + [SMEM] * len(flat),
         out_specs=out_specs,
         scratch_shapes=[*factors, matrix, *scratch],
-        compiler_params=pltpu.CompilerParams(vmem_limit_bytes=61 * 2**20),
+        compiler_params=pltpu.CompilerParams(vmem_limit_bytes=limit * 2**20),
     )(*arrays, *flat)
 
 
@@ -736,33 +727,35 @@
     corner_before = from_below(beyond[rows - H :], "grid")
     corner_after = from_above(beyond[:H], "grid")
     (sums,) = call(
-        functools.partial(edge_kernel, sizes), sizes, (beyond, before, after, sums, *factors), lists, [sums_shape], [HBM],
+        functools.partial(edge_kernel, sizes), sizes, (beyond, before, after, sums, *factors), lists, [sums_shape], [VMEM],
         [
             pltpu.VMEM((outside * sizes.row_size, LANES), jnp.float32), pltpu.VMEM((inside * sizes.edge_size, LANES), jnp.float32),
-            sums_held, pltpu.VMEM(beyond.shape, jnp.float32), pltpu.VMEM((2 * H, planes, depth, LANES), jnp.float32),
+            pltpu.VMEM(beyond.shape, jnp.float32), pltpu.VMEM((2 * H, planes, depth, LANES), jnp.float32),
             pltpu.SemaphoreType.DMA((8,)),
         ],
+        44,
     )
     scale = -softness / scenarios
     devices = grid_count * scen_count
     average, totals = call(
         functools.partial(last_kernel, sizes, scale), sizes, (corner_before, corner_after, sums, *factors), lists,
         [jax.ShapeDtypeStruct(value_next.shape, jnp.float32), jax.ShapeDtypeStruct((devices, 1, LANES), jnp.float32)],
-        [HBM, VMEM],
+        [VMEM, VMEM],
         [
-            pltpu.VMEM((outside * sizes.edge_size, LANES), jnp.float32), sums_held, pltpu.VMEM((2 * H, *beyond.shape[1:]), jnp.float32), pltpu.VMEM(value_next.shape, jnp.float32),
+            pltpu.VMEM((outside * sizes.edge_size, LANES), jnp.float32), sums_held, pltpu.VMEM((2 * H, *beyond.shape[1:]), jnp.float32),
             pltpu.SemaphoreType.DMA((7,)),
         ],
+        24,
     )
     totals = lax.all_to_all(totals, ("scen", "grid"), 0, 0, tiled=True)
     cells = rows * grid_count * depth * scen_count * width
     return pl.pallas_call(
         functools.partial(mean_kernel, sizes, cells),
         out_shape=jax.ShapeDtypeStruct(value_next.shape, jnp.float32),
-        in_specs=[VMEM, HBM],
+        in_specs=[VMEM, VMEM],
         out_specs=HBM,
         scratch_shapes=[pltpu.VMEM(value_next.shape, jnp.float32), pltpu.SemaphoreType.DMA((16,))],
-        compiler_params=pltpu.CompilerParams(vmem_limit_bytes=61 * 2**20),
+        compiler_params=pltpu.CompilerParams(vmem_limit_bytes=8 * 2**20),
     )(totals, average)
 
 

time: 82.6 us -> 71.7 us (0.87); the launches traced: 82.5 us -> 72.5 us
  Pallas kernels: 46.4 us -> 38.1 us
  local copies, waits for them, and re-layouts: 1.96 us -> 0.09 us
    pallas_call x3, Pallas kernels: 38.2 us -> 31.4 us  [call(): pl.pallas_call(body, out_shape=outs, in_specs=[ANY] * len(arrays) + [SMEM...]
    pallas_call x1, Pallas kernels: 3.13 us -> 1.57 us  [on_device(): pl.pallas_call(functools.partial(mean_kernel, sizes, cells), out_shape=ja...]
    unnamed x4 -> x12, local copies, waits for them, and re-layouts: 0.96 us -> 0.03 us
    slice x1, local copies, waits for them, and re-layouts: 0.99 us -> 0.07 us  [on_device(): corner_after = from_above(beyond[:H], 'grid')]
    ppermute x2, starting transfers between devices: 7.93 us -> 7.07 us  [from_below(): lax.ppermute(cells, axis, [(i, i + hops) for i in range(count - hops)])]
  transfers between devices with their start and end apart: 6 -> 6, of which waited for: 1 -> 1; matrix products, arithmetic and copies ran while one was open for 1% -> 0% of each run, Pallas kernels for 43% -> 43%
where the time goes in v5:
time: 71.7 us; the launch traced here: 72.5 us
  Pallas kernels  38.1 us (53%)
  blocking collectives  17.7 us (25%)
  starting transfers between devices  12.7 us (18%)
  waiting for transfers between devices  3.17 us (4%)
  between operations  0.86 us (1%)
    pallas_call x3, Pallas kernels, call(): pl.pallas_call(body, out_shape=outs, in_specs=[ANY] * len(arrays) + [SMEM...  31.4 us
    all_to_all x1, blocking collectives, on_device(): totals = lax.all_to_all(totals, ('scen', 'grid'), 0, 0, tiled=True)  17.7 us
    ppermute x2, starting transfers between devices, from_below(): lax.ppermute(cells, axis, [(i, i + hops) for i in range(count - hops)])  7.07 us
    pallas_call x1, Pallas kernels, on_device(): pl.pallas_call(functools.partial(planes_kernel, sizes), out_shape=made, i...  5.13 us
    ppermute x1, waiting for transfers between devices, on_device(): beyond = lax.ppermute(made[-1], 'scen', [(0, 1), (1, 0)])  3.16 us
    ppermute x1, starting transfers between devices, on_device(): lax.ppermute(scenario_ids, 'scen', [(i, (i + hop) % scen_count) for i in...  2.94 us
    ppermute x2, starting transfers between devices, from_above(): lax.ppermute(cells, axis, [(i + hops, i) for i in range(count - hops)])  2.58 us
    pallas_call x1, Pallas kernels, on_device(): pl.pallas_call(functools.partial(mean_kernel, sizes, cells), out_shape=ja...  1.57 us
  transfers between devices with their start and end apart: 6, of which 1 were waited for; matrix products, arithmetic and copies ran while one was open for 0% of the time, Pallas kernels for 43%

profile of v5, /device:TPU:0, one launch (start us, length us, event | category | flops | bytes accessed | tf_op | source)
XLA Modules:
  0.0 72.5 jit_solution(14156011920888214951)
XLA Ops:
  0.0 2.9 %collective-permute-start = (s32[1]{0:T(128)}, s32[1]{0:T(128)}, u32[]{:S(2)}, u32[]{:S(2)}) collective-permute-start(s32[1]{0:T(128)} %param.6), channel_id=1, source_target_pairs={{0,16},{16,0},{1,17},{17,1},{2,18},{18,2},{3,19},{19,3},{4,20},{20... | collective-permute-start | bytes 20 | tf_op jit(solution)/shard_map/ppermute | solution.py:679
  2.9 5.1 %shard_map.55 = (f32[8,8,32,128]{3,2,1,0:T(8,128)}, f32[8,8,32,128]{3,2,1,0:T(8,128)}, f32[16,8,16,128]{3,2,1,0:T(8,128)}) custom-call(f32[16,32,1024]{2,1,0:T(8,128)} %values.1), custom_call_target="tpu_custom_call" | custom-call | tf_op jit(solution)/shard_map/pallas_call | solution.py:689
  8.1 0.0 collective-permute-done.refs_6_
  8.1 0.1 collective-permute-start.1
  8.2 1.3 %collective-permute-start.5 = (f32[8,8,32,128]{3,2,1,0:T(8,128)}, f32[8,8,32,128]{3,2,1,0:T(8,128)S(1)}, u32[]{:S(2)}, u32[]{:S(2)}) collective-permute-start(f32[8,8,32,128]{3,2,1,0:T(8,128)} %get-tuple-element.28.refs_0_), channel_id=1, source_target_pairs={{1,0},{2,1},{3,2},{4,3},{5,4},{6,5},{7,6},{8,7},{9,8},{10,9},{11,1... | collective-permute-start | bytes 3145736 | tf_op jit(solution)/shard_map/ppermute | solution.py:646
  9.5 4.0 %collective-permute-start.4 = (f32[8,8,32,128]{3,2,1,0:T(8,128)}, f32[8,8,32,128]{3,2,1,0:T(8,128)}, u32[]{:S(2)}, u32[]{:S(2)}) collective-permute-start(f32[8,8,32,128]{3,2,1,0:T(8,128)} %get-tuple-element.29.refs_1_), channel_id=1, source_target_pairs={{0,1},{1,2},{2,3},{3,4},{4,5},{5,6},{6,7},{7,8},{8,9},{9,10},{10,1... | collective-permute-start | bytes 3145736 | tf_op jit(solution)/shard_map/ppermute | solution.py:651
  14.1 15.6 %shard_map.56 = (f32[2,16,8,32,128]{4,3,2,1,0:T(8,128)}, f32[1088,128]{1,0:T(8,128)}, f32[544,128]{1,0:T(8,128)}, f32[272,128]{1,0:T(8,128)}, s32[22]{0:T(128)}, /*index=5*/s32[119]{0:T(128)}, s32[38]{0:T(128)}) custom-call(f32[8,8,32,128]{3,2,1,0:T(8,128)} %get-tuple-element.28.refs_0_, f32[8,8,32,128]{3,2,1,0:T(8,128)} %get-tuple-element.29.refs_1_, ...), custom_call_target="tpu_custom_call" | custom-call | tf_op jit(solution)/shard_map/pallas_call | solution.py:634
  29.8 0.0 copy-start
  29.8 0.0 copy-start.1
  29.8 0.0 copy-start.2
  29.8 0.0 copy-start.3
  29.8 0.0 copy-start.4
  29.8 0.0 copy-start.5
  29.8 3.2 %collective-permute-done.1.refs_0_ = f32[16,8,16,128]{3,2,1,0:T(8,128)S(1)} collective-permute-done((f32[16,8,16,128]{3,2,1,0:T(8,128)}, f32[16,8,16,128]{3,2,1,0:T(8,128)S(1)}, u32[]{:S(2)}, u32[]{:S(2)}) %collective-permute-start.1) | collective-permute-done | bytes 1048608 | tf_op jit(solution)/shard_map/ppermute | solution.py:704
  33.0 0.1 fusion
  33.1 1.3 %collective-permute-start.3 = (f32[8,8,16,128]{3,2,1,0:T(8,128)S(1)}, f32[8,8,16,128]{3,2,1,0:T(8,128)S(1)}, u32[]{:S(2)}, u32[]{:S(2)}) collective-permute-start(f32[8,8,16,128]{3,2,1,0:T(8,128)S(1)} %get-tuple-element.43), channel_id=1, source_target_pairs={{1,0},{2,1},{3,2},{4,3},{5,4},{6,5},{7,6},{8,7},{9,8},{10,9},{11,1... | collective-permute-start | bytes 1572872 | tf_op jit(solution)/shard_map/ppermute | solution.py:646
  34.4 3.1 %collective-permute-start.2 = (f32[8,8,16,128]{3,2,1,0:T(8,128)S(1)}, f32[8,8,16,128]{3,2,1,0:T(8,128)S(1)}, u32[]{:S(2)}, u32[]{:S(2)}) collective-permute-start(f32[8,8,16,128]{3,2,1,0:T(8,128)S(1)} %get-tuple-element.44), channel_id=1, source_target_pairs={{0,1},{1,2},{2,3},{3,4},{4,5},{5,6},{6,7},{7,8},{8,9},{9,10},{10,1... | collective-permute-start | bytes 1572872 | tf_op jit(solution)/shard_map/ppermute | solution.py:651
  37.4 0.0 collective-permute-done.5.refs_2_
  37.4 0.0 collective-permute-done.4.refs_1_
  37.4 0.0 copy-done
  37.5 0.0 copy-done.1
  37.5 0.0 copy-done.2
  37.5 0.0 copy-done.3
  37.5 0.0 copy-done.4
  37.5 0.0 copy-done.5
  37.5 10.3 %shard_map.57.refs_2_ = f32[2,16,8,32,128]{4,3,2,1,0:T(8,128)S(1)} custom-call(f32[16,8,16,128]{3,2,1,0:T(8,128)S(1)} %collective-permute-done.1.refs_0_, f32[8,8,32,128]{3,2,1,0:T(8,128)} %collective-permute-done.4.refs_1_, f32[8,8,32,128]{3,2,1,0:T(8,128)S(1)} %collective-permute-done.5.refs_2_, f32[2,16,8,32,128]{4,3,2,1,0:T(8,128)} %get-tuple-element.34.refs_3_, ...), custom_call_target="tpu_custom_call" | custom-call | tf_op jit(solution)/shard_map/pallas_call | solution.py:634
  47.8 0.0 collective-permute-done.3.refs_1_
  47.8 0.0 collective-permute-done.2.refs_0_
  47.9 5.4 %shard_map.58 = (f32[16,32,1024]{2,1,0:T(8,128)S(1)}, f32[32,1,128]{2,1,0:T(1,128)S(1)}) custom-call(f32[8,8,16,128]{3,2,1,0:T(8,128)S(1)} %collective-permute-done.2.refs_0_, f32[8,8,16,128]{3,2,1,0:T(8,128)S(1)} %collective-permute-done.3.refs_1_, f32[2,16,8,32,128]{4,3,2,1,0:T(8,128)S(1)} %shard_map.57.refs_2_, f32[1088,128]{1,0:T(8,128)S(1)} %copy-done, ...), custom_call_target="tpu_custom_call" | custom-call | tf_op jit(solution)/shard_map/pallas_call | solution.py:634
  53.3 17.7 %all_to_all.5.totals = f32[32,1,128]{2,1,0:T(1,128)S(1)} all-to-all(f32[32,1,128]{2,1,0:T(1,128)S(1)} %get-tuple-element.41), channel_id=1, replica_groups=mesh['scen'=2,'grid'=16] {'scen','grid'}, dimensions={0} | all-to-all | bytes 32768 | tf_op jit(solution)/shard_map/all_to_all | solution.py:750
  71.0 1.6 %shard_map.59 = f32[16,32,1024]{2,1,0:T(8,128)} custom-call(f32[32,1,128]{2,1,0:T(1,128)S(1)} %all_to_all.5.totals, f32[16,32,1024]{2,1,0:T(8,128)S(1)} %get-tuple-element.42.average), custom_call_target="tpu_custom_call" | custom-call | tf_op jit(solution)/shard_map/pallas_call | solution.py:752
Async XLA Ops:
  0.0 8.1 %collective-permute-start = (s32[1]{0:T(128)}, s32[1]{0:T(128)}, u32[]{:S(2)}, u32[]{:S(2)}) collective-permute-start(s32[1]{0:T(128)} %param.6), channel_id=1, source_target_pairs={{0,16},{16,0},{1,17},{17,1},{2,18},{18,2},{3,19},{19,3},{4,20},{20... | collective-permute-start | bytes 20 | tf_op jit(solution)/shard_map/ppermute | solution.py:679
  8.1 24.9 %collective-permute-start.1 = (f32[16,8,16,128]{3,2,1,0:T(8,128)}, f32[16,8,16,128]{3,2,1,0:T(8,128)S(1)}, u32[]{:S(2)}, u32[]{:S(2)}) collective-permute-start(f32[16,8,16,128]{3,2,1,0:T(8,128)} %get-tuple-element.27), channel_id=1, source_target_pairs={{0,16},{16,0},{1,17},{17,1},{2,18},{18,2},{3,19},{19,3},{4,20},{20... | collective-permute-start | bytes 3145736 | tf_op jit(solution)/shard_map/ppermute | solution.py:704
  8.2 29.3 %collective-permute-start.5 = (f32[8,8,32,128]{3,2,1,0:T(8,128)}, f32[8,8,32,128]{3,2,1,0:T(8,128)S(1)}, u32[]{:S(2)}, u32[]{:S(2)}) collective-permute-start(f32[8,8,32,128]{3,2,1,0:T(8,128)} %get-tuple-element.28.refs_0_), channel_id=1, source_target_pairs={{1,0},{2,1},{3,2},{4,3},{5,4},{6,5},{7,6},{8,7},{9,8},{10,9},{11,1... | collective-permute-start | bytes 3145736 | tf_op jit(solution)/shard_map/ppermute | solution.py:646
  9.5 28.0 %collective-permute-start.4 = (f32[8,8,32,128]{3,2,1,0:T(8,128)}, f32[8,8,32,128]{3,2,1,0:T(8,128)}, u32[]{:S(2)}, u32[]{:S(2)}) collective-permute-start(f32[8,8,32,128]{3,2,1,0:T(8,128)} %get-tuple-element.29.refs_1_), channel_id=1, source_target_pairs={{0,1},{1,2},{2,3},{3,4},{4,5},{5,6},{6,7},{7,8},{8,9},{9,10},{10,1... | collective-permute-start | bytes 3145736 | tf_op jit(solution)/shard_map/ppermute | solution.py:651
  29.8 7.7 %copy-start = (f32[1088,128]{1,0:T(8,128)S(1)}, f32[1088,128]{1,0:T(8,128)}, u32[]{:S(2)}) copy-start(f32[1088,128]{1,0:T(8,128)} %get-tuple-element.35.refs_4_.refs_3_) | copy-start | bytes 1671172
  29.8 7.7 %copy-start.1 = (f32[544,128]{1,0:T(8,128)S(1)}, f32[544,128]{1,0:T(8,128)}, u32[]{:S(2)}) copy-start(f32[544,128]{1,0:T(8,128)} %get-tuple-element.36.refs_5_.refs_4_) | copy-start | bytes 835588
  29.8 7.7 %copy-start.2 = (f32[272,128]{1,0:T(8,128)S(1)}, f32[272,128]{1,0:T(8,128)}, u32[]{:S(2)}) copy-start(f32[272,128]{1,0:T(8,128)} %get-tuple-element.37.refs_6_.refs_5_) | copy-start | bytes 417796
  29.8 7.7 %copy-start.3 = (s32[22]{0:T(128)S(1)}, s32[22]{0:T(128)}, u32[]{:S(2)}) copy-start(s32[22]{0:T(128)} %get-tuple-element.38.refs_7_.refs_6_) | copy-start | bytes 268
  29.8 7.7 %copy-start.4 = (s32[119]{0:T(128)S(1)}, s32[119]{0:T(128)}, u32[]{:S(2)}) copy-start(s32[119]{0:T(128)} %get-tuple-element.39.refs_8_.refs_7_) | copy-start | bytes 1432
  29.8 7.7 %copy-start.5 = (s32[38]{0:T(128)S(1)}, s32[38]{0:T(128)}, u32[]{:S(2)}) copy-start(s32[38]{0:T(128)} %get-tuple-element.40.refs_9_.refs_8_) | copy-start | bytes 460
  33.1 14.8 %collective-permute-start.3 = (f32[8,8,16,128]{3,2,1,0:T(8,128)S(1)}, f32[8,8,16,128]{3,2,1,0:T(8,128)S(1)}, u32[]{:S(2)}, u32[]{:S(2)}) collective-permute-start(f32[8,8,16,128]{3,2,1,0:T(8,128)S(1)} %get-tuple-element.43), channel_id=1, source_target_pairs={{1,0},{2,1},{3,2},{4,3},{5,4},{6,5},{7,6},{8,7},{9,8},{10,9},{11,1... | collective-permute-start | bytes 1572872 | tf_op jit(solution)/shard_map/ppermute | solution.py:646
  34.4 13.5 %collective-permute-start.2 = (f32[8,8,16,128]{3,2,1,0:T(8,128)S(1)}, f32[8,8,16,128]{3,2,1,0:T(8,128)S(1)}, u32[]{:S(2)}, u32[]{:S(2)}) collective-permute-start(f32[8,8,16,128]{3,2,1,0:T(8,128)S(1)} %get-tuple-element.44), channel_id=1, source_target_pairs={{0,1},{1,2},{2,3},{3,4},{4,5},{5,6},{6,7},{7,8},{8,9},{9,10},{10,1... | collective-permute-start | bytes 1572872 | tf_op jit(solution)/shard_map/ppermute | solution.py:651

commit v6 on v5

--- a/solution.py
+++ b/solution.py
@@ -431,47 +431,33 @@
 
 
 def planes_kernel(sizes, values, *refs):
-    outs, (held, planes_held, sems) = refs[:-3], refs[-3:]
-    size = 4 if all(count % 4 == 0 for _, count in sizes.pieces) else 1
-    copies = [
-        pltpu.make_async_copy(values.at[pl.ds(row, size)], held.at[pl.ds(row, size)], sems.at[i])
-        for i, row in enumerate(range(0, sizes.rows, size))
-    ]
-    for copy in copies:
-        copy.start()
+    *outs, sent_sem = refs
     start = pl.multiple_of(jnp.where(lax.axis_index("scen") == 0, sizes.depth - HIGH, 0), SUB) if sizes.pair else None
-    sent_sem, first_sem = sems.at[len(copies)], len(copies) + 1
-
-    def step(row, _):
+
+    def step(out, first, row, _):
         for strip in range(sizes.strips):
             levels = slice(strip * SUB, strip * SUB + SUB)
             blocks = (
-                jnp.exp(held[row, levels, block * LANES : block * LANES + LANES] * (-1.0 / softness))
+                jnp.exp(values[row, levels, block * LANES : block * LANES + LANES] * (-1.0 / softness))
                 for block in range(sizes.planes)
             )
             for plane, each in enumerate(transpose(blocks)):
-                planes_held[row, plane, levels, :] = each
+                out[row - first, plane, levels, :] = each
         if sizes.pair:
-            pltpu.make_async_copy(planes_held.at[row, :, pl.ds(start, HIGH)], outs[-1].at[row], sent_sem).start()
+            pltpu.make_async_copy(out.at[row - first, :, pl.ds(start, HIGH)], outs[-1].at[row], sent_sem).start()
         return 0
 
-    pieces = []
-    for i, (first, count) in enumerate(sizes.pieces):
-        for row in range(first, first + count, size):
-            copies[row // size].wait()
-            lax.fori_loop(row, row + size, step, 0)
-        pieces.append(pltpu.make_async_copy(planes_held.at[pl.ds(first, count)], outs[i], sems.at[first_sem + i]))
-        pieces[-1].start()
+    for out, (first, count) in zip(outs, sizes.pieces):
+        lax.fori_loop(first, first + count, functools.partial(step, out, first), 0)
     if sizes.pair:
-        pltpu.make_async_copy(planes_held.at[:, :, pl.ds(start, HIGH)], outs[-1], sent_sem).wait()
-    for piece in pieces:
-        piece.wait()
+        for out, (first, count) in zip(outs, sizes.pieces):
+            pltpu.make_async_copy(out.at[:, :, pl.ds(start, HIGH)], outs[-1].at[pl.ds(first, count)], sent_sem).wait()
 
 
 def own_kernel(sizes, *refs):
     own, refs = refs[: len(sizes.pieces)], refs[len(sizes.pieces) :]
-    release, inflow, price, ids, sums_out, gains_out, depths_out, heights_out, below, table, far, factors, matrix, *refs = refs
-    weights, sums, held, sems = refs
+    release, inflow, price, ids, sums, gains, depths, heights, below, table, far, matrix, *refs = refs
+    weights, held, sems = refs
     copies = [
         pltpu.make_async_copy(piece, held.at[pl.ds(first, count)], sems.at[5 + i])
         for i, (piece, (first, count)) in enumerate(zip(own, sizes.pieces, strict=True))
@@ -479,13 +465,8 @@
     for copy in copies:
         copy.start()
     make_lists(sizes, release, inflow, ids, below, table, far)
+    factors = gains, depths, heights
     make_factors(sizes, release, price, table, *factors)
-    backs = [
-        pltpu.make_async_copy(ref, out, sems.at[2 + i])
-        for i, (ref, out) in enumerate(zip(factors, (gains_out, depths_out, heights_out), strict=True))
-    ]
-    for back in backs:
-        back.start()
     plan = Plan(sizes, below, table, far, factors, matrix)
     for copy in copies:
         copy.wait()
@@ -495,25 +476,13 @@
 
     def store(scenario, row, first, count, values, is_last):
         store_sums(sums, sizes, scenario, row, first, count, values)
-        if is_last:
-            pltpu.make_async_copy(sums.at[scenario, row], sums_out.at[scenario, row], sems.at[1]).start()
 
     chunk = CHUNK if sizes.releases % CHUNK == 0 else None
     plan.own_terms(lambda scenario, row, first, count: [zero] * (sizes.planes * count), store, weights, False, 0, sizes.strips, 0, chunk)
-    for back in backs:
-        back.wait()
-    pltpu.make_async_copy(sums, sums_out, sems.at[1]).wait()
-
-
-def start_copies(refs, held, sems):
-    copies = [pltpu.make_async_copy(ref, to, sems.at[i]) for i, (ref, to) in enumerate(zip(refs, held, strict=True))]
-    for copy in copies:
-        copy.start()
-    return copies
 
 
 def edge_kernel(
-    sizes, beyond, before, after, sums_in, gains, depths, heights, below, table, far, sums, factors, matrix, weights, edges, held,
+    sizes, beyond, before, after, sums_in, gains, depths, heights, below, table, far, sums, matrix, weights, edges, held,
     rows_held, sems,
 ):
     copies = [
@@ -524,13 +493,11 @@
     ]
     for copy in copies:
         copy.start()
-    copies += start_copies((gains, depths, heights), factors, sems.at[pl.ds(5, 3)])
-    plan = Plan(sizes, below, table, far, factors, matrix)
+    plan = Plan(sizes, below, table, far, (gains, depths, heights), matrix)
     copies[0].wait()
     fill_rows(sizes.rows, held, lambda rows, values: plan.put_edges(edges, [row + 1 for row in rows], values))
     plan.fill_beyond(edges, sizes.edge_size)
-    for copy in (copies[1], *copies[4:]):
-        copy.wait()
+    copies[1].wait()
 
     def store(scenario, row, first, count, values, is_last):
         store_sums(sums, sizes, scenario, row, first, count, values)
@@ -553,7 +520,7 @@
 
 
 def last_kernel(
-    sizes, scale, before, after, sums_in, gains, depths, heights, below, table, far, average, totals_out, factors, matrix, edges, sums,
+    sizes, scale, before, after, sums_in, gains, depths, heights, below, table, far, average, totals_out, matrix, edges, sums,
     held, sems,
 ):
     copies = [
@@ -563,8 +530,7 @@
     ]
     for copy in copies:
         copy.start()
-    copies += start_copies((gains, depths, heights), factors, sems.at[pl.ds(4, 3)])
-    plan = Plan(sizes, below, table, far, factors, matrix)
+    plan = Plan(sizes, below, table, far, (gains, depths, heights), matrix)
     copies[0].wait()
     copies[1].wait()
 
@@ -619,9 +585,6 @@
 
 
 def call(kernel, sizes, arrays, scalars, outs, out_specs, scratch, limit=61):
-    listed = sizes.listed
-    factors = [(listed * sizes.planes * SUB, LANES), (listed * sizes.depth, LANES), (listed * sizes.rows, LANES)]
-    factors = [pltpu.VMEM(shape, jnp.float32) for shape in factors]
     matrix = pltpu.VMEM((2 * LANES, len(turns(sizes)) * LANES), jnp.bfloat16)
     flat, tree = jax.tree.flatten(scalars)
 
@@ -629,14 +592,14 @@
         ins, refs = refs[: len(arrays)], refs[len(arrays) :]
         scalar_refs, refs = jax.tree.unflatten(tree, refs[: len(flat)]), refs[len(flat) :]
         out_refs, refs = refs[: len(outs)], refs[len(outs) :]
-        kernel(*ins, *scalar_refs, *out_refs, refs[: len(factors)], *refs[len(factors) :])
+        kernel(*ins, *scalar_refs, *out_refs, *refs)
 
     return pl.pallas_call(
         body,
         out_shape=outs,
-        in_specs=[ANY] * len(arrays) + [SMEM] * len(flat),
+        in_specs=[VMEM if array.ndim == 2 else ANY for array in arrays] + [SMEM] * len(flat),
         out_specs=out_specs,
-        scratch_shapes=[*factors, matrix, *scratch],
+        scratch_shapes=[matrix, *scratch],
         compiler_params=pltpu.CompilerParams(vmem_limit_bytes=limit * 2**20),
     )(*arrays, *flat)
 
@@ -689,13 +652,10 @@
     made = pl.pallas_call(
         functools.partial(planes_kernel, sizes),
         out_shape=made,
-        in_specs=[HBM],
-        out_specs=[HBM] * len(made),
-        scratch_shapes=[
-            pltpu.VMEM(value_next.shape, jnp.float32), pltpu.VMEM((rows, planes, depth, LANES), jnp.float32),
-            pltpu.SemaphoreType.DMA((rows + 4,)),
-        ],
-        compiler_params=pltpu.CompilerParams(vmem_limit_bytes=61 * 2**20),
+        in_specs=[VMEM],
+        out_specs=[VMEM] * len(made),
+        scratch_shapes=[pltpu.SemaphoreType.DMA],
+        compiler_params=pltpu.CompilerParams(vmem_limit_bytes=12 * 2**20),
     )(value_next)
     made, ids = lax.optimization_barrier((made, ids))
     pieces = made[: len(sizes.pieces)]
@@ -716,11 +676,12 @@
     lists = [2 * (H + 2) + scenarios, listed * sizes.columns, scenarios * sizes.far_size]
     lists = [like(size, kind=jnp.int32) for size in lists]
     sums, *factors = call(
-        functools.partial(own_kernel, sizes), sizes, pieces, scalars, [sums_shape, *factors, *lists], [HBM] * 4 + [SMEM] * 3,
+        functools.partial(own_kernel, sizes), sizes, pieces, scalars, [sums_shape, *factors, *lists], [VMEM] * 4 + [SMEM] * 3,
         [
-            pltpu.VMEM((inside * sizes.row_size, LANES), jnp.float32), sums_held,
-            pltpu.VMEM((rows, planes, depth, LANES), jnp.float32), pltpu.SemaphoreType.DMA((8,)),
+            pltpu.VMEM((inside * sizes.row_size, LANES), jnp.float32), pltpu.VMEM((rows, planes, depth, LANES), jnp.float32),
+            pltpu.SemaphoreType.DMA((8,)),
         ],
+        28,
     )
     factors, lists = factors[:3], factors[3:]
     beyond, sums = lax.optimization_barrier((beyond, sums))

time: 71.7 us -> 69.6 us (0.971); the launches traced: 72.5 us -> 68.7 us
  Pallas kernels: 38.1 us -> 34.3 us
  local copies, waits for them, and re-layouts: 0.09 us -> 3.63 us
  blocking collectives: 17.7 us -> 15.3 us
  starting transfers between devices: 12.7 us -> 11.8 us
    unnamed x12 -> x10, local copies, waits for them, and re-layouts: 0.03 us -> 3.54 us
    all_to_all x1, blocking collectives: 17.7 us -> 15.3 us  [on_device(): totals = lax.all_to_all(totals, ('scen', 'grid'), 0, 0, tiled=True)]
    pallas_call x1, Pallas kernels: 5.13 us -> 3.07 us  [on_device(): pl.pallas_call(functools.partial(planes_kernel, sizes), out_shape=made, i...]
    pallas_call x3, Pallas kernels: 31.4 us -> 29.7 us  [call(): pl.pallas_call(body, out_shape=outs, in_specs=[VMEM if array.ndim == 2 el...]
    ppermute x2, starting transfers between devices: 7.07 us -> 6.16 us  [from_below(): lax.ppermute(cells, axis, [(i, i + hops) for i in range(count - hops)])]
  transfers between devices with their start and end apart: 6 -> 6, of which waited for: 1 -> 1; matrix products, arithmetic and copies ran while one was open for 0% -> 0% of each run, Pallas kernels for 43% -> 40%
where the time goes in v6:
time: 69.6 us; the launch traced here: 68.7 us
  Pallas kernels  34.3 us (49%)
  blocking collectives  15.3 us (22%)
  starting transfers between devices  11.8 us (17%)
  local copies, waits for them, and re-layouts  3.63 us (5%)
  waiting for transfers between devices  2.97 us (4%)
  between operations  0.8 us (1%)
    pallas_call x3, Pallas kernels, call(): pl.pallas_call(body, out_shape=outs, in_specs=[VMEM if array.ndim == 2 el...  29.7 us
    all_to_all x1, blocking collectives, on_device(): totals = lax.all_to_all(totals, ('scen', 'grid'), 0, 0, tiled=True)  15.3 us
    ppermute x2, starting transfers between devices, from_below(): lax.ppermute(cells, axis, [(i, i + hops) for i in range(count - hops)])  6.16 us
    unnamed x10, local copies, waits for them, and re-layouts  3.54 us
    pallas_call x1, Pallas kernels, on_device(): pl.pallas_call(functools.partial(planes_kernel, sizes), out_shape=made, i...  3.07 us
    ppermute x1, waiting for transfers between devices, on_device(): beyond = lax.ppermute(made[-1], 'scen', [(0, 1), (1, 0)])  2.96 us
    ppermute x1, starting transfers between devices, on_device(): lax.ppermute(scenario_ids, 'scen', [(i, (i + hop) % scen_count) for i in...  2.94 us
    ppermute x2, starting transfers between devices, from_above(): lax.ppermute(cells, axis, [(i + hops, i) for i in range(count - hops)])  2.58 us
  transfers between devices with their start and end apart: 6, of which 1 were waited for; matrix products, arithmetic and copies ran while one was open for 0% of the time, Pallas kernels for 40%

profile of v6, /device:TPU:0, one launch (start us, length us, event | category | flops | bytes accessed | tf_op | source)
XLA Modules:
  0.0 68.7 jit_solution(3362265886176243828)
XLA Ops:
  0.0 2.9 %collective-permute-start = (s32[1]{0:T(128)}, s32[1]{0:T(128)}, u32[]{:S(2)}, u32[]{:S(2)}) collective-permute-start(s32[1]{0:T(128)} %param.6), channel_id=1, source_target_pairs={{0,16},{16,0},{1,17},{17,1},{2,18},{18,2},{3,19},{19,3},{4,20},{20... | collective-permute-start | bytes 20 | tf_op jit(solution)/shard_map/ppermute | solution.py:642
  2.9 0.0 copy-start.1
  2.9 1.6 %copy-done.1 = f32[16,32,1024]{2,1,0:T(8,128)S(1)} copy-done((f32[16,32,1024]{2,1,0:T(8,128)S(1)}, f32[16,32,1024]{2,1,0:T(8,128)}, u32[]{:S(2)}) %copy-start.1) | copy-done | bytes 2097176
  4.5 0.0 copy-start.2
  4.5 0.0 copy-start.3
  4.5 0.0 copy-start.4
  4.5 3.1 %shard_map.55 = (f32[8,8,32,128]{3,2,1,0:T(8,128)S(1)}, f32[8,8,32,128]{3,2,1,0:T(8,128)S(1)}, f32[16,8,16,128]{3,2,1,0:T(8,128)S(1)}) custom-call(f32[16,32,1024]{2,1,0:T(8,128)S(1)} %copy-done.1), custom_call_target="tpu_custom_call" | custom-call | tf_op jit(solution)/shard_map/pallas_call | solution.py:652
  7.6 0.0 collective-permute-done.refs_6_
  7.6 0.1 collective-permute-start.1
  7.7 1.3 %collective-permute-start.5 = (f32[8,8,32,128]{3,2,1,0:T(8,128)S(1)}, f32[8,8,32,128]{3,2,1,0:T(8,128)S(1)}, u32[]{:S(2)}, u32[]{:S(2)}) collective-permute-start(f32[8,8,32,128]{3,2,1,0:T(8,128)S(1)} %get-tuple-element.28.refs_0_), channel_id=1, source_target_pairs={{1,0},{2,1},{3,2},{4,3},{5,4},{6,5},{7,6},{8,7},{9,8},{10,9},{11,1... | collective-permute-start | bytes 3145736 | tf_op jit(solution)/shard_map/ppermute | solution.py:609
  9.0 3.1 %collective-permute-start.4 = (f32[8,8,32,128]{3,2,1,0:T(8,128)S(1)}, f32[8,8,32,128]{3,2,1,0:T(8,128)S(1)}, u32[]{:S(2)}, u32[]{:S(2)}) collective-permute-start(f32[8,8,32,128]{3,2,1,0:T(8,128)S(1)} %get-tuple-element.29.refs_1_), channel_id=1, source_target_pairs={{0,1},{1,2},{2,3},{3,4},{4,5},{5,6},{6,7},{7,8},{8,9},{9,10},{10,1... | collective-permute-start | bytes 3145736 | tf_op jit(solution)/shard_map/ppermute | solution.py:614
  12.8 0.0 copy-done.2
  12.8 0.0 copy-done.3
  12.8 0.0 copy-done.4
  12.8 14.6 %shard_map.56 = (f32[2,16,8,32,128]{4,3,2,1,0:T(8,128)S(1)}, f32[1088,128]{1,0:T(8,128)S(1)}, f32[544,128]{1,0:T(8,128)S(1)}, f32[272,128]{1,0:T(8,128)S(1)}, s3...) custom-call(f32[8,8,32,128]{3,2,1,0:T(8,128)S(1)} %get-tuple-element.28.refs_0_, ...), custom_call_target="tpu_custom_call" | custom-call | tf_op jit(solution)/shard_map/pallas_call | solution.py:597
  27.4 0.0 copy-start
  27.4 1.9 %copy-done = f32[2,16,8,32,128]{4,3,2,1,0:T(8,128)} copy-done((f32[2,16,8,32,128]{4,3,2,1,0:T(8,128)}, f32[2,16,8,32,128]{4,3,2,1,0:T(8,128)S(1)}, u32[]{:S(2)}) %copy-start) | copy-done | bytes 4194328
  29.4 3.0 %collective-permute-done.1.refs_0_ = f32[16,8,16,128]{3,2,1,0:T(8,128)S(1)} collective-permute-done((f32[16,8,16,128]{3,2,1,0:T(8,128)S(1)}, f32[16,8,16,128]{3,2,1,0:T(8,128)S(1)}, u32[]{:S(2)}, u32[]{:S(2)}) %collective-permute-start.1) | collective-permute-done | bytes 1048608 | tf_op jit(solution)/shard_map/ppermute | solution.py:664
  32.3 0.1 fusion
  32.4 1.3 %collective-permute-start.3 = (f32[8,8,16,128]{3,2,1,0:T(8,128)S(1)}, f32[8,8,16,128]{3,2,1,0:T(8,128)S(1)}, u32[]{:S(2)}, u32[]{:S(2)}) collective-permute-start(f32[8,8,16,128]{3,2,1,0:T(8,128)S(1)} %get-tuple-element.43), channel_id=1, source_target_pairs={{1,0},{2,1},{3,2},{4,3},{5,4},{6,5},{7,6},{8,7},{9,8},{10,9},{11,1... | collective-permute-start | bytes 1572872 | tf_op jit(solution)/shard_map/ppermute | solution.py:609
  33.7 3.1 %collective-permute-start.2 = (f32[8,8,16,128]{3,2,1,0:T(8,128)S(1)}, f32[8,8,16,128]{3,2,1,0:T(8,128)S(1)}, u32[]{:S(2)}, u32[]{:S(2)}) collective-permute-start(f32[8,8,16,128]{3,2,1,0:T(8,128)S(1)} %get-tuple-element.44), channel_id=1, source_target_pairs={{0,1},{1,2},{2,3},{3,4},{4,5},{5,6},{6,7},{7,8},{8,9},{9,10},{10,1... | collective-permute-start | bytes 1572872 | tf_op jit(solution)/shard_map/ppermute | solution.py:614
  36.8 0.0 collective-permute-done.5.refs_2_
  36.8 0.0 collective-permute-done.4.refs_1_
  36.8 9.7 %shard_map.57.refs_2_ = f32[2,16,8,32,128]{4,3,2,1,0:T(8,128)S(1)} custom-call(f32[16,8,16,128]{3,2,1,0:T(8,128)S(1)} %collective-permute-done.1.refs_0_, f32[8,8,32,128]{3,2,1,0:T(8,128)S(1)} %collective-permute-done.4.refs_1_, f32[8,8,32,128]{3,2,1,0:T(8,128)S(1)} %collective-permute-done.5.refs_2_, f32[2,16,8,32,128]{4,3,2,1,0:T(8,128)} %copy-done, ...), custom_call_target="tpu_custom_call" | custom-call | tf_op jit(solution)/shard_map/pallas_call | solution.py:597
  46.5 0.0 collective-permute-done.3.refs_1_
  46.5 0.0 collective-permute-done.2.refs_0_
  46.5 5.4 %shard_map.58 = (f32[16,32,1024]{2,1,0:T(8,128)S(1)}, f32[32,1,128]{2,1,0:T(1,128)S(1)}) custom-call(f32[8,8,16,128]{3,2,1,0:T(8,128)S(1)} %collective-permute-done.2.refs_0_, f32[8,8,16,128]{3,2,1,0:T(8,128)S(1)} %collective-permute-done.3.refs_1_, f32[2,16,8,32,128]{4,3,2,1,0:T(8,128)S(1)} %shard_map.57.refs_2_, ...), custom_call_target="tpu_custom_call" | custom-call | tf_op jit(solution)/shard_map/pallas_call | solution.py:597
  51.9 15.3 %all_to_all.5.totals = f32[32,1,128]{2,1,0:T(1,128)S(1)} all-to-all(f32[32,1,128]{2,1,0:T(1,128)S(1)} %get-tuple-element.41), channel_id=1, replica_groups=mesh['scen'=2,'grid'=16] {'scen','grid'}, dimensions={0} | all-to-all | bytes 32768 | tf_op jit(solution)/shard_map/all_to_all | solution.py:711
  67.2 1.6 %shard_map.59 = f32[16,32,1024]{2,1,0:T(8,128)} custom-call(f32[32,1,128]{2,1,0:T(1,128)S(1)} %all_to_all.5.totals, f32[16,32,1024]{2,1,0:T(8,128)S(1)} %get-tuple-element.42.average), custom_call_target="tpu_custom_call" | custom-call | tf_op jit(solution)/shard_map/pallas_call | solution.py:713
Async XLA Ops:
  0.0 7.6 %collective-permute-start = (s32[1]{0:T(128)}, s32[1]{0:T(128)}, u32[]{:S(2)}, u32[]{:S(2)}) collective-permute-start(s32[1]{0:T(128)} %param.6), channel_id=1, source_target_pairs={{0,16},{16,0},{1,17},{17,1},{2,18},{18,2},{3,19},{19,3},{4,20},{20... | collective-permute-start | bytes 20 | tf_op jit(solution)/shard_map/ppermute | solution.py:642
  2.9 1.6 %copy-start.1 = (f32[16,32,1024]{2,1,0:T(8,128)S(1)}, f32[16,32,1024]{2,1,0:T(8,128)}, u32[]{:S(2)}) copy-start(f32[16,32,1024]{2,1,0:T(8,128)} %values.1) | copy-start | bytes 6291460
  4.5 8.2 %copy-start.2 = (s32[16,3]{0,1:T(4,128)S(1)}, s32[16,3]{0,1:T(4,128)}, u32[]{:S(2)}) copy-start(s32[16,3]{0,1:T(4,128)} %param.8) | copy-start | bytes 580
  4.5 8.2 %copy-start.3 = (s32[12,3]{0,1:T(4,128)S(1)}, s32[12,3]{0,1:T(4,128)}, u32[]{:S(2)}) copy-start(s32[12,3]{0,1:T(4,128)} %param.7) | copy-start | bytes 436
  4.5 8.2 %copy-start.4 = (f32[3]{0:T(128)S(1)}, f32[3]{0:T(128)}, u32[]{:S(2)}) copy-start(f32[3]{0:T(128)} %refs_4_.1) | copy-start | bytes 40
  7.6 24.7 %collective-permute-start.1 = (f32[16,8,16,128]{3,2,1,0:T(8,128)S(1)}, f32[16,8,16,128]{3,2,1,0:T(8,128)S(1)}, u32[]{:S(2)}, u32[]{:S(2)}) collective-permute-start(f32[16,8,16,128]{3,2,1,0:T(8,128)S(1)} %get-tuple-element.27), channel_id=1, source_target_pairs={{0,16},{16,0},{1,17},{17,1},{2,18},{18,2},{3,19},{19,3},{4,20},{20... | collective-permute-start | bytes 3145736 | tf_op jit(solution)/shard_map/ppermute | solution.py:664
  7.7 29.1 %collective-permute-start.5 = (f32[8,8,32,128]{3,2,1,0:T(8,128)S(1)}, f32[8,8,32,128]{3,2,1,0:T(8,128)S(1)}, u32[]{:S(2)}, u32[]{:S(2)}) collective-permute-start(f32[8,8,32,128]{3,2,1,0:T(8,128)S(1)} %get-tuple-element.28.refs_0_), channel_id=1, source_target_pairs={{1,0},{2,1},{3,2},{4,3},{5,4},{6,5},{7,6},{8,7},{9,8},{10,9},{11,1... | collective-permute-start | bytes 3145736 | tf_op jit(solution)/shard_map/ppermute | solution.py:609
  9.0 27.8 %collective-permute-start.4 = (f32[8,8,32,128]{3,2,1,0:T(8,128)S(1)}, f32[8,8,32,128]{3,2,1,0:T(8,128)S(1)}, u32[]{:S(2)}, u32[]{:S(2)}) collective-permute-start(f32[8,8,32,128]{3,2,1,0:T(8,128)S(1)} %get-tuple-element.29.refs_1_), channel_id=1, source_target_pairs={{0,1},{1,2},{2,3},{3,4},{4,5},{5,6},{6,7},{7,8},{8,9},{9,10},{10,1... | collective-permute-start | bytes 3145736 | tf_op jit(solution)/shard_map/ppermute | solution.py:614
  27.4 1.9 %copy-start = (f32[2,16,8,32,128]{4,3,2,1,0:T(8,128)}, f32[2,16,8,32,128]{4,3,2,1,0:T(8,128)S(1)}, u32[]{:S(2)}) copy-start(f32[2,16,8,32,128]{4,3,2,1,0:T(8,128)S(1)} %get-tuple-element.34.refs_3_) | copy-start | bytes 12582916
  32.4 14.1 %collective-permute-start.3 = (f32[8,8,16,128]{3,2,1,0:T(8,128)S(1)}, f32[8,8,16,128]{3,2,1,0:T(8,128)S(1)}, u32[]{:S(2)}, u32[]{:S(2)}) collective-permute-start(f32[8,8,16,128]{3,2,1,0:T(8,128)S(1)} %get-tuple-element.43), channel_id=1, source_target_pairs={{1,0},{2,1},{3,2},{4,3},{5,4},{6,5},{7,6},{8,7},{9,8},{10,9},{11,1... | collective-permute-start | bytes 1572872 | tf_op jit(solution)/shard_map/ppermute | solution.py:609
  33.7 12.8 %collective-permute-start.2 = (f32[8,8,16,128]{3,2,1,0:T(8,128)S(1)}, f32[8,8,16,128]{3,2,1,0:T(8,128)S(1)}, u32[]{:S(2)}, u32[]{:S(2)}) collective-permute-start(f32[8,8,16,128]{3,2,1,0:T(8,128)S(1)} %get-tuple-element.44), channel_id=1, source_target_pairs={{0,1},{1,2},{2,3},{3,4},{4,5},{5,6},{6,7},{7,8},{8,9},{9,10},{10,1... | collective-permute-start | bytes 1572872 | tf_op jit(solution)/shard_map/ppermute | solution.py:614

commit v7 on v6

--- a/solution.py
+++ b/solution.py
@@ -12,7 +12,7 @@
 SUB, LANES = 8, 128
 TILE = 2
 CHUNK = 4
-FILL = 8
+FILL = 16
 UNROLL = 2
 softness = 0.5
 

time: 69.6 us -> 70.1 us (level); the launches traced: 68.7 us -> 70.5 us
  Pallas kernels: 34.3 us -> 36.2 us
    pallas_call x3, Pallas kernels: 29.7 us -> 31.5 us  [call(): pl.pallas_call(body, out_shape=outs, in_specs=[VMEM if array.ndim == 2 el...]
  transfers between devices with their start and end apart: 6 -> 6, of which waited for: 1 -> 1; matrix products, arithmetic and copies ran while one was open for 0% -> 0% of each run, Pallas kernels for 40% -> 42%
where the time goes in v7:
time: 70.1 us; the launch traced here: 70.5 us
  Pallas kernels  36.2 us (52%)
  blocking collectives  15.3 us (22%)
  starting transfers between devices  11.8 us (17%)
  local copies, waits for them, and re-layouts  3.63 us (5%)
  waiting for transfers between devices  2.81 us (4%)
  between operations  0.8 us (1%)
    pallas_call x3, Pallas kernels, call(): pl.pallas_call(body, out_shape=outs, in_specs=[VMEM if array.ndim == 2 el...  31.5 us
    all_to_all x1, blocking collectives, on_device(): totals = lax.all_to_all(totals, ('scen', 'grid'), 0, 0, tiled=True)  15.3 us
    ppermute x2, starting transfers between devices, from_below(): lax.ppermute(cells, axis, [(i, i + hops) for i in range(count - hops)])  6.16 us
    unnamed x10, local copies, waits for them, and re-layouts  3.54 us
    pallas_call x1, Pallas kernels, on_device(): pl.pallas_call(functools.partial(planes_kernel, sizes), out_shape=made, i...  3.07 us
    ppermute x1, starting transfers between devices, on_device(): lax.ppermute(scenario_ids, 'scen', [(i, (i + hop) % scen_count) for i in...  2.94 us
    ppermute x1, waiting for transfers between devices, on_device(): beyond = lax.ppermute(made[-1], 'scen', [(0, 1), (1, 0)])  2.8 us
    ppermute x2, starting transfers between devices, from_above(): lax.ppermute(cells, axis, [(i + hops, i) for i in range(count - hops)])  2.58 us
  transfers between devices with their start and end apart: 6, of which 1 were waited for; matrix products, arithmetic and copies ran while one was open for 0% of the time, Pallas kernels for 42%

profile of v7, /device:TPU:0, one launch (start us, length us, event | category | flops | bytes accessed | tf_op | source)
XLA Modules:
  0.0 70.5 jit_solution(7822262204263677228)
XLA Ops:
  0.0 2.9 %collective-permute-start = (s32[1]{0:T(128)}, s32[1]{0:T(128)}, u32[]{:S(2)}, u32[]{:S(2)}) collective-permute-start(s32[1]{0:T(128)} %param.6), channel_id=1, source_target_pairs={{0,16},{16,0},{1,17},{17,1},{2,18},{18,2},{3,19},{19,3},{4,20},{20... | collective-permute-start | bytes 20 | tf_op jit(solution)/shard_map/ppermute | solution.py:642
  2.9 0.0 copy-start.1
  2.9 1.6 %copy-done.1 = f32[16,32,1024]{2,1,0:T(8,128)S(1)} copy-done((f32[16,32,1024]{2,1,0:T(8,128)S(1)}, f32[16,32,1024]{2,1,0:T(8,128)}, u32[]{:S(2)}) %copy-start.1) | copy-done | bytes 2097176
  4.5 0.0 copy-start.2
  4.5 0.0 copy-start.3
  4.5 0.0 copy-start.4
  4.5 3.1 %shard_map.55 = (f32[8,8,32,128]{3,2,1,0:T(8,128)S(1)}, f32[8,8,32,128]{3,2,1,0:T(8,128)S(1)}, f32[16,8,16,128]{3,2,1,0:T(8,128)S(1)}) custom-call(f32[16,32,1024]{2,1,0:T(8,128)S(1)} %copy-done.1), custom_call_target="tpu_custom_call" | custom-call | tf_op jit(solution)/shard_map/pallas_call | solution.py:652
  7.6 0.0 collective-permute-done.refs_6_
  7.6 0.1 collective-permute-start.1
  7.7 1.3 %collective-permute-start.5 = (f32[8,8,32,128]{3,2,1,0:T(8,128)S(1)}, f32[8,8,32,128]{3,2,1,0:T(8,128)S(1)}, u32[]{:S(2)}, u32[]{:S(2)}) collective-permute-start(f32[8,8,32,128]{3,2,1,0:T(8,128)S(1)} %get-tuple-element.28.refs_0_), channel_id=1, source_target_pairs={{1,0},{2,1},{3,2},{4,3},{5,4},{6,5},{7,6},{8,7},{9,8},{10,9},{11,1... | collective-permute-start | bytes 3145736 | tf_op jit(solution)/shard_map/ppermute | solution.py:609
  9.0 3.1 %collective-permute-start.4 = (f32[8,8,32,128]{3,2,1,0:T(8,128)S(1)}, f32[8,8,32,128]{3,2,1,0:T(8,128)S(1)}, u32[]{:S(2)}, u32[]{:S(2)}) collective-permute-start(f32[8,8,32,128]{3,2,1,0:T(8,128)S(1)} %get-tuple-element.29.refs_1_), channel_id=1, source_target_pairs={{0,1},{1,2},{2,3},{3,4},{4,5},{5,6},{6,7},{7,8},{8,9},{9,10},{10,1... | collective-permute-start | bytes 3145736 | tf_op jit(solution)/shard_map/ppermute | solution.py:614
  12.8 0.0 copy-done.2
  12.8 0.0 copy-done.3
  12.8 0.0 copy-done.4
  12.8 14.8 %shard_map.56 = (f32[2,16,8,32,128]{4,3,2,1,0:T(8,128)S(1)}, f32[1088,128]{1,0:T(8,128)S(1)}, f32[544,128]{1,0:T(8,128)S(1)}, f32[272,128]{1,0:T(8,128)S(1)}, s3...) custom-call(f32[8,8,32,128]{3,2,1,0:T(8,128)S(1)} %get-tuple-element.28.refs_0_, ...), custom_call_target="tpu_custom_call" | custom-call | tf_op jit(solution)/shard_map/pallas_call | solution.py:597
  27.6 0.0 copy-start
  27.6 1.9 %copy-done = f32[2,16,8,32,128]{4,3,2,1,0:T(8,128)} copy-done((f32[2,16,8,32,128]{4,3,2,1,0:T(8,128)}, f32[2,16,8,32,128]{4,3,2,1,0:T(8,128)S(1)}, u32[]{:S(2)}) %copy-start) | copy-done | bytes 4194328
  29.5 2.8 %collective-permute-done.1.refs_0_ = f32[16,8,16,128]{3,2,1,0:T(8,128)S(1)} collective-permute-done((f32[16,8,16,128]{3,2,1,0:T(8,128)S(1)}, f32[16,8,16,128]{3,2,1,0:T(8,128)S(1)}, u32[]{:S(2)}, u32[]{:S(2)}) %collective-permute-start.1) | collective-permute-done | bytes 1048608 | tf_op jit(solution)/shard_map/ppermute | solution.py:664
  32.3 0.1 fusion
  32.4 1.3 %collective-permute-start.3 = (f32[8,8,16,128]{3,2,1,0:T(8,128)S(1)}, f32[8,8,16,128]{3,2,1,0:T(8,128)S(1)}, u32[]{:S(2)}, u32[]{:S(2)}) collective-permute-start(f32[8,8,16,128]{3,2,1,0:T(8,128)S(1)} %get-tuple-element.43), channel_id=1, source_target_pairs={{1,0},{2,1},{3,2},{4,3},{5,4},{6,5},{7,6},{8,7},{9,8},{10,9},{11,1... | collective-permute-start | bytes 1572872 | tf_op jit(solution)/shard_map/ppermute | solution.py:609
  33.7 3.1 %collective-permute-start.2 = (f32[8,8,16,128]{3,2,1,0:T(8,128)S(1)}, f32[8,8,16,128]{3,2,1,0:T(8,128)S(1)}, u32[]{:S(2)}, u32[]{:S(2)}) collective-permute-start(f32[8,8,16,128]{3,2,1,0:T(8,128)S(1)} %get-tuple-element.44), channel_id=1, source_target_pairs={{0,1},{1,2},{2,3},{3,4},{4,5},{5,6},{6,7},{7,8},{8,9},{9,10},{10,1... | collective-permute-start | bytes 1572872 | tf_op jit(solution)/shard_map/ppermute | solution.py:614
  36.8 0.0 collective-permute-done.5.refs_2_
  36.8 0.0 collective-permute-done.4.refs_1_
  36.8 11.7 %shard_map.57.refs_2_ = f32[2,16,8,32,128]{4,3,2,1,0:T(8,128)S(1)} custom-call(f32[16,8,16,128]{3,2,1,0:T(8,128)S(1)} %collective-permute-done.1.refs_0_, f32[8,8,32,128]{3,2,1,0:T(8,128)S(1)} %collective-permute-done.4.refs_1_, f32[8,8,32,128]{3,2,1,0:T(8,128)S(1)} %collective-permute-done.5.refs_2_, f32[2,16,8,32,128]{4,3,2,1,0:T(8,128)} %copy-done, ...), custom_call_target="tpu_custom_call" | custom-call | tf_op jit(solution)/shard_map/pallas_call | solution.py:597
  48.5 0.0 collective-permute-done.3.refs_1_
  48.5 0.0 collective-permute-done.2.refs_0_
  48.5 5.1 %shard_map.58 = (f32[16,32,1024]{2,1,0:T(8,128)S(1)}, f32[32,1,128]{2,1,0:T(1,128)S(1)}) custom-call(f32[8,8,16,128]{3,2,1,0:T(8,128)S(1)} %collective-permute-done.2.refs_0_, f32[8,8,16,128]{3,2,1,0:T(8,128)S(1)} %collective-permute-done.3.refs_1_, f32[2,16,8,32,128]{4,3,2,1,0:T(8,128)S(1)} %shard_map.57.refs_2_, ...), custom_call_target="tpu_custom_call" | custom-call | tf_op jit(solution)/shard_map/pallas_call | solution.py:597
  53.6 15.3 %all_to_all.5.totals = f32[32,1,128]{2,1,0:T(1,128)S(1)} all-to-all(f32[32,1,128]{2,1,0:T(1,128)S(1)} %get-tuple-element.41), channel_id=1, replica_groups=mesh['scen'=2,'grid'=16] {'scen','grid'}, dimensions={0} | all-to-all | bytes 32768 | tf_op jit(solution)/shard_map/all_to_all | solution.py:711
  68.9 1.6 %shard_map.59 = f32[16,32,1024]{2,1,0:T(8,128)} custom-call(f32[32,1,128]{2,1,0:T(1,128)S(1)} %all_to_all.5.totals, f32[16,32,1024]{2,1,0:T(8,128)S(1)} %get-tuple-element.42.average), custom_call_target="tpu_custom_call" | custom-call | tf_op jit(solution)/shard_map/pallas_call | solution.py:713
Async XLA Ops:
  0.0 7.6 %collective-permute-start = (s32[1]{0:T(128)}, s32[1]{0:T(128)}, u32[]{:S(2)}, u32[]{:S(2)}) collective-permute-start(s32[1]{0:T(128)} %param.6), channel_id=1, source_target_pairs={{0,16},{16,0},{1,17},{17,1},{2,18},{18,2},{3,19},{19,3},{4,20},{20... | collective-permute-start | bytes 20 | tf_op jit(solution)/shard_map/ppermute | solution.py:642
  2.9 1.6 %copy-start.1 = (f32[16,32,1024]{2,1,0:T(8,128)S(1)}, f32[16,32,1024]{2,1,0:T(8,128)}, u32[]{:S(2)}) copy-start(f32[16,32,1024]{2,1,0:T(8,128)} %values.1) | copy-start | bytes 6291460
  4.5 8.2 %copy-start.2 = (s32[16,3]{0,1:T(4,128)S(1)}, s32[16,3]{0,1:T(4,128)}, u32[]{:S(2)}) copy-start(s32[16,3]{0,1:T(4,128)} %param.8) | copy-start | bytes 580
  4.5 8.2 %copy-start.3 = (s32[12,3]{0,1:T(4,128)S(1)}, s32[12,3]{0,1:T(4,128)}, u32[]{:S(2)}) copy-start(s32[12,3]{0,1:T(4,128)} %param.7) | copy-start | bytes 436
  4.5 8.2 %copy-start.4 = (f32[3]{0:T(128)S(1)}, f32[3]{0:T(128)}, u32[]{:S(2)}) copy-start(f32[3]{0:T(128)} %refs_4_.1) | copy-start | bytes 40
  7.6 24.7 %collective-permute-start.1 = (f32[16,8,16,128]{3,2,1,0:T(8,128)S(1)}, f32[16,8,16,128]{3,2,1,0:T(8,128)S(1)}, u32[]{:S(2)}, u32[]{:S(2)}) collective-permute-start(f32[16,8,16,128]{3,2,1,0:T(8,128)S(1)} %get-tuple-element.27), channel_id=1, source_target_pairs={{0,16},{16,0},{1,17},{17,1},{2,18},{18,2},{3,19},{19,3},{4,20},{20... | collective-permute-start | bytes 3145736 | tf_op jit(solution)/shard_map/ppermute | solution.py:664
  7.7 29.1 %collective-permute-start.5 = (f32[8,8,32,128]{3,2,1,0:T(8,128)S(1)}, f32[8,8,32,128]{3,2,1,0:T(8,128)S(1)}, u32[]{:S(2)}, u32[]{:S(2)}) collective-permute-start(f32[8,8,32,128]{3,2,1,0:T(8,128)S(1)} %get-tuple-element.28.refs_0_), channel_id=1, source_target_pairs={{1,0},{2,1},{3,2},{4,3},{5,4},{6,5},{7,6},{8,7},{9,8},{10,9},{11,1... | collective-permute-start | bytes 3145736 | tf_op jit(solution)/shard_map/ppermute | solution.py:609
  9.0 27.8 %collective-permute-start.4 = (f32[8,8,32,128]{3,2,1,0:T(8,128)S(1)}, f32[8,8,32,128]{3,2,1,0:T(8,128)S(1)}, u32[]{:S(2)}, u32[]{:S(2)}) collective-permute-start(f32[8,8,32,128]{3,2,1,0:T(8,128)S(1)} %get-tuple-element.29.refs_1_), channel_id=1, source_target_pairs={{0,1},{1,2},{2,3},{3,4},{4,5},{5,6},{6,7},{7,8},{8,9},{9,10},{10,1... | collective-permute-start | bytes 3145736 | tf_op jit(solution)/shard_map/ppermute | solution.py:614
  27.6 1.9 %copy-start = (f32[2,16,8,32,128]{4,3,2,1,0:T(8,128)}, f32[2,16,8,32,128]{4,3,2,1,0:T(8,128)S(1)}, u32[]{:S(2)}) copy-start(f32[2,16,8,32,128]{4,3,2,1,0:T(8,128)S(1)} %get-tuple-element.34.refs_3_) | copy-start | bytes 12582916
  32.4 16.1 %collective-permute-start.3 = (f32[8,8,16,128]{3,2,1,0:T(8,128)S(1)}, f32[8,8,16,128]{3,2,1,0:T(8,128)S(1)}, u32[]{:S(2)}, u32[]{:S(2)}) collective-permute-start(f32[8,8,16,128]{3,2,1,0:T(8,128)S(1)} %get-tuple-element.43), channel_id=1, source_target_pairs={{1,0},{2,1},{3,2},{4,3},{5,4},{6,5},{7,6},{8,7},{9,8},{10,9},{11,1... | collective-permute-start | bytes 1572872 | tf_op jit(solution)/shard_map/ppermute | solution.py:609
  33.7 14.8 %collective-permute-start.2 = (f32[8,8,16,128]{3,2,1,0:T(8,128)S(1)}, f32[8,8,16,128]{3,2,1,0:T(8,128)S(1)}, u32[]{:S(2)}, u32[]{:S(2)}) collective-permute-start(f32[8,8,16,128]{3,2,1,0:T(8,128)S(1)} %get-tuple-element.44), channel_id=1, source_target_pairs={{0,1},{1,2},{2,3},{3,4},{4,5},{5,6},{6,7},{7,8},{8,9},{9,10},{10,1... | collective-permute-start | bytes 1572872 | tf_op jit(solution)/shard_map/ppermute | solution.py:614
